TPU v7x, 128 devices: a whole 4x4x4 slice. The times are simulated.
128 devices in a mesh: enc: 2 (over core), img: 64 (over y, z, x).
Axes of the slice: x: 4, y: 4, z: 4, core: 2. Of those that a mesh axis runs over, the one named last changes fastest.
Arguments:
- real_images: bfloat16 [4096, 3072], P('img'), may hold values from -6 to 6
- real_labels: int32 [4096], P('img'), may hold values from 0 to 21840, as said below
- class_ids: int32 [64], replicated, may hold values from 0 to 21840, as said below
- synthetic: float32 [640, 3072], P('img'), may hold values from -6 to 6
- patch_weight: bfloat16 [4, 192, 768], P('enc', 'img'), may hold values from -0.4375 to 0.4375
- position: bfloat16 [4, 16, 768], P('enc'), may hold values from -3 to 3
- qkv_weight: bfloat16 [4, 768, 2304], P('enc', 'img'), may hold values from -0.21875 to 0.21875
- out_weight: bfloat16 [4, 768, 768], P('enc', 'img'), may hold values from -0.21875 to 0.21875
Outputs:
- real_means: float32 [4, 64, 768], P('enc', 'img')
- pixel_grad: float32 [640, 3072], P('img')
Inputs may be any that keep to these rules, and one draw needn't show every extreme that they name: class_ids are distinct. `real_labels`: every label is one of class_ids; classes are unevenly represented.
All inputs are finite; a program needn't handle non-finite values.
Results may differ from a plain program's by a relative error of at most 0.014.
Values may be sent and summed in bfloat16 or wider, within the bound.
No kernel may reach another device: no remote copies, remote signals or barrier semaphores. Data moves between devices by JAX's collectives and lax.ppermute only.
A program may use at most 192 MiB of HBM per device.

v0:
```python
import jax
import jax.numpy as jnp
from jax import lax
from jax.sharding import PartitionSpec as P

HEADS = 12
IPC = 10


def layer_norm(h):
    mean = jnp.mean(h, axis=-1, keepdims=True)
    centred = h - mean
    var = jnp.mean(centred * centred, axis=-1, keepdims=True)
    return centred / jnp.sqrt(var + 1e-06)


def encode(pixels, patch_w, pos, qkv_w, out_w):
    count = pixels.shape[0]
    patch_len = patch_w.shape[0]
    width = patch_w.shape[1]
    tokens = pixels.shape[1] // patch_len
    head_size = width // HEADS
    patches = pixels.astype(jnp.bfloat16).reshape(count * tokens, patch_len)
    embed = jnp.dot(patches, patch_w, preferred_element_type=jnp.float32).reshape(
        count, tokens, width
    )
    embed = embed + pos.astype(jnp.float32)
    normed = layer_norm(embed).astype(jnp.bfloat16).reshape(count * tokens, width)
    qkv = jnp.dot(normed, qkv_w, preferred_element_type=jnp.float32).astype(jnp.bfloat16)
    qkv = qkv.reshape(count, tokens, 3, HEADS, head_size)
    query, keys, values = (qkv[:, :, 0], qkv[:, :, 1], qkv[:, :, 2])
    scores = jnp.einsum(
        "nqhd,nkhd->nhqk", query, keys, preferred_element_type=jnp.float32
    ) * head_size ** (-0.5)
    probs = jax.nn.softmax(scores, axis=-1).astype(jnp.bfloat16)
    attended = jnp.einsum(
        "nhqk,nkhd->nqhd", probs, values, preferred_element_type=jnp.float32
    ).astype(jnp.bfloat16)
    attended = attended.reshape(count * tokens, width)
    hidden = embed + jnp.dot(attended, out_w, preferred_element_type=jnp.float32).reshape(
        count, tokens, width
    )
    return jnp.mean(layer_norm(hidden), axis=1)


def local(
    real_images, real_labels, class_ids, synthetic, patch_weight, position, qkv_weight, out_weight
):
    local_enc = patch_weight.shape[0]
    onehot = (real_labels[None, :] == class_ids[:, None]).astype(jnp.bfloat16)
    counts = jnp.sum(onehot.astype(jnp.float32), axis=1)
    weights = []
    terms = []
    for enc in range(local_enc):
        patch_w, qkv_w, out_w = (
            lax.all_gather(patch_weight[enc], "img", axis=0, tiled=True),
            lax.all_gather(qkv_weight[enc], "img", axis=0, tiled=True),
            lax.all_gather(out_weight[enc], "img", axis=0, tiled=True),
        )
        weights.append((patch_w, position[enc], qkv_w, out_w))
        feats = encode(real_images, patch_w, position[enc], qkv_w, out_w).astype(jnp.bfloat16)
        terms.append(jnp.dot(onehot, feats, preferred_element_type=jnp.float32))
    stacked = jnp.stack(terms)
    owned = synthetic.shape[0] // IPC
    totals, all_counts = lax.psum((stacked, counts), "img")
    start = lax.axis_index("img") * owned
    sums = lax.dynamic_slice_in_dim(totals, start, owned, 1)
    own_counts = lax.dynamic_slice_in_dim(all_counts, start, owned, 0)
    real_means = sums / jnp.maximum(own_counts, 1.0)[None, :, None]

    def matching(pixels):
        total = jnp.zeros((), jnp.float32)
        for enc in range(local_enc):
            patch_w, pos, qkv_w, out_w = weights[enc]
            feats = encode(pixels, patch_w, pos, qkv_w, out_w)
            synth_mean = jnp.mean(feats.reshape(owned, IPC, feats.shape[1]), axis=1)
            diff = synth_mean - real_means[enc]
            total = total + jnp.sum(diff * diff)
        return total

    local_grad = jax.grad(matching)(synthetic)
    pixel_grad = lax.psum(local_grad.astype(jnp.bfloat16), "enc").astype(jnp.float32)
    return (real_means, pixel_grad)


def solution(mesh):
    return jax.shard_map(
        local,
        mesh=mesh,
        in_specs=(
            P("img", None),
            P("img"),
            P(),
            P("img", None),
            P("enc", "img", None),
            P("enc", None, None),
            P("enc", "img", None),
            P("enc", "img", None),
        ),
        out_specs=(P("enc", "img", None), P("img", None)),
        check_vma=False,
    )
```

profile of v0, /device:TPU:1, one launch (start us, length us, event | category | flops | bytes accessed | tf_op | source)
XLA Modules:
  0.0 867.4 jit_solution(7063876045152750216)
XLA Ops:
  7.2 1.9 fusion.118
  9.9 1.5 fusion.119
  12.9 1.6 dot_general.120
  15.3 155.7 %all-gather.3 = bf16[1,192,768]{2,0,1:T(2,128)(2,1)S(1)} all-gather(bf16[1,3,768]{2,0,1:T(2,128)(2,1)S(1)} %get-tuple-element.23), channel_id=5, replica_groups=mesh['enc'=2,'img'=64] {'img'}, dimensions={1}, use_global_device_ids=true | all-gather | bytes 299520 | tf_op jit(solution)/shard_map/all_gather | solution.py:56
  171.0 155.2 %all-gather = bf16[1,192,768]{2,0,1:T(2,128)(2,1)} all-gather(bf16[1,3,768]{2,0,1:T(2,128)(2,1)S(1)} %get-tuple-element.22), channel_id=2, replica_groups=mesh['enc'=2,'img'=64] {'img'}, dimensions={1}, use_global_device_ids=true | all-gather | bytes 299520 | tf_op jit(solution)/shard_map/all_gather | solution.py:56
  328.2 1.7 add_reduce_fusion.1
  331.5 1.6 divide_convert_fusion.4
  333.8 1.6 divide_convert_fusion.5
  335.6 145.8 %psum.22 = f32[64]{0:T(128)S(1)} all-reduce(f32[64]{0:T(128)S(1)} %convert_reduce_fusion), channel_id=1, replica_groups=mesh['enc'=2,'img'=64] {'img'}, use_global_device_ids=true, to_apply=%region_16.0 | all-reduce | flops 64 | bytes 512 | tf_op jit(solution)/shard_map/psum | solution.py:65
  483.2 1.9 divide_convert_fusion.13
  486.9 1.9 divide_convert_fusion.12
  490.0 9.6 %convolution_convert_fusion = bf16[1024,2304]{1,0:T(8,128)(2,1)} fusion(bf16[1024,768]{1,0:T(8,128)(2,1)} %bitcast.230, bf16[1,768,2304]{2,0,1:T(2,128)(2,1)} %all-gather.15.cloned.1.call-done), kind=kOutput, calls=%fused_computation.8 | convolution fusion | flops 3626237952 | bytes 9830400 | tf_op jit(solution)/shard_map/dot_general | solution.py:29
  499.6 14.9 %reshape.330 = bf16[64,16,3,12,64]{4,3,2,1,0:T(8,128)(2,1)} reshape(bf16[1024,2304]{1,0:T(8,128)(2,1)} %convolution_convert_fusion) | data formatting | bytes 9437184 | tf_op jit(solution)/shard_map/reshape | solution.py:30
  514.5 7.7 fusion.115
  522.3 1.8 fusion.20
  524.0 5.6 fusion.121
  529.7 9.5 %convolution_convert_fusion.1 = bf16[1024,2304]{1,0:T(8,128)(2,1)} fusion(bf16[1024,768]{1,0:T(8,128)(2,1)} %bitcast.229, bf16[1,768,2304]{2,0,1:T(2,128)(2,1)} %all-gather.11.cloned.1.call-done), kind=kOutput, calls=%fused_computation.9 | convolution fusion | flops 3626237952 | bytes 9830400 | tf_op jit(solution)/shard_map/dot_general | solution.py:29
  539.2 14.9 %reshape.328 = bf16[64,16,3,12,64]{4,3,2,1,0:T(8,128)(2,1)} reshape(bf16[1024,2304]{1,0:T(8,128)(2,1)} %convolution_convert_fusion.1) | data formatting | bytes 9437184 | tf_op jit(solution)/shard_map/reshape | solution.py:30
  554.1 7.9 fusion.114
  562.1 1.8 fusion.21
  563.9 4.9 fusion.123
  568.7 2.9 convert_bitcast_fusion
  571.7 7.3 convert_bitcast_fusion.1
  579.0 3.1 copy.133
  582.0 6.1 dot_general.132
  588.1 4.9 copy.128
  593.0 6.2 dot_general.125
  599.3 4.7 fusion.122
  605.5 3.7 fusion.124
  611.6 3.8 convolution_convert_fusion.3
  618.0 2.2 fusion.126
  622.2 2.1 fusion.127
  625.3 4.6 convolution_convert_fusion.2
  629.9 2.8 reshape.338
  632.8 1.5 fusion.116
  634.3 2.0 fusion.129
  639.2 2.1 fusion.130
  643.7 169.7 %all-reduce.8.cloned.1.call-done = f32[2,64,768]{2,1,0:T(8,128)} async-done(((f32[2,64,768]{2,1,0:T(8,128)}), f32[2,64,768]{2,1,0:T(8,128)}) %all-reduce.8.cloned.1.call-update) | async-done | bytes 393232 | tf_op jit(solution)/shard_map/psum | solution.py:65
  816.0 2.2 convolution_convert_fusion.15
  818.6 1.8 multiply_reduce_fusion.7
  826.4 1.8 multiply_reduce_fusion.6
  832.2 1.7 copy.142
  834.0 3.2 reshape.335
  837.2 4.4 fusion.43
  842.3 1.7 copy.151
  844.1 3.0 reshape.341
  847.1 4.4 fusion.40
  853.7 6.0 psum.23
  (255 shorter events, 42.1 us)
Async XLA Ops:
  7.2 319.0 %copy-start.36 = (f32[10,3072]{1,0:T(8,128)S(1)}, f32[10,3072]{1,0:T(8,128)}, u32[]{:S(2)}) copy-start(f32[10,3072]{1,0:T(8,128)} %param.11) | copy-start | bytes 368644
  7.2 482.9 %all-gather.15.cloned.1.call-start = ((), (), s32[]{:S(2)}) async-start(), calls=%async_computation.3 | async-start | bytes 7188480 | tf_op jit(solution)/shard_map/all_gather | solution.py:57
  9.1 520.6 %all-gather.11.cloned.1.call-start = ((), (), s32[]{:S(2)}) async-start(), calls=%async_computation.1 | async-start | bytes 7188480 | tf_op jit(solution)/shard_map/all_gather | solution.py:57
  9.9 589.4 %all-gather.17.cloned.1.call-start = ((), (), s32[]{:S(2)}) async-start(), calls=%async_computation.4 | async-start | bytes 2396160 | tf_op jit(solution)/shard_map/all_gather | solution.py:58
  11.5 594.0 %all-gather.13.cloned.1.call-start = ((), (), s32[]{:S(2)}) async-start(), calls=%async_computation.2 | async-start | bytes 2396160 | tf_op jit(solution)/shard_map/all_gather | solution.py:58
  12.1 801.3 %all-reduce.8.cloned.1.call-start = ((), (), s32[]{:S(2)}) async-start(), calls=%async_computation | async-start | bytes 786432 | tf_op jit(solution)/shard_map/psum | solution.py:65
  14.5 313.7 %copy-start.3 = (bf16[64,16,192]{2,1,0:T(8,128)(2,1)}, bf16[64,16,192]{2,1,0:T(8,128)(2,1)S(1)}, u32[]{:S(2)}) copy-start(bf16[64,16,192]{2,1,0:T(8,128)(2,1)S(1)} %dot_general.120) | copy-start | bytes 1179652
  171.0 157.2 %copy-start.7 = (bf16[1,192,768]{2,0,1:T(2,128)(2,1)}, bf16[1,192,768]{2,0,1:T(2,128)(2,1)S(1)}, u32[]{:S(2)}) copy-start(bf16[1,192,768]{2,0,1:T(2,128)(2,1)S(1)} %all-gather.3) | copy-start | bytes 884740
  326.3 1.9 copy-start.5
  327.0 4.5 copy-start
  482.6 2.5 copy-start.59
  486.3 13.3 %copy-start.57 = (f32[10,16]{1,0:T(8,128)}, f32[10,16]{1,0:T(8,128)S(1)}, u32[]{:S(2)}) copy-start(f32[10,16]{1,0:T(8,128)S(1)} %multiply_reduce_fusion.10) | copy-start | bytes 1924
  486.9 12.7 %copy-start.37 = (f32[10,16]{1,0:T(8,128)}, f32[10,16]{1,0:T(8,128)S(1)}, u32[]{:S(2)}) copy-start(f32[10,16]{1,0:T(8,128)S(1)} %get-tuple-element.25) | copy-start | bytes 1924
  562.0 6.7 slice-start
  563.8 4.9 slice-start.1
  563.8 4.9 copy-start.4
  563.9 4.9 copy-start.23
  571.7 7.3 copy-start.9
  609.7 1.9 copy-start.30
  618.0 3.6 copy-start.12
  618.0 3.6 copy-start.20
  620.2 4.0 copy-start.51
  620.2 1.9 copy-start.2
  621.6 3.7 copy-start.29
  625.1 190.3 %copy-start.31 = (f32[10,16]{1,0:T(8,128)}, f32[10,16]{1,0:T(8,128)S(1)}, u32[]{:S(2)}) copy-start(f32[10,16]{1,0:T(8,128)S(1)} %get-tuple-element.30) | copy-start | bytes 1924
  636.3 6.7 copy-start.49
  636.3 2.9 copy-start.1
  638.7 176.2 %copy-start.66 = (f32[10,16]{1,0:T(8,128)S(1)}, f32[10,16]{1,0:T(8,128)}, u32[]{:S(2)}) copy-start(f32[10,16]{1,0:T(8,128)} %get-tuple-element.31) | copy-start | bytes 1924
  641.4 177.3 %copy-start.13 = (bf16[10,16,1,12,64]{4,3,2,1,0:T(8,128)(2,1)S(1)}, bf16[10,16,1,12,64]{4,3,2,1,0:T(8,128)(2,1)}, u32[]{:S(2)}) copy-start(bf16[10,16,1,12,64]{4,3,2,1,0:T(8,128)(2,1)} %copy-done.12) | copy-start | bytes 737284
  641.6 174.0 %copy-start.61 = (f32[10,16]{1,0:T(8,128)}, f32[10,16]{1,0:T(8,128)S(1)}, u32[]{:S(2)}) copy-start(f32[10,16]{1,0:T(8,128)S(1)} %multiply_reduce_fusion.9) | copy-start | bytes 1924
  642.2 173.4 %copy-start.33 = (f32[10,16]{1,0:T(8,128)}, f32[10,16]{1,0:T(8,128)S(1)}, u32[]{:S(2)}) copy-start(f32[10,16]{1,0:T(8,128)S(1)} %get-tuple-element.26) | copy-start | bytes 1924
  822.9 2.4 copy-start.10
  824.2 2.2 copy-start.11
  826.3 1.9 copy-start.15
  826.3 1.9 copy-start.19
  826.3 1.9 copy-start.50
  837.2 4.5 copy-start.64
  837.2 4.7 copy-start.60
  837.2 4.7 copy-start.27
  837.2 4.7 copy-start.28
  847.0 4.5 copy-start.63
  847.0 4.7 copy-start.58
  847.0 4.8 copy-start.38
  847.0 4.8 copy-start.40
  847.1 5.2 copy-start.32
  847.1 5.2 copy-start.42
  847.1 5.2 copy-start.46
  847.1 5.2 copy-start.54
  (31 other events, 38.6 us)
Sparse Core Ops, SparseCore 0:
  10.8 78.3 all-gather.14
  92.4 74.9 all-gather.10
  170.2 64.5 all-gather.16
  237.4 63.3 all-gather.12
  611.7 201.6 all-reduce.7
where the time goes:
time: 877 us; the launch traced here: 867 us
  blocking collectives  463 us (53%)
  waiting for transfers between devices  171 us (19%)
  local copies, waits for them, and re-layouts  94.5 us (11%)
  matrix products  86.9 us (10%)
  other arithmetic  35.7 us (4%)
  between operations  16.3 us (2%)
    all_gather x2, blocking collectives, local(): lax.all_gather(patch_weight[enc], 'img', axis=0, tiled=True)  311 us
    psum x1, waiting for transfers between devices, local(): totals, all_counts = lax.psum((stacked, counts), 'img')  170 us
    psum x1, blocking collectives, local(): totals, all_counts = lax.psum((stacked, counts), 'img')  146 us
    reshape x6, local copies, waits for them, and re-layouts, encode(): qkv = qkv.reshape(count, tokens, 3, HEADS, head_size)  40.1 us
    dot_general x6, matrix products, encode(): jnp.dot(normed, qkv_w, preferred_element_type=jnp.float32)  36.3 us
    slice x4, local copies, waits for them, and re-layouts, encode(): query, keys, values = (qkv[:, :, 0], qkv[:, :, 1], qkv[:, :, 2])  18.6 us
    dot_general x8, matrix products, encode(): jnp.einsum('nhqk,nkhd->nqhd', probs, values, preferred_element_type=jnp.f...  18 us
  transfers between devices with their start and end apart: 5, of which 1 were waited for; matrix products, arithmetic and copies ran while one was open for 19% of the time, Pallas kernels for 0%

commit v1 on v0

v1 whole, which is shorter than its diff:
```python
import jax
import jax.numpy as jnp
from jax import lax
from jax.experimental import pallas as pl
from jax.experimental.pallas import tpu as pltpu
from jax.sharding import PartitionSpec as P

AXES = ("enc", "img")
BF = jnp.bfloat16
F32 = jnp.float32
D = 768
PIXELS = 3072
IPC = 10
SLOT = 6
SYN = 4 * SLOT
BLOCK_ROWS = 48
COLS = 2 * D + 128
STEP = 16
REAL = 128
TOKENS = 16
VMEM_LIMIT = 56 * 1024 * 1024


def flat(c, y, z, x):
    return (c % 2) * 64 + (y % 4) * 16 + (z % 4) * 4 + (x % 4)


PLACES = [(c, y, z, x) for c in range(2) for y in range(4) for z in range(4) for x in range(4)]


def permute(a, target):
    return lax.ppermute(a, AXES, [(flat(*p), flat(*target(*p))) for p in PLACES])


def swap_cores(a):
    return permute(a, lambda c, y, z, x: (1 - c, y, z, x))


def from_x(a, k):
    return permute(a, lambda c, y, z, x: (c, y, z, x - k))


def from_first(a, k):
    return permute(a, lambda c, y, z, x: (c, y - k, z, x) if c == 0 else (c, y, z - k, x))


def from_second(a, k):
    return permute(a, lambda c, y, z, x: (c, y, z - k, x) if c == 0 else (c, y - k, z, x))


def normalise(h):
    mean = jnp.mean(h, axis=-1, keepdims=True)
    centred = h - mean
    var = jnp.mean(centred * centred, axis=-1, keepdims=True)
    rstd = lax.rsqrt(var + 1e-06)
    return centred * rstd, rstd


def dot(a, b):
    return jnp.dot(a, b, preferred_element_type=F32)


def dot_nt(a, b):
    return lax.dot_general(a, b, (((1,), (1,)), ((), ())), preferred_element_type=F32)


def dot_tn(a, b):
    return lax.dot_general(a, b, (((0,), (0,)), ((), ())), preferred_element_type=F32)


def low_half():
    return lax.broadcasted_iota(jnp.int32, (128, 128), 1) < 64


def by_head(a, low):
    zero = jnp.zeros_like(a)
    return jnp.concatenate([jnp.where(low, a, zero), jnp.where(low, zero, a)], axis=0)


def image_bias():
    row = lax.broadcasted_iota(jnp.int32, (128, 128), 0)
    col = lax.broadcasted_iota(jnp.int32, (128, 128), 1)
    return jnp.where(row % 8 == col % 8, 0.0, -1e30).astype(F32)


def embed_tiles(x32, wp_ref, posx, tiles):
    halves = []
    for odd in range(2):
        rows = [
            x32[8 * t : 8 * t + 8, 384 * j + 128 * odd : 384 * j + 128 * odd + 256]
            for t in range(tiles)
            for j in range(8)
        ]
        halves.append(dot(jnp.concatenate(rows, axis=0).astype(BF), wp_ref[odd]))
    return [
        jnp.concatenate([h[64 * t : 64 * t + 64] for h in halves], axis=0) + posx
        for t in range(tiles)
    ]


def scores_exp(q, kbd, bias):
    s = dot_nt(q, kbd)
    parts = []
    for h in range(2):
        sh = s[:, 128 * h : 128 * h + 128] + bias
        parts.append(jnp.exp(sh - jnp.max(sh, axis=-1, keepdims=True)))
    return jnp.concatenate(parts, axis=1)


def real_kernel(
    where_ref, x_ref, posx_ref, l0, l1, l2, l3, o0, o1, o2, o3,
    csum_ref, w_ref, wp_ref, e_ref, n_ref, qkv_ref, att_ref, feat_ref, hot_ref, sems,
):
    step = pl.program_id(0)
    tiles = STEP // 8

    @pl.when(step == 0)
    def _():
        core, y, z = where_ref[0], where_ref[1], where_ref[2]
        copies = []
        for other, refs in enumerate(((l0, l1, l2, l3), (o0, o1, o2, o3))):
            part = lax.rem(core + other, 2)
            for j in range(4):
                for i in range(4):
                    dy = jnp.where(part == 0, i, j)
                    dz = jnp.where(part == 0, j, i)
                    block = lax.rem(y + dy, 4) * 4 + lax.rem(z + dz, 4)
                    row = pl.multiple_of(block * BLOCK_ROWS, 16)
                    copies.append(
                        pltpu.make_async_copy(
                            refs[j].at[i],
                            w_ref.at[part, pl.ds(row, BLOCK_ROWS), :],
                            sems.at[other * 16 + j * 4 + i],
                        )
                    )
        for copy in copies:
            copy.start()
        for copy in copies:
            copy.wait()
        out_row = lax.broadcasted_iota(jnp.int32, (192, D), 0)
        in_row = lax.broadcasted_iota(jnp.int32, (192, D), 1)
        wp_ref[...] = jnp.zeros_like(wp_ref)
        for j in range(3):
            pick = jnp.where(in_row == 4 * out_row + j, 1.0, 0.0).astype(BF)
            for part in range(2):
                piece = dot(pick, w_ref[part, :, 2 * D :]).astype(BF)
                at = 384 * part + 128 * j
                wp_ref[0, 0:192, at : at + 128] = piece
                wp_ref[1, 64:256, at : at + 128] = piece

    x32 = x_ref[...].astype(F32)
    for t, e in enumerate(embed_tiles(x32, wp_ref, posx_ref[...], tiles)):
        e_ref[128 * t : 128 * t + 128] = e
        n_ref[128 * t : 128 * t + 128] = normalise(e)[0].astype(BF)
    normed = n_ref[...]
    qkv_ref[:, : 2 * D] = dot(normed, w_ref[0, :, : 2 * D]).astype(BF)
    qkv_ref[:, 2 * D :] = dot(normed, w_ref[1, :, :D]).astype(BF)
    low = low_half()
    bias = image_bias()
    ones = by_head(jnp.ones((128, 128), BF), low)
    for t in range(tiles):
        rows = slice(128 * t, 128 * t + 128)
        for p in range(6):
            at = 128 * p
            q = qkv_ref[rows, at : at + 128] * jnp.asarray(0.125, BF)
            kbd = by_head(qkv_ref[rows, D + at : D + at + 128], low)
            vbd = by_head(qkv_ref[rows, 2 * D + at : 2 * D + at + 128], low)
            ex = scores_exp(q, kbd, bias).astype(BF)
            o = dot(ex, jnp.concatenate([vbd, ones], axis=1))
            att_ref[rows, at : at + 128] = (o[:, :128] / o[:, 128:]).astype(BF)
    hidden = e_ref[...] + dot(att_ref[...], w_ref[1, :, D : 2 * D])
    feats = []
    for t in range(tiles):
        xhat = normalise(hidden[128 * t : 128 * t + 128])[0]
        feats.append(jnp.sum(xhat.reshape(TOKENS, 8, D), axis=0) * (1.0 / TOKENS))
    at = pl.multiple_of(step * STEP, STEP)
    feat_ref[pl.ds(at, STEP), :D] = jnp.concatenate(feats, axis=0).astype(BF)
    feat_ref[pl.ds(at, STEP), D:] = jnp.ones((STEP, 128), BF)
    cls = lax.broadcasted_iota(jnp.int32, (STEP, 128), 1).astype(F32)
    hot_ref[pl.ds(at, STEP), :] = jnp.where(x32[:, PIXELS:] == cls, 1.0, 0.0).astype(BF)

    @pl.when(step == REAL // STEP - 1)
    def _():
        csum_ref[...] = dot_tn(hot_ref[...], feat_ref[...])[:64].astype(csum_ref.dtype)


def synth_kernel(
    x_ref, posx_ref, w_ref, wp_ref,
    feat_ref, xhat1_ref, r1_ref, qkv_ref, p_ref, xhat2_ref, r2_ref, e_ref, n_ref, att_ref,
):
    tiles = SYN // 8
    x32 = x_ref[...].astype(F32)
    for t, e in enumerate(embed_tiles(x32, wp_ref, posx_ref[...], tiles)):
        rows = slice(128 * t, 128 * t + 128)
        e_ref[rows] = e
        xhat, rstd = normalise(e)
        xhat1_ref[rows] = xhat
        r1_ref[rows] = jnp.broadcast_to(rstd, (128, 128))
        n_ref[rows] = xhat.astype(BF)
    normed = n_ref[...]
    qkv_ref[:, : 2 * D] = dot(normed, w_ref[0, :, : 2 * D]).astype(BF)
    qkv_ref[:, 2 * D :] = dot(normed, w_ref[1, :, :D]).astype(BF)
    low = low_half()
    bias = image_bias()
    for t in range(tiles):
        rows = slice(128 * t, 128 * t + 128)
        for p in range(6):
            at = 128 * p
            q = qkv_ref[rows, at : at + 128] * jnp.asarray(0.125, BF)
            kbd = by_head(qkv_ref[rows, D + at : D + at + 128], low)
            vbd = by_head(qkv_ref[rows, 2 * D + at : 2 * D + at + 128], low)
            ex = scores_exp(q, kbd, bias)
            probs = jnp.concatenate(
                [
                    ex[:, 128 * h : 128 * h + 128]
                    / jnp.sum(ex[:, 128 * h : 128 * h + 128], axis=-1, keepdims=True)
                    for h in range(2)
                ],
                axis=1,
            ).astype(BF)
            p_ref[rows, 256 * p : 256 * p + 256] = probs
            att_ref[rows, at : at + 128] = dot(probs, vbd).astype(BF)
    hidden = e_ref[...] + dot(att_ref[...], w_ref[1, :, D : 2 * D])
    for t in range(tiles):
        rows = slice(128 * t, 128 * t + 128)
        xhat, rstd = normalise(hidden[rows])
        xhat2_ref[rows] = xhat
        r2_ref[rows] = jnp.broadcast_to(rstd, (128, 128))
        feat_ref[8 * t : 8 * t + 8] = jnp.sum(xhat.reshape(TOKENS, 8, D), axis=0) * (1.0 / TOKENS)


def norm_back(g, xhat, rstd):
    mean_g = jnp.mean(g, axis=-1, keepdims=True)
    mean_gx = jnp.mean(g * xhat, axis=-1, keepdims=True)
    return rstd[:, :1] * (g - mean_g - xhat * mean_gx)


def back_kernel(
    g_ref, w_ref, wp_ref, xhat1_ref, r1_ref, qkv_ref, p_ref, xhat2_ref, r2_ref,
    out_ref, dh_ref, dhb_ref, da_ref, dqkv_ref,
):
    tiles = SYN // 8
    for t in range(tiles):
        rows = slice(128 * t, 128 * t + 128)
        g = jnp.broadcast_to(g_ref[8 * t : 8 * t + 8][None], (TOKENS, 8, D)).reshape(128, D)
        dh = norm_back(g, xhat2_ref[rows], r2_ref[rows])
        dh_ref[rows] = dh
        dhb_ref[rows] = dh.astype(BF)
    da_ref[...] = dot_nt(dhb_ref[...], w_ref[1, :, D : 2 * D]).astype(BF)
    low = low_half()
    for t in range(tiles):
        rows = slice(128 * t, 128 * t + 128)
        for p in range(6):
            at = 128 * p
            q = qkv_ref[rows, at : at + 128]
            kbd = by_head(qkv_ref[rows, D + at : D + at + 128], low)
            vbd = by_head(qkv_ref[rows, 2 * D + at : 2 * D + at + 128], low)
            da = da_ref[rows, at : at + 128]
            probs = p_ref[rows, 256 * p : 256 * p + 256]
            p32 = probs.astype(F32)
            dp = dot_nt(da, vbd)
            ds = []
            for h in range(2):
                ph, dph = p32[:, 128 * h : 128 * h + 128], dp[:, 128 * h : 128 * h + 128]
                inner = jnp.sum(ph * dph, axis=-1, keepdims=True)
                ds.append(ph * (dph - inner) * 0.125)
            ds = jnp.concatenate(ds, axis=1).astype(BF)
            dqkv_ref[rows, at : at + 128] = dot(ds, kbd).astype(BF)
            dk = dot_tn(ds, q)
            dqkv_ref[rows, D + at : D + at + 128] = jnp.where(low, dk[:128], dk[128:]).astype(BF)
            dv = dot_tn(probs, da)
            dqkv_ref[rows, 2 * D + at : 2 * D + at + 128] = jnp.where(
                low, dv[:128], dv[128:]
            ).astype(BF)
    dn = dot_nt(dqkv_ref[:, : 2 * D], w_ref[0, :, : 2 * D])
    dn = dn + dot_nt(dqkv_ref[:, 2 * D :], w_ref[1, :, :D])
    for t in range(tiles):
        rows = slice(128 * t, 128 * t + 128)
        de = dh_ref[rows] + norm_back(dn[rows], xhat1_ref[rows], r1_ref[rows])
        dhb_ref[rows] = de.astype(BF)
    pieces = []
    for t in range(tiles):
        even = dot_nt(dhb_ref[128 * t : 128 * t + 64], wp_ref[0])
        odd = dot_nt(dhb_ref[128 * t + 64 : 128 * t + 128], wp_ref[1])
        pieces.append(
            jnp.concatenate([even[:, :128], even[:, 128:] + odd[:, :128], odd[:, 128:]], axis=1)
        )
    for j in range(8):
        out_ref[:, 384 * j : 384 * j + 384] = jnp.concatenate(
            [piece[8 * j : 8 * j + 8] for piece in pieces], axis=0
        ).astype(BF)


def full_spec(shape):
    return pl.BlockSpec(shape, lambda *_: (0,) * len(shape))


def run_real(place, x, posx, mine, theirs):
    steps = REAL // STEP
    rows = STEP * TOKENS
    return pl.pallas_call(
        real_kernel,
        grid=(steps,),
        in_specs=[
            pl.BlockSpec(memory_space=pltpu.SMEM),
            pl.BlockSpec((STEP, PIXELS + 128), lambda i: (i, 0)),
            full_spec((128, D)),
        ]
        + [pl.BlockSpec(memory_space=pl.ANY)] * 8,
        out_specs=[full_spec((64, D + 128)), full_spec((2, D, COLS)), full_spec((2, 256, D))],
        out_shape=[
            jax.ShapeDtypeStruct((64, D + 128), BF),
            jax.ShapeDtypeStruct((2, D, COLS), BF),
            jax.ShapeDtypeStruct((2, 256, D), BF),
        ],
        scratch_shapes=[
            pltpu.VMEM((rows, D), F32),
            pltpu.VMEM((rows, D), BF),
            pltpu.VMEM((rows, 3 * D), BF),
            pltpu.VMEM((rows, D), BF),
            pltpu.VMEM((REAL, D + 128), BF),
            pltpu.VMEM((REAL, 128), BF),
            pltpu.SemaphoreType.DMA((32,)),
        ],
        compiler_params=pltpu.CompilerParams(vmem_limit_bytes=VMEM_LIMIT),
        cost_estimate=pl.CostEstimate(
            flops=14_000_000_000, bytes_accessed=12_000_000, transcendentals=3_000_000
        ),
        name="real_forward",
    )(place, x, posx, *mine, *theirs)


def run_synth(x, posx, w, wp):
    rows = SYN * TOKENS
    shapes = [
        ((SYN, D), F32),
        ((rows, D), F32),
        ((rows, 128), F32),
        ((rows, 3 * D), BF),
        ((rows, 2 * D), BF),
        ((rows, D), F32),
        ((rows, 128), F32),
    ]
    return pl.pallas_call(
        synth_kernel,
        out_shape=[jax.ShapeDtypeStruct(s, t) for s, t in shapes],
        scratch_shapes=[
            pltpu.VMEM((rows, D), F32),
            pltpu.VMEM((rows, D), BF),
            pltpu.VMEM((rows, D), BF),
        ],
        compiler_params=pltpu.CompilerParams(vmem_limit_bytes=VMEM_LIMIT),
        cost_estimate=pl.CostEstimate(
            flops=3_000_000_000, bytes_accessed=12_000_000, transcendentals=600_000
        ),
        name="synth_forward",
    )(x, posx, w, wp)


def run_back(g, w, wp, saved):
    rows = SYN * TOKENS
    return pl.pallas_call(
        back_kernel,
        out_shape=jax.ShapeDtypeStruct((SYN, PIXELS), BF),
        scratch_shapes=[
            pltpu.VMEM((rows, D), F32),
            pltpu.VMEM((rows, D), BF),
            pltpu.VMEM((rows, D), BF),
            pltpu.VMEM((rows, 3 * D), BF),
        ],
        compiler_params=pltpu.CompilerParams(vmem_limit_bytes=VMEM_LIMIT),
        cost_estimate=pl.CostEstimate(
            flops=4_000_000_000, bytes_accessed=12_000_000, transcendentals=0
        ),
        name="synth_backward",
    )(g, w, wp, *saved)


def gather_weights(core, x, patch_weight, qkv_weight, out_weight):
    columns = jnp.concatenate([qkv_weight, out_weight], axis=-1)
    patch = jnp.pad(patch_weight.reshape(2, 3, 2, 3, 128), ((0, 0),) * 3 + ((0, 1), (0, 0)))
    patch = patch.transpose(0, 1, 3, 2, 4).reshape(2, 12, 2, 128)
    both = jnp.concatenate([columns.reshape(2, 12, 2, 2 * D), patch], axis=-1)
    both = both.transpose(0, 2, 1, 3).reshape(4, 12, COLS)
    parts = []
    for k in range(4):
        to = (x - k) % 4
        first = to // 2 == core
        index = (to % 2) * 2 + jnp.where(first, 0, 1)

        def target(c, yy, zz, xx, k=k):
            to = (xx - k) % 4
            return (0, yy, zz, to) if to // 2 == c else (1, yy, zz, (to + 2) % 4)

        parts.append(permute(lax.dynamic_index_in_dim(both, index, 0, keepdims=False), target))
    ring = jnp.roll(jnp.stack(parts), x + 2 * core, axis=0).reshape(BLOCK_ROWS, COLS)
    line = jnp.stack([ring] + [from_first(ring, k) for k in (1, 2, 3)])
    mine = [line] + [from_second(line, k) for k in (1, 2, 3)]
    theirs = [swap_cores(a) for a in mine]
    return mine, theirs


def local(
    real_images, real_labels, class_ids, synthetic, patch_weight, position, qkv_weight, out_weight
):
    core, img = lax.axis_index("enc"), lax.axis_index("img")
    y, z, x = img // 16, (img // 4) % 4, img % 4
    place = jnp.stack([core, y, z, x]).astype(jnp.int32)

    hit = real_labels[:, None] == class_ids[None, :]
    index = jnp.sum(jnp.where(hit, jnp.arange(64, dtype=F32)[None, :], 0.0), axis=1)
    tagged = jnp.concatenate(
        [real_images, jnp.broadcast_to(index[:, None], (64, 128)).astype(BF)], axis=1
    )
    syn = lax.dynamic_slice_in_dim(synthetic, 5 * core, 5, 0).astype(BF)
    images = jnp.concatenate(
        [lax.dynamic_slice_in_dim(tagged, 32 * core, 32, 0), jnp.pad(syn, ((0, 1), (0, 128)))],
        axis=0,
    )
    images = jnp.stack([images] + [from_x(images, k) for k in (1, 2, 3)])
    real_x = images[:, :32].reshape(REAL, PIXELS + 128)
    syn_x = images[:, 32:, :PIXELS].reshape(SYN, PIXELS)

    their_pos = swap_cores(position)
    pos = lax.dynamic_index_in_dim(
        jnp.where(x // 2 == core, position, their_pos), x % 2, 0, keepdims=False
    ).astype(F32)
    posx = jnp.repeat(pos.reshape(8, 2, D).transpose(1, 0, 2).reshape(TOKENS, D), 8, axis=0)

    mine, theirs = gather_weights(core, x, patch_weight, qkv_weight, out_weight)
    csum, w, wp = run_real(place, real_x, posx, mine, theirs)

    groups = [[yz * 4 + xx for yz in range(16)] for xx in range(4)]
    got = lax.all_to_all(
        csum.reshape(16, 4, D + 128), "img", 0, 0, axis_index_groups=groups
    )
    half = jnp.sum(got.astype(F32), axis=0)
    total = half + swap_cores(half)
    means = total[:, :D] / jnp.maximum(total[:, D : D + 1], 1.0)

    feats, *saved = run_synth(syn_x, posx, w, wp)
    own = jnp.sum(feats.reshape(4, SLOT, D)[:, :5], axis=1)
    syn_mean = (own + swap_cores(own)) * (1.0 / IPC)
    g = (syn_mean - jnp.roll(means, -x, axis=0)) * (2.0 / (IPC * TOKENS))
    grads = run_back(jnp.repeat(g, SLOT, axis=0), w, wp, saved)

    sent = []
    for m in range(2):
        row = lax.dynamic_index_in_dim(means, (x - m) % 2 + 2 * core, 0, keepdims=True)
        sent.append(
            permute(row, lambda c, yy, zz, xx, m=m: (xx // 2, yy, zz, (xx - m) % 2 + 2 * c))
        )
    first = jnp.where(x % 2 == 0, sent[0], sent[1])
    second = jnp.where(x % 2 == 0, sent[1], sent[0])
    real_means = jnp.stack([first, second])

    grads = grads.reshape(4, SLOT, PIXELS)
    pixel = grads[0].astype(F32)
    for k in (1, 2, 3):
        pixel = pixel + from_x(grads[k], -k).astype(F32)
    pixel = pixel[:5]
    other = swap_cores(pixel)
    pixel_grad = jnp.concatenate(
        [jnp.where(core == 0, pixel, other), jnp.where(core == 0, other, pixel)], axis=0
    )
    return (real_means, pixel_grad)


def solution(mesh):
    return jax.shard_map(
        local,
        mesh=mesh,
        in_specs=(
            P("img", None),
            P("img"),
            P(),
            P("img", None),
            P("enc", "img", None),
            P("enc", None, None),
            P("enc", "img", None),
            P("enc", "img", None),
        ),
        out_specs=(P("enc", "img", None), P("img", None)),
        check_vma=False,
    )
```

time: 877 us -> 133 us (0.15); the launches traced: 867 us -> 132 us
  blocking collectives: 463 us -> 0 us
  waiting for transfers between devices: 171 us -> 25.9 us
  matrix products: 86.9 us -> 0 us
  local copies, waits for them, and re-layouts: 94.5 us -> 7.89 us
  Pallas kernels: 0 us -> 56.4 us
  starting transfers between devices: 0.2 us -> 36.8 us
  other arithmetic: 35.7 us -> 4.04 us
  between operations: 16.3 us -> 1.3 us
    all_gather x2 -> x0, blocking collectives: 311 us -> none  [local(): lax.all_gather(patch_weight[enc], 'img', axis=0, tiled=True)]
    psum x1 -> x0, waiting for transfers between devices: 170 us -> none  [local(): totals, all_counts = lax.psum((stacked, counts), 'img')]
    psum x2 -> x0, blocking collectives: 152 us -> none  [the longest x1 146 us: local(): totals, all_counts = lax.psum((stacked, counts), 'img')]
    dot_general x34 -> x0, matrix products: 82.7 us -> none  [the longest x6 36.3 us: encode(): jnp.dot(normed, qkv_w, preferred_element_type=jnp.float32)]
    pallas_call x0 -> x3, Pallas kernels: none -> 56.4 us  [the longest x1 32.9 us: run_real(): pl.pallas_call(real_kernel, grid=(steps,), in_specs=[pl.BlockSpec(memory_...]
    reshape x8 -> x12, local copies, waits for them, and re-layouts: 40.8 us -> 5.53 us  [the longest x1 1.57 us: local(): csum.reshape(16, 4, D + 128)]
    ppermute x0 -> x26, starting transfers between devices: none -> 33.1 us  [permute(): lax.ppermute(a, AXES, [(flat(*p), flat(*target(*p))) for p in PLACES])]
    ppermute x0 -> x26, waiting for transfers between devices: none -> 25.9 us  [permute(): lax.ppermute(a, AXES, [(flat(*p), flat(*target(*p))) for p in PLACES])]
  transfers between devices with their start and end apart: 5 -> 27, of which waited for: 1 -> 11; matrix products, arithmetic and copies ran while one was open for 19% -> 5% of each run, Pallas kernels for 0% -> 18%
where the time goes in v1:
time: 133 us; the launch traced here: 132 us
  Pallas kernels  56.4 us (42%)
  starting transfers between devices  36.8 us (28%)
  waiting for transfers between devices  25.9 us (19%)
  local copies, waits for them, and re-layouts  7.89 us (6%)
  other arithmetic  4.04 us (3%)
    ppermute x26, starting transfers between devices, permute(): lax.ppermute(a, AXES, [(flat(*p), flat(*target(*p))) for p in PLACES])  33.1 us
    pallas_call x1, Pallas kernels, run_real(): pl.pallas_call(real_kernel, grid=(steps,), in_specs=[pl.BlockSpec(memory_...  32.9 us
    ppermute x26, waiting for transfers between devices, permute(): lax.ppermute(a, AXES, [(flat(*p), flat(*target(*p))) for p in PLACES])  25.9 us
    pallas_call x1, Pallas kernels, run_back(): pl.pallas_call(back_kernel, out_shape=jax.ShapeDtypeStruct((SYN, PIXELS),...  14.5 us
    pallas_call x1, Pallas kernels, run_synth(): pl.pallas_call(synth_kernel, out_shape=[jax.ShapeDtypeStruct(s, t) for s,...  9.07 us
    all_to_all x1, starting transfers between devices, local(): lax.all_to_all(csum.reshape(16, 4, D + 128), 'img', 0, 0, axis_index_grou...  3.69 us
  transfers between devices with their start and end apart: 27, of which 11 were waited for; matrix products, arithmetic and copies ran while one was open for 5% of the time, Pallas kernels for 18%

profile of v1, /device:TPU:1, one launch (start us, length us, event | category | flops | bytes accessed | tf_op | source)
XLA Modules:
  0.0 132.3 jit_solution(254563270250162586)
XLA Ops:
  0.9 0.7 reshape.64
  1.7 1.1 pad_maximum_fusion.4
  3.1 3.4 %collective-permute-start.7 = (bf16[12,1664]{1,0:T(8,128)(2,1)S(1)}, bf16[12,1664]{1,0:T(8,128)(2,1)S(1)}, u32[]{:S(2)}, u32[]{:S(2)}) collective-permute-start(bf16[12,1664]{1,0:T(8,128)(2,1)S(1)} %get-tuple-element.24), channel_id=1, source_target_pairs={{0,1},{1,64},{2,65},{3,0},{4,5},{5,68},{6,69},{7,4},{8,9},{9,72},{... | collective-permute-start | bytes 119816 | tf_op jit(solution)/shard_map/ppermute | solution.py:32
  6.4 2.7 %collective-permute-start.6 = (bf16[12,1664]{1,0:T(8,128)(2,1)S(1)}, bf16[12,1664]{1,0:T(8,128)(2,1)S(1)}, u32[]{:S(2)}, u32[]{:S(2)}) collective-permute-start(bf16[12,1664]{1,0:T(8,128)(2,1)S(1)} %get-tuple-element.25), channel_id=1, source_target_pairs={{0,64},{1,65},{2,0},{3,1},{4,68},{5,69},{6,4},{7,5},{8,72},{9,73},... | collective-permute-start | bytes 119816 | tf_op jit(solution)/shard_map/ppermute | solution.py:32
  9.2 1.2 collective-permute-start.5
  10.4 1.9 %collective-permute-start.4 = (bf16[12,1664]{1,0:T(8,128)(2,1)S(1)}, bf16[12,1664]{1,0:T(8,128)(2,1)S(1)}, u32[]{:S(2)}, u32[]{:S(2)}) collective-permute-start(bf16[12,1664]{1,0:T(8,128)(2,1)S(1)} %get-tuple-element.27), channel_id=1, source_target_pairs={{0,0},{1,1},{2,64},{3,65},{4,4},{5,5},{6,68},{7,69},{8,8},{9,9},{1... | collective-permute-start | bytes 119816 | tf_op jit(solution)/shard_map/ppermute | solution.py:32
  12.4 0.2 select_reduce_fusion
  12.7 4.7 %collective-permute-done.4 = bf16[12,1664]{1,0:T(8,128)(2,1)S(1)} collective-permute-done((bf16[12,1664]{1,0:T(8,128)(2,1)S(1)}, bf16[12,1664]{1,0:T(8,128)(2,1)S(1)}, u32[]{:S(2)}, u32[]{:S(2)}) %collective-permute-start.4) | collective-permute-done | bytes 39968 | tf_op jit(solution)/shard_map/ppermute | solution.py:32
  17.6 1.7 %collective-permute-start.10 = (bf16[48,1664]{1,0:T(8,128)(2,1)S(1)}, bf16[48,1664]{1,0:T(8,128)(2,1)S(1)}, u32[]{:S(2)}, u32[]{:S(2)}) collective-permute-start(bf16[48,1664]{1,0:T(8,128)(2,1)S(1)} %reshape.67), channel_id=1, source_target_pairs={{0,16},{1,17},{2,18},{3,19},{4,20},{5,21},{6,22},{7,23},{8,24},{9,... | collective-permute-start | bytes 479240 | tf_op jit(solution)/shard_map/ppermute | solution.py:32
  19.3 3.3 %collective-permute-start.9 = (bf16[48,1664]{1,0:T(8,128)(2,1)S(1)}, bf16[48,1664]{1,0:T(8,128)(2,1)S(1)}, u32[]{:S(2)}, u32[]{:S(2)}) collective-permute-start(bf16[48,1664]{1,0:T(8,128)(2,1)S(1)} %reshape.67), channel_id=1, source_target_pairs={{0,32},{1,33},{2,34},{3,35},{4,36},{5,37},{6,38},{7,39},{8,40},{9,... | collective-permute-start | bytes 479240 | tf_op jit(solution)/shard_map/ppermute | solution.py:32
  22.6 0.7 collective-permute-start.8
  23.4 0.7 collective-permute-done.10
  24.1 2.9 %collective-permute-done.9 = bf16[48,1664]{1,0:T(8,128)(2,1)S(1)} collective-permute-done((bf16[48,1664]{1,0:T(8,128)(2,1)S(1)}, bf16[48,1664]{1,0:T(8,128)(2,1)S(1)}, u32[]{:S(2)}, u32[]{:S(2)}) %collective-permute-start.9) | collective-permute-done | bytes 159776 | tf_op jit(solution)/shard_map/ppermute | solution.py:32
  27.1 1.4 %collective-permute-start.13 = (bf16[4,48,1664]{2,1,0:T(8,128)(2,1)S(1)}, bf16[4,48,1664]{2,1,0:T(8,128)(2,1)S(1)}, u32[]{:S(2)}, u32[]{:S(2)}) collective-permute-start(bf16[4,48,1664]{2,1,0:T(8,128)(2,1)S(1)} %pad_maximum_fusion.1.l0), channel_id=1, source_target_pairs={{0,4},{1,5},{2,6},{3,7},{4,8},{5,9},{6,10},{7,11},{8,12},{9,13},{1... | collective-permute-start | bytes 1916936 | tf_op jit(solution)/shard_map/ppermute | solution.py:32
  28.4 2.6 %collective-permute-start.12 = (bf16[4,48,1664]{2,1,0:T(8,128)(2,1)S(1)}, bf16[4,48,1664]{2,1,0:T(8,128)(2,1)S(1)}, u32[]{:S(2)}, u32[]{:S(2)}) collective-permute-start(bf16[4,48,1664]{2,1,0:T(8,128)(2,1)S(1)} %pad_maximum_fusion.1.l0), channel_id=1, source_target_pairs={{0,8},{1,9},{2,10},{3,11},{4,12},{5,13},{6,14},{7,15},{8,0},{9,1},... | collective-permute-start | bytes 1916936 | tf_op jit(solution)/shard_map/ppermute | solution.py:32
  31.1 1.1 collective-permute-start.11
  32.3 2.3 %collective-permute-start.3 = (bf16[2,16,768]{2,1,0:T(8,128)(2,1)S(1)}, bf16[2,16,768]{2,1,0:T(8,128)(2,1)S(1)}, u32[]{:S(2)}, u32[]{:S(2)}) collective-permute-start(bf16[2,16,768]{2,1,0:T(8,128)(2,1)S(1)} %copy-done.3), channel_id=1, source_target_pairs={{0,64},{1,65},{2,66},{3,67},{4,68},{5,69},{6,70},{7,71},{8,72},{9,... | collective-permute-start | bytes 147464 | tf_op jit(solution)/shard_map/ppermute | solution.py:32
  34.6 0.6 pad_add_fusion.where_ref
  35.2 0.3 collective-permute-done.3
  35.5 5.7 %collective-permute-done.1 = bf16[38,3200]{1,0:T(8,128)(2,1)S(1)} collective-permute-done((bf16[38,3200]{1,0:T(8,128)(2,1)S(1)}, bf16[38,3200]{1,0:T(8,128)(2,1)S(1)}, u32[]{:S(2)}, u32[]{:S(2)}) %collective-permute-start.1) | collective-permute-done | bytes 243232 | tf_op jit(solution)/shard_map/ppermute | solution.py:32
  41.2 0.4 collective-permute-start.2
  41.7 0.8 broadcast_bitcast_fusion.posx_ref
  42.4 2.1 %collective-permute-done = bf16[38,3200]{1,0:T(8,128)(2,1)S(1)} collective-permute-done((bf16[38,3200]{1,0:T(8,128)(2,1)S(1)}, bf16[38,3200]{1,0:T(8,128)(2,1)S(1)}, u32[]{:S(2)}, u32[]{:S(2)}) %collective-permute-start) | collective-permute-done | bytes 243232 | tf_op jit(solution)/shard_map/ppermute | solution.py:32
  44.6 1.4 %collective-permute-start.14 = (bf16[4,48,1664]{2,1,0:T(8,128)(2,1)S(1)}, bf16[4,48,1664]{2,1,0:T(8,128)(2,1)}, u32[]{:S(2)}, u32[]{:S(2)}) collective-permute-start(bf16[4,48,1664]{2,1,0:T(8,128)(2,1)S(1)} %pad_maximum_fusion.1.l0), channel_id=1, source_target_pairs={{0,64},{1,65},{2,66},{3,67},{4,68},{5,69},{6,70},{7,71},{8,72},{9,... | collective-permute-start | bytes 1916936 | tf_op jit(solution)/shard_map/ppermute | solution.py:32
  46.1 0.4 collective-permute-start.16
  46.7 3.7 %collective-permute-done.2 = bf16[38,3200]{1,0:T(8,128)(2,1)S(1)} collective-permute-done((bf16[38,3200]{1,0:T(8,128)(2,1)S(1)}, bf16[38,3200]{1,0:T(8,128)(2,1)S(1)}, u32[]{:S(2)}, u32[]{:S(2)}) %collective-permute-start.2) | collective-permute-done | bytes 243232 | tf_op jit(solution)/shard_map/ppermute | solution.py:32
  50.4 0.7 reshape.69.x_ref
  51.1 0.2 pad_maximum_fusion
  51.3 1.0 slice.44
  52.3 32.9 %real_forward.1 = (bf16[64,896]{1,0:T(8,128)(2,1)}, bf16[2,768,1664]{2,1,0:T(8,128)(2,1)}, bf16[2,256,768]{2,1,0:T(8,128)(2,1)}) custom-call(s32[4]{0:T(128)} %pad_add_fusion.where_ref, bf16[128,3200]{1,0:T(8,128)(2,1)} %bitcast.61, f32[128,768]{1,0:T(8,128)} %broadcast_bitcast_fusion.posx_ref, bf16[4,48,1664]{2,1,0:T(8,128)(2,1)} %copy-done.1, ...), custom_call_target="tpu_custom_call" | custom-call | flops 14000000000 | bytes 12000000 | tf_op jit(solution)/shard_map/real_forward/pallas_call | solution.py:301
  85.2 1.6 %reshape.68 = bf16[16,4,896]{2,1,0:T(4,128)(2,1)} reshape(bf16[64,896]{1,0:T(8,128)(2,1)} %get-tuple-element.12) | data formatting | bytes 229376 | tf_op jit(solution)/shard_map/reshape | solution.py:435
  86.7 3.7 %all-to-all-start = ((bf16[16,4,896]{2,1,0:T(4,128)(2,1)}), bf16[16,4,896]{2,1,0:T(4,128)(2,1)S(1)}, u32[]{:S(2)}, u32[]{:S(2)}) async-start(bf16[16,4,896]{2,1,0:T(4,128)(2,1)} %reshape.68), calls=%async_computation | async-start | bytes 229376 | tf_op jit(solution)/shard_map/all_to_all | solution.py:434
  90.4 9.1 %synth_forward.1 = (f32[24,768]{1,0:T(8,128)}, f32[384,768]{1,0:T(8,128)}, f32[384,128]{1,0:T(8,128)}, bf16[384,2304]{1,0:T(8,128)(2,1)}, bf16[384,1536]{1,0:T(8...) custom-call(bf16[24,3072]{1,0:T(8,128)(2,1)} %reshape.69.x_ref, f32[128,768]{1,0:T(8,128)} %broadcast_bitcast_fusion.posx_ref, ...), custom_call_target="tpu_custom_call" | custom-call | flops 3000000000 | bytes 12000000 | tf_op jit(solution)/shard_map/synth_forward/pallas_call | solution.py:344
  99.5 0.9 reshape.70
  100.5 0.8 collective-permute-start.18
  101.4 0.7 collective-permute-done.18
  102.4 2.2 %collective-permute-start.19 = (f32[1,768]{1,0:T(1,128)S(1)}, f32[1,768]{1,0:T(1,128)S(1)}, u32[]{:S(2)}, u32[]{:S(2)}) collective-permute-start(f32[1,768]{1,0:T(1,128)S(1)} %get-tuple-element.34), channel_id=1, source_target_pairs={{0,0},{1,1},{2,64},{3,65},{4,4},{5,5},{6,68},{7,69},{8,8},{9,9},{1... | collective-permute-start | bytes 9224 | tf_op jit(solution)/shard_map/ppermute | solution.py:32
  104.5 1.5 %collective-permute-start.20 = (f32[1,768]{1,0:T(1,128)S(1)}, f32[1,768]{1,0:T(1,128)S(1)}, u32[]{:S(2)}, u32[]{:S(2)}) collective-permute-start(f32[1,768]{1,0:T(1,128)S(1)} %get-tuple-element.35), channel_id=1, source_target_pairs={{0,1},{1,0},{2,65},{3,64},{4,5},{5,4},{6,69},{7,68},{8,9},{9,8},{1... | collective-permute-start | bytes 9224 | tf_op jit(solution)/shard_map/ppermute | solution.py:32
  106.1 0.6 reshape.71.g_ref
  106.7 14.5 %synth_backward.1 = bf16[24,3072]{1,0:T(8,128)(2,1)} custom-call(f32[24,768]{1,0:T(8,128)} %reshape.71.g_ref, bf16[2,768,1664]{2,1,0:T(8,128)(2,1)} %get-tuple-element.13.w_ref, bf16[2,256,768]{2,1,0:T(8,128)(2,1)} %get-tuple-element.14.wp_ref, f32[384,768]{1,0:T(8,128)} %get-tuple-element.16.xhat1_ref, f32[384,128]{1,0:T(8,128)} %get-tuple-element.17.r1_ref, ...), custom_call_target="tpu_custom_call" | custom-call | flops 4000000000 | bytes 12000000 | tf_op jit(solution)/shard_map/synth_backward/pallas_call | solution.py:362
  121.2 1.0 fusion.11
  122.4 3.0 %collective-permute-start.23 = (bf16[6,3072]{1,0:T(8,128)(2,1)S(1)}, bf16[6,3072]{1,0:T(8,128)(2,1)S(1)}, u32[]{:S(2)}, u32[]{:S(2)}) collective-permute-start(bf16[6,3072]{1,0:T(8,128)(2,1)S(1)} %get-tuple-element.32), channel_id=1, source_target_pairs={{0,2},{1,3},{2,0},{3,1},{4,6},{5,7},{6,4},{7,5},{8,10},{9,11},{10,... | collective-permute-start | bytes 110600 | tf_op jit(solution)/shard_map/ppermute | solution.py:32
  125.4 1.5 %collective-permute-done.23 = bf16[6,3072]{1,0:T(8,128)(2,1)S(1)} collective-permute-done((bf16[6,3072]{1,0:T(8,128)(2,1)S(1)}, bf16[6,3072]{1,0:T(8,128)(2,1)S(1)}, u32[]{:S(2)}, u32[]{:S(2)}) %collective-permute-start.23) | collective-permute-done | bytes 36896 | tf_op jit(solution)/shard_map/ppermute | solution.py:32
  126.9 3.3 %collective-permute-done.22 = bf16[6,3072]{1,0:T(8,128)(2,1)S(1)} collective-permute-done((bf16[6,3072]{1,0:T(8,128)(2,1)S(1)}, bf16[6,3072]{1,0:T(8,128)(2,1)S(1)}, u32[]{:S(2)}, u32[]{:S(2)}) %collective-permute-start.22) | collective-permute-done | bytes 36896 | tf_op jit(solution)/shard_map/ppermute | solution.py:32
  130.2 0.5 collective-permute-start.25
  130.7 0.6 pad_maximum_fusion.5
  131.3 0.3 collective-permute-done.25
  131.6 0.7 pad_maximum_fusion.3
  (76 shorter events, 1.8 us)
Async XLA Ops:
  0.6 22.7 %copy-start = (f32[10,3072]{1,0:T(8,128)S(1)}, f32[10,3072]{1,0:T(8,128)}, u32[]{:S(2)}) copy-start(f32[10,3072]{1,0:T(8,128)} %param.11) | copy-start | bytes 368644
  0.6 11.7 %copy-start.6 = (s32[64]{0:T(128)S(1)}, s32[64]{0:T(128)}, u32[]{:S(2)}) copy-start(s32[64]{0:T(128)} %param.10) | copy-start | bytes 772
  0.7 11.7 %copy-start.7 = (s32[64]{0:T(128)S(1)}, s32[64]{0:T(128)}, u32[]{:S(2)}) copy-start(s32[64]{0:T(128)} %param.9) | copy-start | bytes 772
  0.7 11.9 %copy-start.2 = (bf16[64,3072]{1,0:T(8,128)(2,1)S(1)}, bf16[64,3072]{1,0:T(8,128)(2,1)}, u32[]{:S(2)}) copy-start(bf16[64,3072]{1,0:T(8,128)(2,1)} %param.8) | copy-start | bytes 1179652
  3.1 14.4 %collective-permute-start.7 = (bf16[12,1664]{1,0:T(8,128)(2,1)S(1)}, bf16[12,1664]{1,0:T(8,128)(2,1)S(1)}, u32[]{:S(2)}, u32[]{:S(2)}) collective-permute-start(bf16[12,1664]{1,0:T(8,128)(2,1)S(1)} %get-tuple-element.24), channel_id=1, source_target_pairs={{0,1},{1,64},{2,65},{3,0},{4,5},{5,68},{6,69},{7,4},{8,9},{9,72},{... | collective-permute-start | bytes 119816 | tf_op jit(solution)/shard_map/ppermute | solution.py:32
  6.4 10.9 %collective-permute-start.6 = (bf16[12,1664]{1,0:T(8,128)(2,1)S(1)}, bf16[12,1664]{1,0:T(8,128)(2,1)S(1)}, u32[]{:S(2)}, u32[]{:S(2)}) collective-permute-start(bf16[12,1664]{1,0:T(8,128)(2,1)S(1)} %get-tuple-element.25), channel_id=1, source_target_pairs={{0,64},{1,65},{2,0},{3,1},{4,68},{5,69},{6,4},{7,5},{8,72},{9,73},... | collective-permute-start | bytes 119816 | tf_op jit(solution)/shard_map/ppermute | solution.py:32
  9.2 8.2 %collective-permute-start.5 = (bf16[12,1664]{1,0:T(8,128)(2,1)S(1)}, bf16[12,1664]{1,0:T(8,128)(2,1)S(1)}, u32[]{:S(2)}, u32[]{:S(2)}) collective-permute-start(bf16[12,1664]{1,0:T(8,128)(2,1)S(1)} %get-tuple-element.26), channel_id=1, source_target_pairs={{0,65},{1,0},{2,1},{3,64},{4,69},{5,4},{6,5},{7,68},{8,73},{9,8},{... | collective-permute-start | bytes 119816 | tf_op jit(solution)/shard_map/ppermute | solution.py:32
  10.4 6.9 %collective-permute-start.4 = (bf16[12,1664]{1,0:T(8,128)(2,1)S(1)}, bf16[12,1664]{1,0:T(8,128)(2,1)S(1)}, u32[]{:S(2)}, u32[]{:S(2)}) collective-permute-start(bf16[12,1664]{1,0:T(8,128)(2,1)S(1)} %get-tuple-element.27), channel_id=1, source_target_pairs={{0,0},{1,1},{2,64},{3,65},{4,4},{5,5},{6,68},{7,69},{8,8},{9,9},{1... | collective-permute-start | bytes 119816 | tf_op jit(solution)/shard_map/ppermute | solution.py:32
  17.6 6.5 %collective-permute-start.10 = (bf16[48,1664]{1,0:T(8,128)(2,1)S(1)}, bf16[48,1664]{1,0:T(8,128)(2,1)S(1)}, u32[]{:S(2)}, u32[]{:S(2)}) collective-permute-start(bf16[48,1664]{1,0:T(8,128)(2,1)S(1)} %reshape.67), channel_id=1, source_target_pairs={{0,16},{1,17},{2,18},{3,19},{4,20},{5,21},{6,22},{7,23},{8,24},{9,... | collective-permute-start | bytes 479240 | tf_op jit(solution)/shard_map/ppermute | solution.py:32
  19.3 7.7 %collective-permute-start.9 = (bf16[48,1664]{1,0:T(8,128)(2,1)S(1)}, bf16[48,1664]{1,0:T(8,128)(2,1)S(1)}, u32[]{:S(2)}, u32[]{:S(2)}) collective-permute-start(bf16[48,1664]{1,0:T(8,128)(2,1)S(1)} %reshape.67), channel_id=1, source_target_pairs={{0,32},{1,33},{2,34},{3,35},{4,36},{5,37},{6,38},{7,39},{8,40},{9,... | collective-permute-start | bytes 479240 | tf_op jit(solution)/shard_map/ppermute | solution.py:32
  22.6 4.4 %collective-permute-start.8 = (bf16[48,1664]{1,0:T(8,128)(2,1)S(1)}, bf16[48,1664]{1,0:T(8,128)(2,1)S(1)}, u32[]{:S(2)}, u32[]{:S(2)}) collective-permute-start(bf16[48,1664]{1,0:T(8,128)(2,1)S(1)} %reshape.67), channel_id=1, source_target_pairs={{0,48},{1,49},{2,50},{3,51},{4,52},{5,53},{6,54},{7,55},{8,56},{9,... | collective-permute-start | bytes 479240 | tf_op jit(solution)/shard_map/ppermute | solution.py:32
  23.3 8.9 %copy-start.3 = (bf16[2,16,768]{2,1,0:T(8,128)(2,1)S(1)}, bf16[2,16,768]{2,1,0:T(8,128)(2,1)}, u32[]{:S(2)}) copy-start(bf16[2,16,768]{2,1,0:T(8,128)(2,1)} %param.13) | copy-start | bytes 147460
  27.1 23.3 %copy-start.1 = (bf16[4,48,1664]{2,1,0:T(8,128)(2,1)}, bf16[4,48,1664]{2,1,0:T(8,128)(2,1)S(1)}, u32[]{:S(2)}) copy-start(bf16[4,48,1664]{2,1,0:T(8,128)(2,1)S(1)} %pad_maximum_fusion.1.l0) | copy-start | bytes 1916932
  27.1 19.0 %collective-permute-start.13 = (bf16[4,48,1664]{2,1,0:T(8,128)(2,1)S(1)}, bf16[4,48,1664]{2,1,0:T(8,128)(2,1)S(1)}, u32[]{:S(2)}, u32[]{:S(2)}) collective-permute-start(bf16[4,48,1664]{2,1,0:T(8,128)(2,1)S(1)} %pad_maximum_fusion.1.l0), channel_id=1, source_target_pairs={{0,4},{1,5},{2,6},{3,7},{4,8},{5,9},{6,10},{7,11},{8,12},{9,13},{1... | collective-permute-start | bytes 1916936 | tf_op jit(solution)/shard_map/ppermute | solution.py:32
  28.4 17.7 %collective-permute-start.12 = (bf16[4,48,1664]{2,1,0:T(8,128)(2,1)S(1)}, bf16[4,48,1664]{2,1,0:T(8,128)(2,1)S(1)}, u32[]{:S(2)}, u32[]{:S(2)}) collective-permute-start(bf16[4,48,1664]{2,1,0:T(8,128)(2,1)S(1)} %pad_maximum_fusion.1.l0), channel_id=1, source_target_pairs={{0,8},{1,9},{2,10},{3,11},{4,12},{5,13},{6,14},{7,15},{8,0},{9,1},... | collective-permute-start | bytes 1916936 | tf_op jit(solution)/shard_map/ppermute | solution.py:32
  31.1 15.5 %collective-permute-start.11 = (bf16[4,48,1664]{2,1,0:T(8,128)(2,1)S(1)}, bf16[4,48,1664]{2,1,0:T(8,128)(2,1)}, u32[]{:S(2)}, u32[]{:S(2)}) collective-permute-start(bf16[4,48,1664]{2,1,0:T(8,128)(2,1)S(1)} %pad_maximum_fusion.1.l0), channel_id=1, source_target_pairs={{0,12},{1,13},{2,14},{3,15},{4,0},{5,1},{6,2},{7,3},{8,4},{9,5},{1... | collective-permute-start | bytes 1916936 | tf_op jit(solution)/shard_map/ppermute | solution.py:32
  32.2 9.0 %collective-permute-start.1 = (bf16[38,3200]{1,0:T(8,128)(2,1)S(1)}, bf16[38,3200]{1,0:T(8,128)(2,1)S(1)}, u32[]{:S(2)}, u32[]{:S(2)}) collective-permute-start(bf16[38,3200]{1,0:T(8,128)(2,1)S(1)} %get-tuple-element.23), channel_id=1, source_target_pairs={{0,2},{1,3},{2,0},{3,1},{4,6},{5,7},{6,4},{7,5},{8,10},{9,11},{10,... | collective-permute-start | bytes 729608 | tf_op jit(solution)/shard_map/ppermute | solution.py:32
  32.3 3.2 %collective-permute-start.3 = (bf16[2,16,768]{2,1,0:T(8,128)(2,1)S(1)}, bf16[2,16,768]{2,1,0:T(8,128)(2,1)S(1)}, u32[]{:S(2)}, u32[]{:S(2)}) collective-permute-start(bf16[2,16,768]{2,1,0:T(8,128)(2,1)S(1)} %copy-done.3), channel_id=1, source_target_pairs={{0,64},{1,65},{2,66},{3,67},{4,68},{5,69},{6,70},{7,71},{8,72},{9,... | collective-permute-start | bytes 147464 | tf_op jit(solution)/shard_map/ppermute | solution.py:32
  35.5 9.1 %collective-permute-start = (bf16[38,3200]{1,0:T(8,128)(2,1)S(1)}, bf16[38,3200]{1,0:T(8,128)(2,1)S(1)}, u32[]{:S(2)}, u32[]{:S(2)}) collective-permute-start(bf16[38,3200]{1,0:T(8,128)(2,1)S(1)} %get-tuple-element.23), channel_id=1, source_target_pairs={{0,3},{1,0},{2,1},{3,2},{4,7},{5,4},{6,5},{7,6},{8,11},{9,8},{10,9... | collective-permute-start | bytes 729608 | tf_op jit(solution)/shard_map/ppermute | solution.py:32
  41.2 9.1 %collective-permute-start.2 = (bf16[38,3200]{1,0:T(8,128)(2,1)S(1)}, bf16[38,3200]{1,0:T(8,128)(2,1)S(1)}, u32[]{:S(2)}, u32[]{:S(2)}) collective-permute-start(bf16[38,3200]{1,0:T(8,128)(2,1)S(1)} %get-tuple-element.23), channel_id=1, source_target_pairs={{0,1},{1,2},{2,3},{3,0},{4,5},{5,6},{6,7},{7,4},{8,9},{9,10},{10,1... | collective-permute-start | bytes 729608 | tf_op jit(solution)/shard_map/ppermute | solution.py:32
  44.6 7.7 %collective-permute-start.14 = (bf16[4,48,1664]{2,1,0:T(8,128)(2,1)S(1)}, bf16[4,48,1664]{2,1,0:T(8,128)(2,1)}, u32[]{:S(2)}, u32[]{:S(2)}) collective-permute-start(bf16[4,48,1664]{2,1,0:T(8,128)(2,1)S(1)} %pad_maximum_fusion.1.l0), channel_id=1, source_target_pairs={{0,64},{1,65},{2,66},{3,67},{4,68},{5,69},{6,70},{7,71},{8,72},{9,... | collective-permute-start | bytes 1916936 | tf_op jit(solution)/shard_map/ppermute | solution.py:32
  46.0 5.3 %copy-start.4 = (bf16[4,48,1664]{2,1,0:T(8,128)(2,1)}, bf16[4,48,1664]{2,1,0:T(8,128)(2,1)S(1)}, u32[]{:S(2)}) copy-start(bf16[4,48,1664]{2,1,0:T(8,128)(2,1)S(1)} %collective-permute-done.13.l3) | copy-start | bytes 1916932
  46.0 6.3 %collective-permute-start.17 = (bf16[4,48,1664]{2,1,0:T(8,128)(2,1)S(1)}, bf16[4,48,1664]{2,1,0:T(8,128)(2,1)}, u32[]{:S(2)}, u32[]{:S(2)}) collective-permute-start(bf16[4,48,1664]{2,1,0:T(8,128)(2,1)S(1)} %collective-permute-done.13.l3), channel_id=1, source_target_pairs={{0,64},{1,65},{2,66},{3,67},{4,68},{5,69},{6,70},{7,71},{8,72},{9,... | collective-permute-start | bytes 1916936 | tf_op jit(solution)/shard_map/ppermute | solution.py:32
  46.1 5.2 %copy-start.5 = (bf16[4,48,1664]{2,1,0:T(8,128)(2,1)}, bf16[4,48,1664]{2,1,0:T(8,128)(2,1)S(1)}, u32[]{:S(2)}) copy-start(bf16[4,48,1664]{2,1,0:T(8,128)(2,1)S(1)} %collective-permute-done.12.l2) | copy-start | bytes 1916932
  46.1 6.2 %collective-permute-start.16 = (bf16[4,48,1664]{2,1,0:T(8,128)(2,1)S(1)}, bf16[4,48,1664]{2,1,0:T(8,128)(2,1)}, u32[]{:S(2)}, u32[]{:S(2)}) collective-permute-start(bf16[4,48,1664]{2,1,0:T(8,128)(2,1)S(1)} %collective-permute-done.12.l2), channel_id=1, source_target_pairs={{0,64},{1,65},{2,66},{3,67},{4,68},{5,69},{6,70},{7,71},{8,72},{9,... | collective-permute-start | bytes 1916936 | tf_op jit(solution)/shard_map/ppermute | solution.py:32
  46.6 5.8 %collective-permute-start.15 = (bf16[4,48,1664]{2,1,0:T(8,128)(2,1)}, bf16[4,48,1664]{2,1,0:T(8,128)(2,1)}, u32[]{:S(2)}, u32[]{:S(2)}) collective-permute-start(bf16[4,48,1664]{2,1,0:T(8,128)(2,1)} %collective-permute-done.11.l1), channel_id=1, source_target_pairs={{0,64},{1,65},{2,66},{3,67},{4,68},{5,69},{6,70},{7,71},{8,72},{9,... | collective-permute-start | bytes 1916936 | tf_op jit(solution)/shard_map/ppermute | solution.py:32
  86.7 13.7 %all-to-all-start = ((bf16[16,4,896]{2,1,0:T(4,128)(2,1)}), bf16[16,4,896]{2,1,0:T(4,128)(2,1)S(1)}, u32[]{:S(2)}, u32[]{:S(2)}) async-start(bf16[16,4,896]{2,1,0:T(4,128)(2,1)} %reshape.68), calls=%async_computation | async-start | bytes 229376 | tf_op jit(solution)/shard_map/all_to_all | solution.py:434
  100.5 1.7 %collective-permute-start.18 = (f32[4,896]{1,0:T(4,128)S(1)}, f32[4,896]{1,0:T(4,128)S(1)}, u32[]{:S(2)}, u32[]{:S(2)}) collective-permute-start(f32[4,896]{1,0:T(4,128)S(1)} %convert_reduce_fusion), channel_id=1, source_target_pairs={{0,64},{1,65},{2,66},{3,67},{4,68},{5,69},{6,70},{7,71},{8,72},{9,... | collective-permute-start | bytes 43016 | tf_op jit(solution)/shard_map/ppermute | solution.py:32
  101.3 4.7 %collective-permute-start.21 = (f32[4,768]{1,0:T(4,128)S(1)}, f32[4,768]{1,0:T(4,128)S(1)}, u32[]{:S(2)}, u32[]{:S(2)}) collective-permute-start(f32[4,768]{1,0:T(4,128)S(1)} %slice_reduce_fusion), channel_id=1, source_target_pairs={{0,64},{1,65},{2,66},{3,67},{4,68},{5,69},{6,70},{7,71},{8,72},{9,... | collective-permute-start | bytes 36872 | tf_op jit(solution)/shard_map/ppermute | solution.py:32
  102.4 23.0 %collective-permute-start.19 = (f32[1,768]{1,0:T(1,128)S(1)}, f32[1,768]{1,0:T(1,128)S(1)}, u32[]{:S(2)}, u32[]{:S(2)}) collective-permute-start(f32[1,768]{1,0:T(1,128)S(1)} %get-tuple-element.34), channel_id=1, source_target_pairs={{0,0},{1,1},{2,64},{3,65},{4,4},{5,5},{6,68},{7,69},{8,8},{9,9},{1... | collective-permute-start | bytes 9224 | tf_op jit(solution)/shard_map/ppermute | solution.py:32
  104.5 20.9 %collective-permute-start.20 = (f32[1,768]{1,0:T(1,128)S(1)}, f32[1,768]{1,0:T(1,128)S(1)}, u32[]{:S(2)}, u32[]{:S(2)}) collective-permute-start(f32[1,768]{1,0:T(1,128)S(1)} %get-tuple-element.35), channel_id=1, source_target_pairs={{0,1},{1,0},{2,65},{3,64},{4,5},{5,4},{6,69},{7,68},{8,9},{9,8},{1... | collective-permute-start | bytes 9224 | tf_op jit(solution)/shard_map/ppermute | solution.py:32
  122.3 3.1 %collective-permute-start.24 = (bf16[6,3072]{1,0:T(8,128)(2,1)S(1)}, bf16[6,3072]{1,0:T(8,128)(2,1)S(1)}, u32[]{:S(2)}, u32[]{:S(2)}) collective-permute-start(bf16[6,3072]{1,0:T(8,128)(2,1)S(1)} %get-tuple-element.31), channel_id=1, source_target_pairs={{0,3},{1,0},{2,1},{3,2},{4,7},{5,4},{6,5},{7,6},{8,11},{9,8},{10,9... | collective-permute-start | bytes 110600 | tf_op jit(solution)/shard_map/ppermute | solution.py:32
  122.4 4.5 %collective-permute-start.23 = (bf16[6,3072]{1,0:T(8,128)(2,1)S(1)}, bf16[6,3072]{1,0:T(8,128)(2,1)S(1)}, u32[]{:S(2)}, u32[]{:S(2)}) collective-permute-start(bf16[6,3072]{1,0:T(8,128)(2,1)S(1)} %get-tuple-element.32), channel_id=1, source_target_pairs={{0,2},{1,3},{2,0},{3,1},{4,6},{5,7},{6,4},{7,5},{8,10},{9,11},{10,... | collective-permute-start | bytes 110600 | tf_op jit(solution)/shard_map/ppermute | solution.py:32
  125.4 4.8 %collective-permute-start.22 = (bf16[6,3072]{1,0:T(8,128)(2,1)S(1)}, bf16[6,3072]{1,0:T(8,128)(2,1)S(1)}, u32[]{:S(2)}, u32[]{:S(2)}) collective-permute-start(bf16[6,3072]{1,0:T(8,128)(2,1)S(1)} %get-tuple-element.33), channel_id=1, source_target_pairs={{0,1},{1,2},{2,3},{3,0},{4,5},{5,6},{6,7},{7,4},{8,9},{9,10},{10,1... | collective-permute-start | bytes 110600 | tf_op jit(solution)/shard_map/ppermute | solution.py:32
  130.2 1.4 %collective-permute-start.25 = (f32[5,3072]{1,0:T(8,128)S(1)}, f32[5,3072]{1,0:T(8,128)S(1)}, u32[]{:S(2)}, u32[]{:S(2)}) collective-permute-start(f32[5,3072]{1,0:T(8,128)S(1)} %convert_add_fusion), channel_id=1, source_target_pairs={{0,64},{1,65},{2,66},{3,67},{4,68},{5,69},{6,70},{7,71},{8,72},{9,... | collective-permute-start | bytes 184328 | tf_op jit(solution)/shard_map/ppermute | solution.py:32

commit v2 on v1

v2 whole, which is shorter than its diff:
```python
import jax
import jax.numpy as jnp
from jax import lax
from jax.experimental import pallas as pl
from jax.experimental.pallas import tpu as pltpu
from jax.sharding import PartitionSpec as P

AXES = ("enc", "img")
BF = jnp.bfloat16
F32 = jnp.float32
D = 768
PIXELS = 3072
IPC = 10
SLOT = 6
SYN = 4 * SLOT
BLOCK_ROWS = 48
COLS = 2 * D + 128
OUT_AT = COLS + D
STEP = 64
QKV_UNROLL = 9
SYN_QKV_UNROLL = 9
REAL = 128
TOKENS = 16
VMEM_LIMIT = 60 * 1024 * 1024


def flat(c, y, z, x):
    return (c % 2) * 64 + (y % 4) * 16 + (z % 4) * 4 + (x % 4)


PLACES = [(c, y, z, x) for c in range(2) for y in range(4) for z in range(4) for x in range(4)]


def permute(a, target):
    return lax.ppermute(a, AXES, [(flat(*p), flat(*target(*p))) for p in PLACES])


def swap_cores(a):
    return permute(a, lambda c, y, z, x: (1 - c, y, z, x))


def from_x(a, k):
    return permute(a, lambda c, y, z, x: (c, y, z, x - k))


def from_first(a, k):
    return permute(a, lambda c, y, z, x: (c, y - k, z, x) if c == 0 else (c, y, z - k, x))


def from_second(a, k):
    return permute(a, lambda c, y, z, x: (c, y, z - k, x) if c == 0 else (c, y - k, z, x))


def normalise(h):
    mean = jnp.mean(h, axis=-1, keepdims=True)
    centred = h - mean
    var = jnp.mean(centred * centred, axis=-1, keepdims=True)
    rstd = lax.rsqrt(var + 1e-06)
    return centred * rstd, rstd


def dot(a, b):
    return jnp.dot(a, b, preferred_element_type=F32)


def dot_nt(a, b):
    return lax.dot_general(a, b, (((1,), (1,)), ((), ())), preferred_element_type=F32)


def dot_tn(a, b):
    return lax.dot_general(a, b, (((0,), (0,)), ((), ())), preferred_element_type=F32)


def low_half():
    return lax.broadcasted_iota(jnp.int32, (128, 128), 1) < 64


def by_head(a, low):
    zero = jnp.zeros_like(a)
    return jnp.concatenate([jnp.where(low, a, zero), jnp.where(low, zero, a)], axis=0)


def image_bias():
    row = lax.broadcasted_iota(jnp.int32, (128, 128), 0)
    col = lax.broadcasted_iota(jnp.int32, (128, 128), 1)
    return jnp.where(row % 8 == col % 8, 0.0, -1e30).astype(F32)


def embed_rows(x32, wp_ref, tiles):
    halves = []
    for odd in range(2):
        rows = [
            x32[8 * t : 8 * t + 8, 384 * j + 128 * odd : 384 * j + 128 * odd + 256]
            for t in range(tiles)
            for j in range(8)
        ]
        halves.append(dot(jnp.concatenate(rows, axis=0).astype(BF), wp_ref[odd]))
    return [
        jnp.concatenate([h[64 * t : 64 * t + 64] for h in halves], axis=0) for t in range(tiles)
    ]


def exp_scores(s, bias):
    parts = []
    for h in range(2):
        sh = s[:, 128 * h : 128 * h + 128] + bias
        parts.append(jnp.exp(sh - jnp.max(sh, axis=-1, keepdims=True)))
    return parts


def pipeline(count, first, second, third):
    made = {}
    for k in range(count + 2):
        if k < count:
            made[k] = first(k)
        if 0 <= k - 2 < count:
            third(k - 2, *made.pop(k - 2))
        if 0 <= k - 1 < count:
            out = second(k - 1, made.pop(k - 1))
            made[k - 1] = () if out is None else (out,)


def loop(count, fn, unroll=1):
    def body(i, carry):
        fn(i)
        return carry

    lax.fori_loop(0, count, body, 0, unroll=unroll)


def mult(value, of):
    return value if isinstance(value, int) else pl.multiple_of(value, of)


def patch_sum(xhat):
    return jnp.sum(xhat.reshape(TOKENS, 8, D), axis=0) * (1.0 / TOKENS)


def qkv_product(n_ref, w_ref, qkv_ref, unroll):
    def chunk(c):
        at = mult(256 * c, 128)
        col = mult(256 * c + jnp.where(c >= 6, 128, 0), 128)
        out = dot(n_ref[...], w_ref[:, pl.ds(col, 256)])
        qkv_ref[:, pl.ds(at, 256)] = (out * jnp.where(c < 3, 0.125, 1.0)).astype(BF)

    loop(9, chunk, unroll)


def out_product(att_ref, w_ref, e_ref):
    def chunk(c):
        at = mult(256 * c, 128)
        e_ref[:, pl.ds(at, 256)] += dot(att_ref[...], w_ref[:, pl.ds(OUT_AT + at, 256)])

    loop(3, chunk, 3)


def spread_position(where_ref, mine_ref, theirs_ref, posx_ref):
    core, x = where_ref[0], where_ref[3]
    local = x // 2 == core
    pos = jnp.where(local, mine_ref[lax.rem(x, 2)], theirs_ref[lax.rem(x, 2)]).astype(F32)
    for patch in range(TOKENS):
        at = (patch % 2) * 64 + (patch // 2) * 8
        posx_ref[at : at + 8] = jnp.broadcast_to(pos[patch : patch + 1], (8, D))


def real_kernel(
    where_ref, mine_ref, theirs_ref, i0, i1, i2, i3,
    l0, l1, l2, l3, l4, l5, l6, l7, o0, o1, o2, o3, o4, o5, o6, o7,
    csum_ref, w_out, wp_out,
    e_ref, n_ref, qkv_ref, att_ref, feat_ref, hot_ref, x_ref, posx_ref, w_ref, wp_ref, sems,
):
    tiles = STEP // 8
    groups = REAL // STEP
    core, y, z = where_ref[0], where_ref[1], where_ref[2]

    for k, ref in enumerate((i0, i1, i2, i3)):
        pltpu.make_async_copy(ref.at[0:32], x_ref.at[32 * k : 32 * k + 32], sems.at[1]).start()
    mine = (l0, l1, l2, l3, l4, l5, l6, l7)
    theirs = (o0, o1, o2, o3, o4, o5, o6, o7)
    for other, refs in enumerate((mine, theirs)):
        part = lax.rem(core + other, 2)
        for j in range(4):
            for i in range(4):
                dy = jnp.where(part == 0, i, j)
                dz = jnp.where(part == 0, j, i)
                block = lax.rem(y + dy, 4) * 4 + lax.rem(z + dz, 4)
                row = pl.multiple_of(block * BLOCK_ROWS, 16)
                pltpu.make_async_copy(
                    refs[2 * j + i // 2].at[i % 2],
                    w_ref.at[pl.ds(row, BLOCK_ROWS), pl.ds(pl.multiple_of(part * COLS, 128), COLS)],
                    sems.at[0],
                ).start()
    wp_ref[...] = jnp.zeros_like(wp_ref)
    spread_position(where_ref, mine_ref, theirs_ref, posx_ref)
    cls = lax.broadcasted_iota(jnp.int32, (REAL, 128), 1).astype(F32)
    pltpu.make_async_copy(x_ref, x_ref, sems.at[1]).wait()
    hot_ref[...] = jnp.where(x_ref[:, PIXELS:].astype(F32) == cls, 1.0, 0.0).astype(BF)
    feat_ref[:, D:] = jnp.ones((REAL, 128), BF)
    pltpu.make_async_copy(w_ref, w_ref, sems.at[0]).wait()
    save_w = pltpu.make_async_copy(w_ref, w_out, sems.at[2])
    save_w.start()
    out_row = lax.broadcasted_iota(jnp.int32, (192, D), 0)
    in_row = lax.broadcasted_iota(jnp.int32, (192, D), 1)

    def decode(j):
        pick = jnp.where(in_row == 4 * out_row + j, 1.0, 0.0).astype(BF)
        for part in range(2):
            piece = dot(pick, w_ref[:, part * COLS + 2 * D : (part + 1) * COLS]).astype(BF)
            at = mult(384 * part + 128 * j, 128)
            wp_ref[0, 0:192, pl.ds(at, 128)] = piece
            wp_ref[1, 64:256, pl.ds(at, 128)] = piece

    loop(3, decode, 3)
    save_wp = pltpu.make_async_copy(wp_ref, wp_out, sems.at[3])
    save_wp.start()
    low = low_half()
    bias = image_bias()
    ones = by_head(jnp.ones((128, 128), BF), low)

    def score(u):
        rows = pl.ds((u // 6) * 128, 128)
        at = (u % 6) * 128
        kbd = by_head(qkv_ref[rows, D + at : D + at + 128], low)
        return dot_nt(qkv_ref[rows, at : at + 128], kbd)

    def soften(u, s):
        return jnp.concatenate(exp_scores(s, bias), axis=1).astype(BF)

    def weigh(u, ex):
        rows = pl.ds((u // 6) * 128, 128)
        at = (u % 6) * 128
        vbd = by_head(qkv_ref[rows, 2 * D + at : 2 * D + at + 128], low)
        o = dot(ex, jnp.concatenate([vbd, ones], axis=1))
        att_ref[rows, at : at + 128] = (o[:, :128] / o[:, 128:]).astype(BF)

    def group(g):
        at = mult(g * STEP, STEP)
        x32 = x_ref[pl.ds(at, STEP), :PIXELS].astype(F32)
        for t, e in enumerate(embed_rows(x32, wp_ref, tiles)):
            e = e + posx_ref[...]
            e_ref[128 * t : 128 * t + 128] = e
            n_ref[128 * t : 128 * t + 128] = normalise(e)[0].astype(BF)
        qkv_product(n_ref, w_ref, qkv_ref, QKV_UNROLL)
        pipeline(6 * tiles, score, soften, weigh)
        out_product(att_ref, w_ref, e_ref)
        feats = [patch_sum(normalise(e_ref[128 * t : 128 * t + 128])[0]) for t in range(tiles)]
        feat_ref[pl.ds(at, STEP), :D] = jnp.concatenate(feats, axis=0).astype(BF)

    loop(groups, group)
    sums = dot_tn(hot_ref[...], feat_ref[...])
    for b in range(16):
        block = sums[4 * b : 4 * b + 4].astype(csum_ref.dtype)
        csum_ref[b] = block
        csum_ref[16 + b] = block
    save_w.wait()
    save_wp.wait()


def copies_of(pairs, sems):
    copies = [pltpu.make_async_copy(src, dst, sems.at[i]) for i, (src, dst) in enumerate(pairs)]
    for copy in copies:
        copy.start()
    return copies


def synth_kernel(
    where_ref, mine_ref, theirs_ref, i0, i1, i2, i3, w_in, wp_in,
    sum_ref, n_out, r1_out, qkv_out, p_out, xhat2_out, r2_out,
    n_ref, r1_ref, qkv_ref, p_ref, xhat2_ref, r2_ref,
    e_ref, att_ref, x_ref, posx_ref, w_ref, wp_ref, in_sems, sems,
):
    tiles = SYN // 8
    pairs = [
        (ref.at[32:48, :PIXELS], x_ref.at[16 * k : 16 * k + 16])
        for k, ref in enumerate((i0, i1, i2, i3))
    ]
    loads = copies_of(pairs + [(wp_in, wp_ref), (w_in, w_ref)], in_sems)
    saves = [
        pltpu.make_async_copy(src, dst, sems.at[i])
        for i, (src, dst) in enumerate(
            (
                (n_ref, n_out), (r1_ref, r1_out), (qkv_ref, qkv_out),
                (p_ref, p_out), (xhat2_ref, xhat2_out), (r2_ref, r2_out),
            )
        )
    ]
    spread_position(where_ref, mine_ref, theirs_ref, posx_ref)
    for copy in loads[:5]:
        copy.wait()
    x32 = jnp.concatenate([x_ref[16 * k : 16 * k + 16].astype(F32)[:SLOT] for k in range(4)], axis=0)
    for t, e in enumerate(embed_rows(x32, wp_ref, tiles)):
        rows = slice(128 * t, 128 * t + 128)
        e = e + posx_ref[...]
        e_ref[rows] = e
        xhat, rstd = normalise(e)
        r1_ref[rows] = jnp.broadcast_to(rstd, (128, 128))
        n_ref[rows] = xhat.astype(BF)
    saves[0].start()
    saves[1].start()
    loads[5].wait()
    qkv_product(n_ref, w_ref, qkv_ref, SYN_QKV_UNROLL)
    saves[2].start()
    low = low_half()
    bias = image_bias()

    def score(u):
        rows, at = pl.ds((u // 6) * 128, 128), (u % 6) * 128
        kbd = by_head(qkv_ref[rows, D + at : D + at + 128], low)
        return dot_nt(qkv_ref[rows, at : at + 128], kbd)

    def soften(u, s):
        rows, at = pl.ds((u // 6) * 128, 128), (u % 6) * 256
        parts = [ex / jnp.sum(ex, axis=-1, keepdims=True) for ex in exp_scores(s, bias)]
        p_ref[rows, at : at + 256] = jnp.concatenate(parts, axis=1).astype(BF)

    def weigh(u):
        rows, at = pl.ds((u // 6) * 128, 128), (u % 6) * 128
        vbd = by_head(qkv_ref[rows, 2 * D + at : 2 * D + at + 128], low)
        att_ref[rows, at : at + 128] = dot(p_ref[rows, 2 * at : 2 * at + 256], vbd).astype(BF)

    pipeline(6 * tiles, score, soften, weigh)
    saves[3].start()
    out_product(att_ref, w_ref, e_ref)
    feats = []
    for t in range(tiles):
        rows = slice(128 * t, 128 * t + 128)
        xhat, rstd = normalise(e_ref[rows])
        xhat2_ref[rows] = xhat.astype(BF)
        r2_ref[rows] = jnp.broadcast_to(rstd, (128, 128))
        feats.append(patch_sum(xhat))
    saves[4].start()
    saves[5].start()
    feats = jnp.concatenate(feats, axis=0)
    for s in range(4):
        sum_ref[s : s + 1] = jnp.sum(feats[SLOT * s : SLOT * s + 5], axis=0, keepdims=True)
    for copy in saves:
        copy.wait()


def norm_back(g, xhat, rstd):
    mean_g = jnp.mean(g, axis=-1, keepdims=True)
    mean_gx = jnp.mean(g * xhat, axis=-1, keepdims=True)
    return rstd[:, :1] * (g - mean_g - xhat * mean_gx)


def back_kernel(
    g_ref, w_in, wp_in, n_in, r1_in, qkv_in, p_in, xhat2_in, r2_in,
    out_ref,
    w_ref, wp_ref, n_ref, r1_ref, qkv_ref, p_ref, xhat2_ref, r2_ref,
    dh_ref, dhb_ref, da_ref, dqkv_ref, dn_ref, spread_ref, px_ref, sems,
):
    tiles = SYN // 8
    out_cols = pl.ds(OUT_AT, D)
    loads = copies_of(
        (
            (xhat2_in, xhat2_ref), (r2_in, r2_ref),
            (w_in.at[:, out_cols], w_ref.at[:, out_cols]),
            (qkv_in, qkv_ref), (p_in, p_ref),
            (w_in.at[:, :OUT_AT], w_ref.at[:, :OUT_AT]),
            (n_in, n_ref), (r1_in, r1_ref), (wp_in, wp_ref),
        ),
        sems,
    )
    image = lax.broadcasted_iota(jnp.int32, (SYN, D), 0)
    spread = jnp.zeros((SYN, D), F32)
    for s in range(4):
        mine = (image >= SLOT * s) & (image < SLOT * s + 5)
        spread = jnp.where(mine, g_ref[s : s + 1], spread)
    spread_ref[...] = spread
    loads[0].wait()
    loads[1].wait()

    def second_norm(t):
        rows = pl.ds(mult(128 * t, 128), 128)
        g = spread_ref[pl.ds(mult(8 * t, 8), 8)]
        g = jnp.broadcast_to(g[None], (TOKENS, 8, D)).reshape(128, D)
        dh = norm_back(g, xhat2_ref[rows].astype(F32), r2_ref[rows])
        dh_ref[rows] = dh
        dhb_ref[rows] = dh.astype(BF)

    loop(tiles, second_norm, tiles)
    loads[2].wait()

    def out_back(c):
        at = mult(256 * c, 128)
        da_ref[:, pl.ds(at, 256)] = dot_nt(
            dhb_ref[...], w_ref[pl.ds(at, 256), OUT_AT : OUT_AT + D]
        ).astype(BF)

    loop(3, out_back, 3)
    loads[3].wait()
    loads[4].wait()
    low = low_half()

    def probs_back(u):
        rows, at = pl.ds((u // 6) * 128, 128), (u % 6) * 128
        da = da_ref[rows, at : at + 128]
        return dot_nt(da, by_head(qkv_ref[rows, 2 * D + at : 2 * D + at + 128], low))

    def scores_back(u, dp):
        rows, at = pl.ds((u // 6) * 128, 128), (u % 6) * 128
        da = da_ref[rows, at : at + 128]
        probs = p_ref[rows, 2 * at : 2 * at + 256]
        dv = dot_tn(probs, da)
        dqkv_ref[rows, 2 * D + at : 2 * D + at + 128] = jnp.where(low, dv[:128], dv[128:]).astype(BF)
        p32 = probs.astype(F32)
        ds = []
        for h in range(2):
            ph, dph = p32[:, 128 * h : 128 * h + 128], dp[:, 128 * h : 128 * h + 128]
            inner = jnp.sum(ph * dph, axis=-1, keepdims=True)
            ds.append(ph * (dph - inner))
        return jnp.concatenate(ds, axis=1).astype(BF)

    def query_key_back(u, ds):
        rows, at = pl.ds((u // 6) * 128, 128), (u % 6) * 128
        kbd = by_head(qkv_ref[rows, D + at : D + at + 128], low)
        dqkv_ref[rows, at : at + 128] = (dot(ds, kbd) * 0.125).astype(BF)
        dk = dot_tn(ds, qkv_ref[rows, at : at + 128])
        dqkv_ref[rows, D + at : D + at + 128] = jnp.where(low, dk[:128], dk[128:]).astype(BF)

    pipeline(6 * tiles, probs_back, scores_back, query_key_back)
    loads[5].wait()

    def qkv_back(c):
        at = mult(256 * c, 128)
        rows = pl.ds(at, 256)
        dn = dot_nt(dqkv_ref[:, : 2 * D], w_ref[rows, : 2 * D])
        dn_ref[:, rows] = dn + dot_nt(dqkv_ref[:, 2 * D :], w_ref[rows, COLS : COLS + D])

    loop(3, qkv_back, 3)
    for copy in loads[6:]:
        copy.wait()

    def first_norm(t):
        rows = pl.ds(mult(128 * t, 128), 128)
        de = dh_ref[rows] + norm_back(dn_ref[rows], n_ref[rows].astype(F32), r1_ref[rows])
        de = de.astype(BF)
        even = dot_nt(de[:64], wp_ref[0])
        odd = dot_nt(de[64:], wp_ref[1])
        px_ref[t] = jnp.concatenate(
            [even[:, :128], even[:, 128:] + odd[:, :128], odd[:, 128:]], axis=1
        )

    loop(tiles, first_norm, tiles)
    for j in range(8):
        out_ref[:, 384 * j : 384 * j + 384] = jnp.concatenate(
            [px_ref[t, 8 * j : 8 * j + 8] for t in range(tiles)], axis=0
        ).astype(BF)


SMEM_SPEC = pl.BlockSpec(memory_space=pltpu.SMEM)
VMEM_SPEC = pl.BlockSpec(memory_space=pltpu.VMEM)
ANY_SPEC = pl.BlockSpec(memory_space=pltpu.HBM)


def buffer(shape, kind):
    return pltpu.VMEM(shape, kind)


def run_real(place, mine_pos, their_pos, images, mine, theirs):
    rows = STEP * TOKENS
    return pl.pallas_call(
        real_kernel,
        in_specs=[SMEM_SPEC, VMEM_SPEC, VMEM_SPEC] + [ANY_SPEC] * 20,
        out_specs=[pl.BlockSpec((32, 4, D + 128), lambda: (0, 0, 0)), ANY_SPEC, ANY_SPEC],
        out_shape=[
            jax.ShapeDtypeStruct((32, 4, D + 128), BF),
            jax.ShapeDtypeStruct((D, 2 * COLS), BF),
            jax.ShapeDtypeStruct((2, 256, D), BF),
        ],
        scratch_shapes=[
            buffer((rows, D), F32),
            buffer((rows, D), BF),
            buffer((rows, 3 * D), BF),
            buffer((rows, D), BF),
            buffer((REAL, D + 128), BF),
            buffer((REAL, 128), BF),
            buffer((REAL, PIXELS + 128), BF),
            buffer((128, D), F32),
            buffer((D, 2 * COLS), BF),
            buffer((2, 256, D), BF),
            pltpu.SemaphoreType.DMA((4,)),
        ],
        compiler_params=pltpu.CompilerParams(vmem_limit_bytes=VMEM_LIMIT),
        cost_estimate=pl.CostEstimate(
            flops=14_000_000_000, bytes_accessed=12_000_000, transcendentals=3_000_000
        ),
        name="real_forward",
    )(place, mine_pos, their_pos, *images, *mine, *theirs)


SYN_ROWS = SYN * TOKENS
SAVED = [
    ((SYN_ROWS, D), BF),
    ((SYN_ROWS, 128), F32),
    ((SYN_ROWS, 3 * D), BF),
    ((SYN_ROWS, 2 * D), BF),
    ((SYN_ROWS, D), BF),
    ((SYN_ROWS, 128), F32),
]
WEIGHTS = [((D, 2 * COLS), BF), ((2, 256, D), BF)]


def run_synth(place, mine_pos, their_pos, images, w, wp):
    return pl.pallas_call(
        synth_kernel,
        in_specs=[SMEM_SPEC, VMEM_SPEC, VMEM_SPEC] + [ANY_SPEC] * 6,
        out_specs=[pl.BlockSpec((4, D), lambda: (0, 0))] + [ANY_SPEC] * 6,
        out_shape=[jax.ShapeDtypeStruct((4, D), F32)]
        + [jax.ShapeDtypeStruct(s, t) for s, t in SAVED],
        scratch_shapes=[buffer(s, t) for s, t in SAVED]
        + [
            buffer((SYN_ROWS, D), F32),
            buffer((SYN_ROWS, D), BF),
            buffer((64, PIXELS), BF),
            buffer((128, D), F32),
        ]
        + [buffer(s, t) for s, t in WEIGHTS]
        + [pltpu.SemaphoreType.DMA((6,)), pltpu.SemaphoreType.DMA((6,))],
        compiler_params=pltpu.CompilerParams(vmem_limit_bytes=VMEM_LIMIT),
        cost_estimate=pl.CostEstimate(
            flops=3_000_000_000, bytes_accessed=12_000_000, transcendentals=600_000
        ),
        name="synth_forward",
    )(place, mine_pos, their_pos, *images, w, wp)


def run_back(g, w, wp, saved):
    return pl.pallas_call(
        back_kernel,
        in_specs=[VMEM_SPEC] + [ANY_SPEC] * 8,
        out_specs=pl.BlockSpec((SYN, PIXELS), lambda: (0, 0)),
        out_shape=jax.ShapeDtypeStruct((SYN, PIXELS), BF),
        scratch_shapes=[buffer(s, t) for s, t in WEIGHTS + SAVED]
        + [
            buffer((SYN_ROWS, D), F32),
            buffer((SYN_ROWS, D), BF),
            buffer((SYN_ROWS, D), BF),
            buffer((SYN_ROWS, 3 * D), BF),
            buffer((SYN_ROWS, D), F32),
            buffer((SYN, D), F32),
            buffer((SYN // 8, 64, 384), F32),
            pltpu.SemaphoreType.DMA((9,)),
        ],
        compiler_params=pltpu.CompilerParams(vmem_limit_bytes=VMEM_LIMIT),
        cost_estimate=pl.CostEstimate(
            flops=4_000_000_000, bytes_accessed=12_000_000, transcendentals=0
        ),
        name="synth_backward",
    )(g, w, wp, *saved)


def gather_weights(core, x, patch_weight, qkv_weight, out_weight, images):
    columns = jnp.concatenate([qkv_weight, out_weight], axis=-1)
    patch = jnp.pad(patch_weight.reshape(2, 3, 2, 3, 128), ((0, 0),) * 3 + ((0, 1), (0, 0)))
    patch = patch.transpose(0, 1, 3, 2, 4).reshape(2, 12, 2, 128)
    both = jnp.concatenate([columns.reshape(2, 12, 2, 2 * D), patch], axis=-1)
    both = both.transpose(0, 2, 1, 3).reshape(4, 12, COLS)
    parts = []
    for k in range(4):
        to = (x - k) % 4
        first = to // 2 == core
        index = (to % 2) * 2 + jnp.where(first, 0, 1)

        def target(c, yy, zz, xx, k=k):
            to = (xx - k) % 4
            return (0, yy, zz, to) if to // 2 == c else (1, yy, zz, (to + 2) % 4)

        parts.append(permute(lax.dynamic_index_in_dim(both, index, 0, keepdims=False), target))
    ring = jnp.roll(jnp.stack(parts), x + 2 * core, axis=0).reshape(BLOCK_ROWS, COLS)
    near, far = (
        jnp.stack([ring, from_first(ring, 1)]),
        jnp.stack([from_first(ring, 2), from_first(ring, 3)]),
    )
    next_near, last_far = from_second(near, 1), from_second(far, 3)
    next_far, last_near = from_second(far, 1), from_second(near, 3)
    over_near, over_far = from_second(next_near, 1), from_second(last_far, 3)
    over_far, *images = lax.optimization_barrier((over_far, *images))
    mine = [near, far, next_near, next_far, over_near, over_far, last_near, last_far]
    theirs = [swap_cores(a) for a in mine]
    return mine, theirs, images


def local(
    real_images, real_labels, class_ids, synthetic, patch_weight, position, qkv_weight, out_weight
):
    core, img = lax.axis_index("enc"), lax.axis_index("img")
    y, z, x = img // 16, (img // 4) % 4, img % 4
    place = jnp.stack([core, y, z, x]).astype(jnp.int32)

    hit = real_labels[:, None] == class_ids[None, :]
    index = jnp.sum(jnp.where(hit, jnp.arange(64, dtype=F32)[None, :], 0.0), axis=1)
    tagged = jnp.concatenate(
        [real_images, jnp.broadcast_to(index[:, None], (64, 128)).astype(BF)], axis=1
    )
    syn = lax.dynamic_slice_in_dim(synthetic, 5 * core, 5, 0).astype(BF)
    images = jnp.concatenate(
        [lax.dynamic_slice_in_dim(tagged, 32 * core, 32, 0), jnp.pad(syn, ((0, 11), (0, 128)))],
        axis=0,
    )
    after = from_x(images, 1)
    images = [images, after, from_x(after, 1), from_x(images, 3)]
    their_pos = swap_cores(position)

    mine, theirs, images = gather_weights(
        core, x, patch_weight, qkv_weight, out_weight, images
    )
    csum, w, wp = run_real(place, position, their_pos, images, mine, theirs)

    groups = [[c * 64 + yz * 4 + xx for c in range(2) for yz in range(16)] for xx in range(4)]
    got = lax.all_to_all(csum, AXES, 0, 0, axis_index_groups=groups)
    total = jnp.sum(got.astype(F32), axis=0)
    means = total[:, :D] / jnp.maximum(total[:, D : D + 1], 1.0)

    own, *saved = run_synth(place, position, their_pos, images, w, wp)
    syn_mean = (own + swap_cores(own)) * (1.0 / IPC)
    g = (syn_mean - jnp.roll(means, -x, axis=0)) * (2.0 / (IPC * TOKENS))
    grads = run_back(g, w, wp, saved)

    sent = []
    for m in range(2):
        row = lax.dynamic_index_in_dim(means, (x - m) % 2 + 2 * core, 0, keepdims=True)
        sent.append(
            permute(row, lambda c, yy, zz, xx, m=m: (xx // 2, yy, zz, (xx - m) % 2 + 2 * c))
        )
    first = jnp.where(x % 2 == 0, sent[0], sent[1])
    second = jnp.where(x % 2 == 0, sent[1], sent[0])
    real_means = jnp.stack([first, second])

    grads = grads.reshape(4, SLOT, PIXELS)
    pixel = grads[0].astype(F32)
    for k in (1, 2, 3):
        pixel = pixel + from_x(grads[k], -k).astype(F32)
    pixel = pixel[:5]
    other = swap_cores(pixel)
    pixel_grad = jnp.concatenate(
        [jnp.where(core == 0, pixel, other), jnp.where(core == 0, other, pixel)], axis=0
    )
    return (real_means, pixel_grad)


def solution(mesh):
    return jax.shard_map(
        local,
        mesh=mesh,
        in_specs=(
            P("img", None),
            P("img"),
            P(),
            P("img", None),
            P("enc", "img", None),
            P("enc", None, None),
            P("enc", "img", None),
            P("enc", "img", None),
        ),
        out_specs=(P("enc", "img", None), P("img", None)),
        check_vma=False,
    )
```

time: 133 us -> 125 us (0.940)
  Pallas kernels: 56.4 us -> 42.7 us
  starting transfers between devices: 36.8 us -> 45 us
  local copies, waits for them, and re-layouts: 7.89 us -> 2.48 us
  waiting for transfers between devices: 25.9 us -> 27.8 us
    pallas_call x3, Pallas kernels: 56.4 us -> 42.7 us  [the longest x1 24 us: run_real(): pl.pallas_call(real_kernel, in_specs=[SMEM_SPEC, VMEM_SPEC, VMEM_SPEC] +...]
    ppermute x26 -> x32, starting transfers between devices: 33.1 us -> 38.2 us  [permute(): lax.ppermute(a, AXES, [(flat(*p), flat(*target(*p))) for p in PLACES])]
    reshape x7 -> x0, local copies, waits for them, and re-layouts: 4.64 us -> none  [the longest x1 1.57 us: local(): csum.reshape(16, 4, D + 128)]
    all_to_all x1, starting transfers between devices: 3.69 us -> 6.74 us  [local(): got = lax.all_to_all(csum, AXES, 0, 0, axis_index_groups=groups)]
    ppermute x26 -> x32, waiting for transfers between devices: 25.9 us -> 27.7 us  [permute(): lax.ppermute(a, AXES, [(flat(*p), flat(*target(*p))) for p in PLACES])]
  transfers between devices with their start and end apart: 27 -> 33, of which waited for: 11 -> 14; matrix products, arithmetic and copies ran while one was open for 5% -> 3% of each run, Pallas kernels for 18% -> 15%
where the time goes in v2:
time: 125 us; the launch traced here: 124 us
  starting transfers between devices  45 us (36%)
  Pallas kernels  42.7 us (34%)
  waiting for transfers between devices  27.8 us (22%)
  other arithmetic  5.07 us (4%)
  local copies, waits for them, and re-layouts  2.48 us (2%)
  between operations  1.31 us (1%)
    ppermute x32, starting transfers between devices, permute(): lax.ppermute(a, AXES, [(flat(*p), flat(*target(*p))) for p in PLACES])  38.2 us
    ppermute x32, waiting for transfers between devices, permute(): lax.ppermute(a, AXES, [(flat(*p), flat(*target(*p))) for p in PLACES])  27.7 us
    pallas_call x1, Pallas kernels, run_real(): pl.pallas_call(real_kernel, in_specs=[SMEM_SPEC, VMEM_SPEC, VMEM_SPEC] +...  24 us
    pallas_call x1, Pallas kernels, run_back(): pl.pallas_call(back_kernel, in_specs=[VMEM_SPEC] + [ANY_SPEC] * 8, out_sp...  9.64 us
    pallas_call x1, Pallas kernels, run_synth(): pl.pallas_call(synth_kernel, in_specs=[SMEM_SPEC, VMEM_SPEC, VMEM_SPEC] +...  9.12 us
    all_to_all x1, starting transfers between devices, local(): got = lax.all_to_all(csum, AXES, 0, 0, axis_index_groups=groups)  6.74 us
  transfers between devices with their start and end apart: 33, of which 14 were waited for; matrix products, arithmetic and copies ran while one was open for 3% of the time, Pallas kernels for 15%

profile of v2, /device:TPU:1, one launch (start us, length us, event | category | flops | bytes accessed | tf_op | source)
XLA Modules:
  0.0 124.3 jit_solution(6158929639371594288)
XLA Ops:
  0.9 0.7 reshape.32
  1.7 1.1 pad_maximum_fusion.3
  3.1 3.4 %collective-permute-start.4 = (bf16[12,1664]{1,0:T(8,128)(2,1)S(1)}, bf16[12,1664]{1,0:T(8,128)(2,1)S(1)}, u32[]{:S(2)}, u32[]{:S(2)}) collective-permute-start(bf16[12,1664]{1,0:T(8,128)(2,1)S(1)} %get-tuple-element.32), channel_id=1, source_target_pairs={{0,1},{1,64},{2,65},{3,0},{4,5},{5,68},{6,69},{7,4},{8,9},{9,72},{... | collective-permute-start | bytes 119816 | tf_op jit(solution)/shard_map/ppermute | solution.py:35
  6.4 2.7 %collective-permute-start.3 = (bf16[12,1664]{1,0:T(8,128)(2,1)S(1)}, bf16[12,1664]{1,0:T(8,128)(2,1)S(1)}, u32[]{:S(2)}, u32[]{:S(2)}) collective-permute-start(bf16[12,1664]{1,0:T(8,128)(2,1)S(1)} %get-tuple-element.33), channel_id=1, source_target_pairs={{0,64},{1,65},{2,0},{3,1},{4,68},{5,69},{6,4},{7,5},{8,72},{9,73},... | collective-permute-start | bytes 119816 | tf_op jit(solution)/shard_map/ppermute | solution.py:35
  9.2 1.2 collective-permute-start.2
  10.4 1.9 %collective-permute-start.1 = (bf16[12,1664]{1,0:T(8,128)(2,1)S(1)}, bf16[12,1664]{1,0:T(8,128)(2,1)S(1)}, u32[]{:S(2)}, u32[]{:S(2)}) collective-permute-start(bf16[12,1664]{1,0:T(8,128)(2,1)S(1)} %get-tuple-element.35), channel_id=1, source_target_pairs={{0,0},{1,1},{2,64},{3,65},{4,4},{5,5},{6,68},{7,69},{8,8},{9,9},{1... | collective-permute-start | bytes 119816 | tf_op jit(solution)/shard_map/ppermute | solution.py:35
  12.7 4.7 %collective-permute-done.1 = bf16[12,1664]{1,0:T(8,128)(2,1)S(1)} collective-permute-done((bf16[12,1664]{1,0:T(8,128)(2,1)S(1)}, bf16[12,1664]{1,0:T(8,128)(2,1)S(1)}, u32[]{:S(2)}, u32[]{:S(2)}) %collective-permute-start.1) | collective-permute-done | bytes 39968 | tf_op jit(solution)/shard_map/ppermute | solution.py:35
  17.6 1.7 %collective-permute-start.6 = (bf16[48,1664]{1,0:T(8,128)(2,1)S(1)}, bf16[48,1664]{1,0:T(8,128)(2,1)S(1)}, u32[]{:S(2)}, u32[]{:S(2)}) collective-permute-start(bf16[48,1664]{1,0:T(8,128)(2,1)S(1)} %reshape.35), channel_id=1, source_target_pairs={{0,16},{1,17},{2,18},{3,19},{4,20},{5,21},{6,22},{7,23},{8,24},{9,... | collective-permute-start | bytes 479240 | tf_op jit(solution)/shard_map/ppermute | solution.py:35
  19.3 3.3 %collective-permute-start.5 = (bf16[48,1664]{1,0:T(8,128)(2,1)S(1)}, bf16[48,1664]{1,0:T(8,128)(2,1)S(1)}, u32[]{:S(2)}, u32[]{:S(2)}) collective-permute-start(bf16[48,1664]{1,0:T(8,128)(2,1)S(1)} %reshape.35), channel_id=1, source_target_pairs={{0,32},{1,33},{2,34},{3,35},{4,36},{5,37},{6,38},{7,39},{8,40},{9,... | collective-permute-start | bytes 479240 | tf_op jit(solution)/shard_map/ppermute | solution.py:35
  22.6 0.8 collective-permute-start.12
  23.4 0.7 collective-permute-done.6
  24.1 2.9 %collective-permute-done.5 = bf16[48,1664]{1,0:T(8,128)(2,1)S(1)} collective-permute-done((bf16[48,1664]{1,0:T(8,128)(2,1)S(1)}, bf16[48,1664]{1,0:T(8,128)(2,1)S(1)}, u32[]{:S(2)}, u32[]{:S(2)}) %collective-permute-start.5) | collective-permute-done | bytes 159776 | tf_op jit(solution)/shard_map/ppermute | solution.py:35
  27.0 1.4 %collective-permute-start.7 = (bf16[2,48,1664]{2,1,0:T(8,128)(2,1)S(1)}, bf16[2,48,1664]{2,1,0:T(8,128)(2,1)S(1)}, u32[]{:S(2)}, u32[]{:S(2)}) collective-permute-start(bf16[2,48,1664]{2,1,0:T(8,128)(2,1)S(1)} %pad_maximum_fusion.l1), channel_id=1, source_target_pairs={{0,4},{1,5},{2,6},{3,7},{4,8},{5,9},{6,10},{7,11},{8,12},{9,13},{1... | collective-permute-start | bytes 958472 | tf_op jit(solution)/shard_map/ppermute | solution.py:35
  28.4 0.6 collective-permute-start.9
  29.1 1.5 %collective-permute-start.14 = (bf16[2,48,1664]{2,1,0:T(8,128)(2,1)S(1)}, bf16[2,48,1664]{2,1,0:T(8,128)(2,1)S(1)}, u32[]{:S(2)}, u32[]{:S(2)}) collective-permute-start(bf16[2,48,1664]{2,1,0:T(8,128)(2,1)S(1)} %pad_maximum_fusion.l1), channel_id=1, source_target_pairs={{0,12},{1,13},{2,14},{3,15},{4,0},{5,1},{6,2},{7,3},{8,4},{9,5},{1... | collective-permute-start | bytes 958472 | tf_op jit(solution)/shard_map/ppermute | solution.py:35
  30.7 1.5 %collective-permute-start.13 = (bf16[2,48,1664]{2,1,0:T(8,128)(2,1)S(1)}, bf16[2,48,1664]{2,1,0:T(8,128)(2,1)S(1)}, u32[]{:S(2)}, u32[]{:S(2)}) collective-permute-start(bf16[2,48,1664]{2,1,0:T(8,128)(2,1)S(1)} %pad_maximum_fusion.1.l0), channel_id=1, source_target_pairs={{0,12},{1,13},{2,14},{3,15},{4,0},{5,1},{6,2},{7,3},{8,4},{9,5},{1... | collective-permute-start | bytes 958472 | tf_op jit(solution)/shard_map/ppermute | solution.py:35
  32.2 2.1 %collective-permute-done.7.l7 = bf16[2,48,1664]{2,1,0:T(8,128)(2,1)S(1)} collective-permute-done((bf16[2,48,1664]{2,1,0:T(8,128)(2,1)S(1)}, bf16[2,48,1664]{2,1,0:T(8,128)(2,1)S(1)}, u32[]{:S(2)}, u32[]{:S(2)}) %collective-permute-start.7) | collective-permute-done | bytes 319520 | tf_op jit(solution)/shard_map/ppermute | solution.py:35
  34.5 1.4 %collective-permute-done.9.i1 = bf16[48,3200]{1,0:T(8,128)(2,1)} collective-permute-done((bf16[48,3200]{1,0:T(8,128)(2,1)S(1)}, bf16[48,3200]{1,0:T(8,128)(2,1)}, u32[]{:S(2)}, u32[]{:S(2)}) %collective-permute-start.9) | collective-permute-done | bytes 307232 | tf_op jit(solution)/shard_map/ppermute | solution.py:35
  35.9 3.3 %collective-permute-start.10 = (bf16[48,3200]{1,0:T(8,128)(2,1)}, bf16[48,3200]{1,0:T(8,128)(2,1)}, u32[]{:S(2)}, u32[]{:S(2)}) collective-permute-start(bf16[48,3200]{1,0:T(8,128)(2,1)} %collective-permute-done.9.i1), channel_id=1, source_target_pairs={{0,3},{1,0},{2,1},{3,2},{4,7},{5,4},{6,5},{7,6},{8,11},{9,8},{10,9... | collective-permute-start | bytes 921608 | tf_op jit(solution)/shard_map/ppermute | solution.py:35
  39.3 4.5 %collective-permute-done.11.i3 = bf16[48,3200]{1,0:T(8,128)(2,1)S(1)} collective-permute-done((bf16[48,3200]{1,0:T(8,128)(2,1)S(1)}, bf16[48,3200]{1,0:T(8,128)(2,1)S(1)}, u32[]{:S(2)}, u32[]{:S(2)}) %collective-permute-start.11) | collective-permute-done | bytes 307232 | tf_op jit(solution)/shard_map/ppermute | solution.py:35
  43.8 0.5 collective-permute-start.17
  44.3 0.4 collective-permute-start.16
  44.8 1.1 collective-permute-done.10.i2
  45.8 1.2 collective-permute-start.20
  47.1 0.8 collective-permute-start.24
  48.0 3.8 %collective-permute-done.16.l6 = bf16[2,48,1664]{2,1,0:T(8,128)(2,1)} collective-permute-done((bf16[2,48,1664]{2,1,0:T(8,128)(2,1)S(1)}, bf16[2,48,1664]{2,1,0:T(8,128)(2,1)}, u32[]{:S(2)}, u32[]{:S(2)}) %collective-permute-start.16) | collective-permute-done | bytes 319520 | tf_op jit(solution)/shard_map/ppermute | solution.py:35
  51.8 0.9 collective-permute-start.23
  52.8 0.5 collective-permute-done.15.l4
  53.5 0.8 collective-permute-start.21
  54.2 0.6 pad_add_fusion.where_ref
  54.9 1.0 collective-permute-done.21.o4
  55.9 24.0 %real_forward.1 = (bf16[32,4,896]{2,1,0:T(4,128)(2,1)}, bf16[768,3328]{1,0:T(8,128)(2,1)}, bf16[2,256,768]{2,1,0:T(8,128)(2,1)}) custom-call(s32[4]{0:T(128)} %pad_add_fusion.where_ref, bf16[2,16,768]{2,1,0:T(8,128)(2,1)} %mine_ref.3, bf16[2,16,768]{2,1,0:T(8,128)(2,1)} %copy-done.14, bf16[48,3200]{1,0:T(8,128)(2,1)} %copy-done.4, ...), custom_call_target="tpu_custom_call" | custom-call | flops 14000000000 | bytes 12000000 | tf_op jit(solution)/shard_map/real_forward/pallas_call | solution.py:462
  79.9 6.7 %all-to-all-start = ((bf16[32,4,896]{2,1,0:T(4,128)(2,1)}), bf16[32,4,896]{2,1,0:T(4,128)(2,1)S(1)}, u32[]{:S(2)}, u32[]{:S(2)}) async-start(bf16[32,4,896]{2,1,0:T(4,128)(2,1)} %get-tuple-element.22), calls=%async_computation | async-start | bytes 458752 | tf_op jit(solution)/shard_map/all_to_all | solution.py:611
  86.6 9.1 %synth_forward.1 = (f32[4,768]{1,0:T(4,128)}, bf16[384,768]{1,0:T(8,128)(2,1)}, f32[384,128]{1,0:T(8,128)}, bf16[384,2304]{1,0:T(8,128)(2,1)}, bf16[384,1536]{1,...) custom-call(s32[4]{0:T(128)} %pad_add_fusion.where_ref, bf16[2,16,768]{2,1,0:T(8,128)(2,1)} %mine_ref.3, ...), custom_call_target="tpu_custom_call" | custom-call | flops 3000000000 | bytes 12000000 | tf_op jit(solution)/shard_map/synth_forward/pallas_call | solution.py:505
  95.8 0.5 collective-permute-start.27
  96.6 3.8 %collective-permute-start.25 = (f32[1,768]{1,0:T(1,128)S(1)}, f32[1,768]{1,0:T(1,128)S(1)}, u32[]{:S(2)}, u32[]{:S(2)}) collective-permute-start(f32[1,768]{1,0:T(1,128)S(1)} %get-tuple-element.42), channel_id=1, source_target_pairs={{0,0},{1,1},{2,64},{3,65},{4,4},{5,5},{6,68},{7,69},{8,8},{9,9},{1... | collective-permute-start | bytes 9224 | tf_op jit(solution)/shard_map/ppermute | solution.py:35
  100.4 1.6 %collective-permute-start.26 = (f32[1,768]{1,0:T(1,128)S(1)}, f32[1,768]{1,0:T(1,128)S(1)}, u32[]{:S(2)}, u32[]{:S(2)}) collective-permute-start(f32[1,768]{1,0:T(1,128)S(1)} %get-tuple-element.43), channel_id=1, source_target_pairs={{0,1},{1,0},{2,65},{3,64},{4,5},{5,4},{6,69},{7,68},{8,9},{9,8},{1... | collective-permute-start | bytes 9224 | tf_op jit(solution)/shard_map/ppermute | solution.py:35
  102.0 1.3 %fusion.5.g_ref = f32[4,768]{1,0:T(4,128)} fusion(s32[]{:T(128)S(6)} %select_n.201, f32[4,768]{1,0:T(4,128)S(1)} %slice_divide_fusion, f32[4,768]{1,0:T(4,128)} %get-tuple-element.25, f32[4,768]{1,0:T(4,128)S(1)} %collective-permute-done.27), kind=kLoop, calls=%fused_computation.33 | loop fusion | flops 15360 | bytes 49156 | tf_op jit(solution)/shard_map/mul | solution.py:617
  103.3 9.6 %synth_backward.1 = bf16[24,3072]{1,0:T(8,128)(2,1)} custom-call(f32[4,768]{1,0:T(4,128)} %fusion.5.g_ref, bf16[768,3328]{1,0:T(8,128)(2,1)} %get-tuple-element.23.w_in, bf16[2,256,768]{2,1,0:T(8,128)(2,1)} %get-tuple-element.24.wp_in, bf16[384,768]{1,0:T(8,128)(2,1)} %get-tuple-element.26.n_in, f32[384,128]{1,0:T(8,128)} %get-tuple-element.27.r1_in, ...), custom_call_target="tpu_custom_call" | custom-call | flops 4000000000 | bytes 12000000 | tf_op jit(solution)/shard_map/synth_backward/pallas_call | solution.py:529
  113.0 1.0 fusion.9
  114.1 2.4 %collective-permute-start.29 = (bf16[6,3072]{1,0:T(8,128)(2,1)S(1)}, bf16[6,3072]{1,0:T(8,128)(2,1)S(1)}, u32[]{:S(2)}, u32[]{:S(2)}) collective-permute-start(bf16[6,3072]{1,0:T(8,128)(2,1)S(1)} %get-tuple-element.40), channel_id=1, source_target_pairs={{0,2},{1,3},{2,0},{3,1},{4,6},{5,7},{6,4},{7,5},{8,10},{9,11},{10,... | collective-permute-start | bytes 110600 | tf_op jit(solution)/shard_map/ppermute | solution.py:35
  116.5 0.5 collective-permute-done.30
  117.0 1.6 %collective-permute-done.29 = bf16[6,3072]{1,0:T(8,128)(2,1)S(1)} collective-permute-done((bf16[6,3072]{1,0:T(8,128)(2,1)S(1)}, bf16[6,3072]{1,0:T(8,128)(2,1)S(1)}, u32[]{:S(2)}, u32[]{:S(2)}) %collective-permute-start.29) | collective-permute-done | bytes 36896 | tf_op jit(solution)/shard_map/ppermute | solution.py:35
  118.6 2.6 %collective-permute-done.28 = bf16[6,3072]{1,0:T(8,128)(2,1)S(1)} collective-permute-done((bf16[6,3072]{1,0:T(8,128)(2,1)S(1)}, bf16[6,3072]{1,0:T(8,128)(2,1)S(1)}, u32[]{:S(2)}, u32[]{:S(2)}) %collective-permute-start.28) | collective-permute-done | bytes 36896 | tf_op jit(solution)/shard_map/ppermute | solution.py:35
  121.2 1.4 %collective-permute-start.31 = (f32[5,3072]{1,0:T(8,128)S(1)}, f32[5,3072]{1,0:T(8,128)S(1)}, u32[]{:S(2)}, u32[]{:S(2)}) collective-permute-start(f32[5,3072]{1,0:T(8,128)S(1)} %convert_add_fusion), channel_id=1, source_target_pairs={{0,64},{1,65},{2,66},{3,67},{4,68},{5,69},{6,70},{7,71},{8,72},{9,... | collective-permute-start | bytes 184328 | tf_op jit(solution)/shard_map/ppermute | solution.py:35
  122.6 0.6 pad_maximum_fusion.4
  123.2 0.3 collective-permute-done.31
  123.6 0.7 pad_maximum_fusion.2
  (93 shorter events, 2.1 us)
Async XLA Ops:
  0.6 22.0 %copy-start = (f32[10,3072]{1,0:T(8,128)S(1)}, f32[10,3072]{1,0:T(8,128)}, u32[]{:S(2)}) copy-start(f32[10,3072]{1,0:T(8,128)} %param.11) | copy-start | bytes 368644
  0.6 11.7 %copy-start.15 = (s32[64]{0:T(128)S(1)}, s32[64]{0:T(128)}, u32[]{:S(2)}) copy-start(s32[64]{0:T(128)} %param.10) | copy-start | bytes 772
  0.7 11.7 %copy-start.16 = (s32[64]{0:T(128)S(1)}, s32[64]{0:T(128)}, u32[]{:S(2)}) copy-start(s32[64]{0:T(128)} %param.9) | copy-start | bytes 772
  0.7 11.9 %copy-start.1 = (bf16[64,3072]{1,0:T(8,128)(2,1)S(1)}, bf16[64,3072]{1,0:T(8,128)(2,1)}, u32[]{:S(2)}) copy-start(bf16[64,3072]{1,0:T(8,128)(2,1)} %param.8) | copy-start | bytes 1179652
  3.1 14.4 %collective-permute-start.4 = (bf16[12,1664]{1,0:T(8,128)(2,1)S(1)}, bf16[12,1664]{1,0:T(8,128)(2,1)S(1)}, u32[]{:S(2)}, u32[]{:S(2)}) collective-permute-start(bf16[12,1664]{1,0:T(8,128)(2,1)S(1)} %get-tuple-element.32), channel_id=1, source_target_pairs={{0,1},{1,64},{2,65},{3,0},{4,5},{5,68},{6,69},{7,4},{8,9},{9,72},{... | collective-permute-start | bytes 119816 | tf_op jit(solution)/shard_map/ppermute | solution.py:35
  6.4 10.9 %collective-permute-start.3 = (bf16[12,1664]{1,0:T(8,128)(2,1)S(1)}, bf16[12,1664]{1,0:T(8,128)(2,1)S(1)}, u32[]{:S(2)}, u32[]{:S(2)}) collective-permute-start(bf16[12,1664]{1,0:T(8,128)(2,1)S(1)} %get-tuple-element.33), channel_id=1, source_target_pairs={{0,64},{1,65},{2,0},{3,1},{4,68},{5,69},{6,4},{7,5},{8,72},{9,73},... | collective-permute-start | bytes 119816 | tf_op jit(solution)/shard_map/ppermute | solution.py:35
  9.2 8.2 %collective-permute-start.2 = (bf16[12,1664]{1,0:T(8,128)(2,1)S(1)}, bf16[12,1664]{1,0:T(8,128)(2,1)S(1)}, u32[]{:S(2)}, u32[]{:S(2)}) collective-permute-start(bf16[12,1664]{1,0:T(8,128)(2,1)S(1)} %get-tuple-element.34), channel_id=1, source_target_pairs={{0,65},{1,0},{2,1},{3,64},{4,69},{5,4},{6,5},{7,68},{8,73},{9,8},{... | collective-permute-start | bytes 119816 | tf_op jit(solution)/shard_map/ppermute | solution.py:35
  10.4 6.9 %collective-permute-start.1 = (bf16[12,1664]{1,0:T(8,128)(2,1)S(1)}, bf16[12,1664]{1,0:T(8,128)(2,1)S(1)}, u32[]{:S(2)}, u32[]{:S(2)}) collective-permute-start(bf16[12,1664]{1,0:T(8,128)(2,1)S(1)} %get-tuple-element.35), channel_id=1, source_target_pairs={{0,0},{1,1},{2,64},{3,65},{4,4},{5,5},{6,68},{7,69},{8,8},{9,9},{1... | collective-permute-start | bytes 119816 | tf_op jit(solution)/shard_map/ppermute | solution.py:35
  12.6 16.4 %copy-start.13 = (bf16[2,16,768]{2,1,0:T(8,128)(2,1)S(1)}, bf16[2,16,768]{2,1,0:T(8,128)(2,1)}, u32[]{:S(2)}) copy-start(bf16[2,16,768]{2,1,0:T(8,128)(2,1)} %mine_ref.3) | copy-start | bytes 147460
  17.6 6.5 %collective-permute-start.6 = (bf16[48,1664]{1,0:T(8,128)(2,1)S(1)}, bf16[48,1664]{1,0:T(8,128)(2,1)S(1)}, u32[]{:S(2)}, u32[]{:S(2)}) collective-permute-start(bf16[48,1664]{1,0:T(8,128)(2,1)S(1)} %reshape.35), channel_id=1, source_target_pairs={{0,16},{1,17},{2,18},{3,19},{4,20},{5,21},{6,22},{7,23},{8,24},{9,... | collective-permute-start | bytes 479240 | tf_op jit(solution)/shard_map/ppermute | solution.py:35
  19.3 7.7 %collective-permute-start.5 = (bf16[48,1664]{1,0:T(8,128)(2,1)S(1)}, bf16[48,1664]{1,0:T(8,128)(2,1)S(1)}, u32[]{:S(2)}, u32[]{:S(2)}) collective-permute-start(bf16[48,1664]{1,0:T(8,128)(2,1)S(1)} %reshape.35), channel_id=1, source_target_pairs={{0,32},{1,33},{2,34},{3,35},{4,36},{5,37},{6,38},{7,39},{8,40},{9,... | collective-permute-start | bytes 479240 | tf_op jit(solution)/shard_map/ppermute | solution.py:35
  22.6 8.0 %collective-permute-start.12 = (bf16[48,1664]{1,0:T(8,128)(2,1)S(1)}, bf16[48,1664]{1,0:T(8,128)(2,1)S(1)}, u32[]{:S(2)}, u32[]{:S(2)}) collective-permute-start(bf16[48,1664]{1,0:T(8,128)(2,1)S(1)} %reshape.35), channel_id=1, source_target_pairs={{0,48},{1,49},{2,50},{3,51},{4,52},{5,53},{6,54},{7,55},{8,56},{9,... | collective-permute-start | bytes 479240 | tf_op jit(solution)/shard_map/ppermute | solution.py:35
  27.0 28.8 %copy-start.2 = (bf16[2,48,1664]{2,1,0:T(8,128)(2,1)}, bf16[2,48,1664]{2,1,0:T(8,128)(2,1)S(1)}, u32[]{:S(2)}) copy-start(bf16[2,48,1664]{2,1,0:T(8,128)(2,1)S(1)} %pad_maximum_fusion.l1) | copy-start | bytes 958468
  27.0 7.3 %collective-permute-start.7 = (bf16[2,48,1664]{2,1,0:T(8,128)(2,1)S(1)}, bf16[2,48,1664]{2,1,0:T(8,128)(2,1)S(1)}, u32[]{:S(2)}, u32[]{:S(2)}) collective-permute-start(bf16[2,48,1664]{2,1,0:T(8,128)(2,1)S(1)} %pad_maximum_fusion.l1), channel_id=1, source_target_pairs={{0,4},{1,5},{2,6},{3,7},{4,8},{5,9},{6,10},{7,11},{8,12},{9,13},{1... | collective-permute-start | bytes 958472 | tf_op jit(solution)/shard_map/ppermute | solution.py:35
  28.4 27.4 %copy-start.4 = (bf16[48,3200]{1,0:T(8,128)(2,1)}, bf16[48,3200]{1,0:T(8,128)(2,1)S(1)}, u32[]{:S(2)}) copy-start(bf16[48,3200]{1,0:T(8,128)(2,1)S(1)} %fusion.1.i0) | copy-start | bytes 921604
  28.4 7.5 %collective-permute-start.9 = (bf16[48,3200]{1,0:T(8,128)(2,1)S(1)}, bf16[48,3200]{1,0:T(8,128)(2,1)}, u32[]{:S(2)}, u32[]{:S(2)}) collective-permute-start(bf16[48,3200]{1,0:T(8,128)(2,1)S(1)} %fusion.1.i0), channel_id=1, source_target_pairs={{0,3},{1,0},{2,1},{3,2},{4,7},{5,4},{6,5},{7,6},{8,11},{9,8},{10,9... | collective-permute-start | bytes 921608 | tf_op jit(solution)/shard_map/ppermute | solution.py:35
  29.0 5.5 %collective-permute-start = (bf16[2,16,768]{2,1,0:T(8,128)(2,1)S(1)}, bf16[2,16,768]{2,1,0:T(8,128)(2,1)S(1)}, u32[]{:S(2)}, u32[]{:S(2)}) collective-permute-start(bf16[2,16,768]{2,1,0:T(8,128)(2,1)S(1)} %copy-done.13), channel_id=1, source_target_pairs={{0,64},{1,65},{2,66},{3,67},{4,68},{5,69},{6,70},{7,71},{8,72},{9,... | collective-permute-start | bytes 147464 | tf_op jit(solution)/shard_map/ppermute | solution.py:35
  29.1 14.8 %collective-permute-start.14 = (bf16[2,48,1664]{2,1,0:T(8,128)(2,1)S(1)}, bf16[2,48,1664]{2,1,0:T(8,128)(2,1)S(1)}, u32[]{:S(2)}, u32[]{:S(2)}) collective-permute-start(bf16[2,48,1664]{2,1,0:T(8,128)(2,1)S(1)} %pad_maximum_fusion.l1), channel_id=1, source_target_pairs={{0,12},{1,13},{2,14},{3,15},{4,0},{5,1},{6,2},{7,3},{8,4},{9,5},{1... | collective-permute-start | bytes 958472 | tf_op jit(solution)/shard_map/ppermute | solution.py:35
  30.6 25.2 %copy-start.3 = (bf16[2,48,1664]{2,1,0:T(8,128)(2,1)}, bf16[2,48,1664]{2,1,0:T(8,128)(2,1)S(1)}, u32[]{:S(2)}) copy-start(bf16[2,48,1664]{2,1,0:T(8,128)(2,1)S(1)} %pad_maximum_fusion.1.l0) | copy-start | bytes 958468
  30.7 13.7 %collective-permute-start.13 = (bf16[2,48,1664]{2,1,0:T(8,128)(2,1)S(1)}, bf16[2,48,1664]{2,1,0:T(8,128)(2,1)S(1)}, u32[]{:S(2)}, u32[]{:S(2)}) collective-permute-start(bf16[2,48,1664]{2,1,0:T(8,128)(2,1)S(1)} %pad_maximum_fusion.1.l0), channel_id=1, source_target_pairs={{0,12},{1,13},{2,14},{3,15},{4,0},{5,1},{6,2},{7,3},{8,4},{9,5},{1... | collective-permute-start | bytes 958472 | tf_op jit(solution)/shard_map/ppermute | solution.py:35
  34.3 21.5 %copy-start.5 = (bf16[2,48,1664]{2,1,0:T(8,128)(2,1)}, bf16[2,48,1664]{2,1,0:T(8,128)(2,1)S(1)}, u32[]{:S(2)}) copy-start(bf16[2,48,1664]{2,1,0:T(8,128)(2,1)S(1)} %collective-permute-done.7.l7) | copy-start | bytes 958468
  34.3 12.8 %collective-permute-start.8 = (bf16[2,48,1664]{2,1,0:T(8,128)(2,1)S(1)}, bf16[2,48,1664]{2,1,0:T(8,128)(2,1)S(1)}, u32[]{:S(2)}, u32[]{:S(2)}) collective-permute-start(bf16[2,48,1664]{2,1,0:T(8,128)(2,1)S(1)} %collective-permute-done.7.l7), channel_id=1, source_target_pairs={{0,4},{1,5},{2,6},{3,7},{4,8},{5,9},{6,10},{7,11},{8,12},{9,13},{1... | collective-permute-start | bytes 958472 | tf_op jit(solution)/shard_map/ppermute | solution.py:35
  34.5 21.3 %copy-start.14 = (bf16[2,16,768]{2,1,0:T(8,128)(2,1)}, bf16[2,16,768]{2,1,0:T(8,128)(2,1)S(1)}, u32[]{:S(2)}) copy-start(bf16[2,16,768]{2,1,0:T(8,128)(2,1)S(1)} %collective-permute-done.theirs_ref) | copy-start | bytes 147460
  34.5 9.3 %collective-permute-start.11 = (bf16[48,3200]{1,0:T(8,128)(2,1)S(1)}, bf16[48,3200]{1,0:T(8,128)(2,1)S(1)}, u32[]{:S(2)}, u32[]{:S(2)}) collective-permute-start(bf16[48,3200]{1,0:T(8,128)(2,1)S(1)} %fusion.1.i0), channel_id=1, source_target_pairs={{0,1},{1,2},{2,3},{3,0},{4,5},{5,6},{6,7},{7,4},{8,9},{9,10},{10,1... | collective-permute-start | bytes 921608 | tf_op jit(solution)/shard_map/ppermute | solution.py:35
  35.9 9.9 %collective-permute-start.10 = (bf16[48,3200]{1,0:T(8,128)(2,1)}, bf16[48,3200]{1,0:T(8,128)(2,1)}, u32[]{:S(2)}, u32[]{:S(2)}) collective-permute-start(bf16[48,3200]{1,0:T(8,128)(2,1)} %collective-permute-done.9.i1), channel_id=1, source_target_pairs={{0,3},{1,0},{2,1},{3,2},{4,7},{5,4},{6,5},{7,6},{8,11},{9,8},{10,9... | collective-permute-start | bytes 921608 | tf_op jit(solution)/shard_map/ppermute | solution.py:35
  43.8 3.3 %collective-permute-start.18 = (bf16[2,48,1664]{2,1,0:T(8,128)(2,1)S(1)}, bf16[2,48,1664]{2,1,0:T(8,128)(2,1)S(1)}, u32[]{:S(2)}, u32[]{:S(2)}) collective-permute-start(bf16[2,48,1664]{2,1,0:T(8,128)(2,1)S(1)} %pad_maximum_fusion.l1), channel_id=1, source_target_pairs={{0,64},{1,65},{2,66},{3,67},{4,68},{5,69},{6,70},{7,71},{8,72},{9,... | collective-permute-start | bytes 958472 | tf_op jit(solution)/shard_map/ppermute | solution.py:35
  43.8 12.0 %copy-start.6 = (bf16[2,48,1664]{2,1,0:T(8,128)(2,1)}, bf16[2,48,1664]{2,1,0:T(8,128)(2,1)S(1)}, u32[]{:S(2)}) copy-start(bf16[2,48,1664]{2,1,0:T(8,128)(2,1)S(1)} %collective-permute-done.14.l3) | copy-start | bytes 958468
  43.8 4.1 %collective-permute-start.17 = (bf16[2,48,1664]{2,1,0:T(8,128)(2,1)S(1)}, bf16[2,48,1664]{2,1,0:T(8,128)(2,1)S(1)}, u32[]{:S(2)}, u32[]{:S(2)}) collective-permute-start(bf16[2,48,1664]{2,1,0:T(8,128)(2,1)S(1)} %pad_maximum_fusion.1.l0), channel_id=1, source_target_pairs={{0,64},{1,65},{2,66},{3,67},{4,68},{5,69},{6,70},{7,71},{8,72},{9,... | collective-permute-start | bytes 958472 | tf_op jit(solution)/shard_map/ppermute | solution.py:35
  44.3 11.5 %copy-start.7 = (bf16[2,48,1664]{2,1,0:T(8,128)(2,1)}, bf16[2,48,1664]{2,1,0:T(8,128)(2,1)S(1)}, u32[]{:S(2)}) copy-start(bf16[2,48,1664]{2,1,0:T(8,128)(2,1)S(1)} %collective-permute-done.13.l2) | copy-start | bytes 958468
  44.3 7.4 %collective-permute-start.16 = (bf16[2,48,1664]{2,1,0:T(8,128)(2,1)S(1)}, bf16[2,48,1664]{2,1,0:T(8,128)(2,1)}, u32[]{:S(2)}, u32[]{:S(2)}) collective-permute-start(bf16[2,48,1664]{2,1,0:T(8,128)(2,1)S(1)} %pad_maximum_fusion.1.l0), channel_id=1, source_target_pairs={{0,4},{1,5},{2,6},{3,7},{4,8},{5,9},{6,10},{7,11},{8,12},{9,13},{1... | collective-permute-start | bytes 958472 | tf_op jit(solution)/shard_map/ppermute | solution.py:35
  45.8 6.9 %collective-permute-start.20 = (bf16[2,48,1664]{2,1,0:T(8,128)(2,1)S(1)}, bf16[2,48,1664]{2,1,0:T(8,128)(2,1)S(1)}, u32[]{:S(2)}, u32[]{:S(2)}) collective-permute-start(bf16[2,48,1664]{2,1,0:T(8,128)(2,1)S(1)} %collective-permute-done.14.l3), channel_id=1, source_target_pairs={{0,64},{1,65},{2,66},{3,67},{4,68},{5,69},{6,70},{7,71},{8,72},{9,... | collective-permute-start | bytes 958472 | tf_op jit(solution)/shard_map/ppermute | solution.py:35
  47.1 8.8 %copy-start.8 = (bf16[2,48,1664]{2,1,0:T(8,128)(2,1)}, bf16[2,48,1664]{2,1,0:T(8,128)(2,1)S(1)}, u32[]{:S(2)}) copy-start(bf16[2,48,1664]{2,1,0:T(8,128)(2,1)S(1)} %collective-permute-done.8.l5) | copy-start | bytes 958468
  47.1 6.2 %collective-permute-start.15 = (bf16[2,48,1664]{2,1,0:T(8,128)(2,1)S(1)}, bf16[2,48,1664]{2,1,0:T(8,128)(2,1)}, u32[]{:S(2)}, u32[]{:S(2)}) collective-permute-start(bf16[2,48,1664]{2,1,0:T(8,128)(2,1)S(1)} %collective-permute-done.13.l2), channel_id=1, source_target_pairs={{0,12},{1,13},{2,14},{3,15},{4,0},{5,1},{6,2},{7,3},{8,4},{9,5},{1... | collective-permute-start | bytes 958472 | tf_op jit(solution)/shard_map/ppermute | solution.py:35
  47.1 8.8 %copy-start.9 = (bf16[2,48,1664]{2,1,0:T(8,128)(2,1)}, bf16[2,48,1664]{2,1,0:T(8,128)(2,1)S(1)}, u32[]{:S(2)}) copy-start(bf16[2,48,1664]{2,1,0:T(8,128)(2,1)S(1)} %collective-permute-done.18.o1) | copy-start | bytes 958468
  47.1 7.7 %collective-permute-start.24 = (bf16[2,48,1664]{2,1,0:T(8,128)(2,1)S(1)}, bf16[2,48,1664]{2,1,0:T(8,128)(2,1)}, u32[]{:S(2)}, u32[]{:S(2)}) collective-permute-start(bf16[2,48,1664]{2,1,0:T(8,128)(2,1)S(1)} %collective-permute-done.7.l7), channel_id=1, source_target_pairs={{0,64},{1,65},{2,66},{3,67},{4,68},{5,69},{6,70},{7,71},{8,72},{9,... | collective-permute-start | bytes 958472 | tf_op jit(solution)/shard_map/ppermute | solution.py:35
  47.9 8.0 %copy-start.10 = (bf16[2,48,1664]{2,1,0:T(8,128)(2,1)}, bf16[2,48,1664]{2,1,0:T(8,128)(2,1)S(1)}, u32[]{:S(2)}) copy-start(bf16[2,48,1664]{2,1,0:T(8,128)(2,1)S(1)} %collective-permute-done.17.o0) | copy-start | bytes 958468
  47.9 6.9 %collective-permute-start.19 = (bf16[2,48,1664]{2,1,0:T(8,128)(2,1)S(1)}, bf16[2,48,1664]{2,1,0:T(8,128)(2,1)}, u32[]{:S(2)}, u32[]{:S(2)}) collective-permute-start(bf16[2,48,1664]{2,1,0:T(8,128)(2,1)S(1)} %collective-permute-done.13.l2), channel_id=1, source_target_pairs={{0,64},{1,65},{2,66},{3,67},{4,68},{5,69},{6,70},{7,71},{8,72},{9,... | collective-permute-start | bytes 958472 | tf_op jit(solution)/shard_map/ppermute | solution.py:35
  51.8 3.0 %collective-permute-start.23 = (bf16[2,48,1664]{2,1,0:T(8,128)(2,1)}, bf16[2,48,1664]{2,1,0:T(8,128)(2,1)}, u32[]{:S(2)}, u32[]{:S(2)}) collective-permute-start(bf16[2,48,1664]{2,1,0:T(8,128)(2,1)} %collective-permute-done.16.l6), channel_id=1, source_target_pairs={{0,64},{1,65},{2,66},{3,67},{4,68},{5,69},{6,70},{7,71},{8,72},{9,... | collective-permute-start | bytes 958472 | tf_op jit(solution)/shard_map/ppermute | solution.py:35
  52.8 2.1 %collective-permute-start.22 = (bf16[2,48,1664]{2,1,0:T(8,128)(2,1)S(1)}, bf16[2,48,1664]{2,1,0:T(8,128)(2,1)}, u32[]{:S(2)}, u32[]{:S(2)}) collective-permute-start(bf16[2,48,1664]{2,1,0:T(8,128)(2,1)S(1)} %collective-permute-done.8.l5), channel_id=1, source_target_pairs={{0,64},{1,65},{2,66},{3,67},{4,68},{5,69},{6,70},{7,71},{8,72},{9,... | collective-permute-start | bytes 958472 | tf_op jit(solution)/shard_map/ppermute | solution.py:35
  53.5 2.4 %collective-permute-start.21 = (bf16[2,48,1664]{2,1,0:T(8,128)(2,1)}, bf16[2,48,1664]{2,1,0:T(8,128)(2,1)}, u32[]{:S(2)}, u32[]{:S(2)}) collective-permute-start(bf16[2,48,1664]{2,1,0:T(8,128)(2,1)} %collective-permute-done.15.l4), channel_id=1, source_target_pairs={{0,64},{1,65},{2,66},{3,67},{4,68},{5,69},{6,70},{7,71},{8,72},{9,... | collective-permute-start | bytes 958472 | tf_op jit(solution)/shard_map/ppermute | solution.py:35
  79.9 16.4 %all-to-all-start = ((bf16[32,4,896]{2,1,0:T(4,128)(2,1)}), bf16[32,4,896]{2,1,0:T(4,128)(2,1)S(1)}, u32[]{:S(2)}, u32[]{:S(2)}) async-start(bf16[32,4,896]{2,1,0:T(4,128)(2,1)} %get-tuple-element.22), calls=%async_computation | async-start | bytes 458752 | tf_op jit(solution)/shard_map/all_to_all | solution.py:611
  95.8 6.2 %collective-permute-start.27 = (f32[4,768]{1,0:T(4,128)}, f32[4,768]{1,0:T(4,128)S(1)}, u32[]{:S(2)}, u32[]{:S(2)}) collective-permute-start(f32[4,768]{1,0:T(4,128)} %get-tuple-element.25), channel_id=1, source_target_pairs={{0,64},{1,65},{2,66},{3,67},{4,68},{5,69},{6,70},{7,71},{8,72},{9,... | collective-permute-start | bytes 36872 | tf_op jit(solution)/shard_map/ppermute | solution.py:35
  96.6 19.9 %collective-permute-start.25 = (f32[1,768]{1,0:T(1,128)S(1)}, f32[1,768]{1,0:T(1,128)S(1)}, u32[]{:S(2)}, u32[]{:S(2)}) collective-permute-start(f32[1,768]{1,0:T(1,128)S(1)} %get-tuple-element.42), channel_id=1, source_target_pairs={{0,0},{1,1},{2,64},{3,65},{4,4},{5,5},{6,68},{7,69},{8,8},{9,9},{1... | collective-permute-start | bytes 9224 | tf_op jit(solution)/shard_map/ppermute | solution.py:35
  100.4 16.1 %collective-permute-start.26 = (f32[1,768]{1,0:T(1,128)S(1)}, f32[1,768]{1,0:T(1,128)S(1)}, u32[]{:S(2)}, u32[]{:S(2)}) collective-permute-start(f32[1,768]{1,0:T(1,128)S(1)} %get-tuple-element.43), channel_id=1, source_target_pairs={{0,1},{1,0},{2,65},{3,64},{4,5},{5,4},{6,69},{7,68},{8,9},{9,8},{1... | collective-permute-start | bytes 9224 | tf_op jit(solution)/shard_map/ppermute | solution.py:35
  114.0 3.0 %collective-permute-start.30 = (bf16[6,3072]{1,0:T(8,128)(2,1)S(1)}, bf16[6,3072]{1,0:T(8,128)(2,1)S(1)}, u32[]{:S(2)}, u32[]{:S(2)}) collective-permute-start(bf16[6,3072]{1,0:T(8,128)(2,1)S(1)} %get-tuple-element.39), channel_id=1, source_target_pairs={{0,3},{1,0},{2,1},{3,2},{4,7},{5,4},{6,5},{7,6},{8,11},{9,8},{10,9... | collective-permute-start | bytes 110600 | tf_op jit(solution)/shard_map/ppermute | solution.py:35
  114.1 4.5 %collective-permute-start.29 = (bf16[6,3072]{1,0:T(8,128)(2,1)S(1)}, bf16[6,3072]{1,0:T(8,128)(2,1)S(1)}, u32[]{:S(2)}, u32[]{:S(2)}) collective-permute-start(bf16[6,3072]{1,0:T(8,128)(2,1)S(1)} %get-tuple-element.40), channel_id=1, source_target_pairs={{0,2},{1,3},{2,0},{3,1},{4,6},{5,7},{6,4},{7,5},{8,10},{9,11},{10,... | collective-permute-start | bytes 110600 | tf_op jit(solution)/shard_map/ppermute | solution.py:35
  116.5 4.7 %collective-permute-start.28 = (bf16[6,3072]{1,0:T(8,128)(2,1)S(1)}, bf16[6,3072]{1,0:T(8,128)(2,1)S(1)}, u32[]{:S(2)}, u32[]{:S(2)}) collective-permute-start(bf16[6,3072]{1,0:T(8,128)(2,1)S(1)} %get-tuple-element.41), channel_id=1, source_target_pairs={{0,1},{1,2},{2,3},{3,0},{4,5},{5,6},{6,7},{7,4},{8,9},{9,10},{10,1... | collective-permute-start | bytes 110600 | tf_op jit(solution)/shard_map/ppermute | solution.py:35
  121.2 2.3 %collective-permute-start.31 = (f32[5,3072]{1,0:T(8,128)S(1)}, f32[5,3072]{1,0:T(8,128)S(1)}, u32[]{:S(2)}, u32[]{:S(2)}) collective-permute-start(f32[5,3072]{1,0:T(8,128)S(1)} %convert_add_fusion), channel_id=1, source_target_pairs={{0,64},{1,65},{2,66},{3,67},{4,68},{5,69},{6,70},{7,71},{8,72},{9,... | collective-permute-start | bytes 184328 | tf_op jit(solution)/shard_map/ppermute | solution.py:35
  (2 other events, 1.7 us)

commit v3 on v2

--- a/solution.py
+++ b/solution.py
@@ -43,6 +43,27 @@
     return permute(a, lambda c, y, z, x: (c, y, z, x - k))
 
 
+def other_x(a):
+    return permute(a, lambda c, y, z, x: (c, y, z, x ^ 1))
+
+
+def across_x(a):
+    return permute(a, lambda c, y, z, x: (c, y, z, 3 - x))
+
+
+def other_second(a):
+    return permute(a, lambda c, y, z, x: (c, y, z ^ 1, x) if c == 0 else (c, y ^ 1, z, x))
+
+
+def across_second(a):
+    return permute(a, lambda c, y, z, x: (c, y, 3 - z, x) if c == 0 else (c, 3 - y, z, x))
+
+
+def ring_order(at):
+    other = at + 1 - 2 * (at % 2)
+    return (at, other, 3 - at, 3 - other)
+
+
 def from_first(a, k):
     return permute(a, lambda c, y, z, x: (c, y - k, z, x) if c == 0 else (c, y, z - k, x))
 
@@ -164,8 +185,7 @@
 
 
 def real_kernel(
-    where_ref, mine_ref, theirs_ref, i0, i1, i2, i3,
-    l0, l1, l2, l3, l4, l5, l6, l7, o0, o1, o2, o3, o4, o5, o6, o7,
+    where_ref, mine_ref, theirs_ref, images_ref, l0, l1, l2, l3, o0, o1, o2, o3,
     csum_ref, w_out, wp_out,
     e_ref, n_ref, qkv_ref, att_ref, feat_ref, hot_ref, x_ref, posx_ref, w_ref, wp_ref, sems,
 ):
@@ -173,32 +193,36 @@
     groups = REAL // STEP
     core, y, z = where_ref[0], where_ref[1], where_ref[2]
 
-    for k, ref in enumerate((i0, i1, i2, i3)):
-        pltpu.make_async_copy(ref.at[0:32], x_ref.at[32 * k : 32 * k + 32], sems.at[1]).start()
-    mine = (l0, l1, l2, l3, l4, l5, l6, l7)
-    theirs = (o0, o1, o2, o3, o4, o5, o6, o7)
-    for other, refs in enumerate((mine, theirs)):
-        part = lax.rem(core + other, 2)
-        for j in range(4):
-            for i in range(4):
-                dy = jnp.where(part == 0, i, j)
-                dz = jnp.where(part == 0, j, i)
-                block = lax.rem(y + dy, 4) * 4 + lax.rem(z + dz, 4)
-                row = pl.multiple_of(block * BLOCK_ROWS, 16)
-                pltpu.make_async_copy(
-                    refs[2 * j + i // 2].at[i % 2],
-                    w_ref.at[pl.ds(row, BLOCK_ROWS), pl.ds(pl.multiple_of(part * COLS, 128), COLS)],
-                    sems.at[0],
-                ).start()
+    for k in range(4):
+        pltpu.make_async_copy(
+            images_ref.at[k, 0:32], x_ref.at[32 * k : 32 * k + 32], sems.at[1]
+        ).start()
+    near_block = ((0, 0), (0, 1), (1, 0), (1, 1))
+    far_block = ((2, 0), (3, 0), (2, 1), (3, 1))
+    for cols, sem in ((pl.ds(2 * D, 128), 0), (pl.ds(0, 2 * D), 4)):
+        for other, refs in enumerate(((l0, l1, l2, l3), (o0, o1, o2, o3))):
+            part = lax.rem(core + other, 2)
+            first, second = jnp.where(part == 0, y, z), jnp.where(part == 0, z, y)
+            target = pl.ds(pl.multiple_of(part * COLS + cols.start, 128), cols.size)
+            for j, at in enumerate(ring_order(second)):
+                for i in range(4):
+                    line = lax.rem(first + i, 4)
+                    block = jnp.where(part == 0, line * 4 + at, at * 4 + line)
+                    row = pl.multiple_of(block * BLOCK_ROWS, 16)
+                    ref, index = (near_block if i < 2 else far_block)[j]
+                    pltpu.make_async_copy(
+                        refs[ref].at[index, i % 2, :, cols],
+                        w_ref.at[pl.ds(row, BLOCK_ROWS), target],
+                        sems.at[sem],
+                    ).start()
     wp_ref[...] = jnp.zeros_like(wp_ref)
     spread_position(where_ref, mine_ref, theirs_ref, posx_ref)
     cls = lax.broadcasted_iota(jnp.int32, (REAL, 128), 1).astype(F32)
     pltpu.make_async_copy(x_ref, x_ref, sems.at[1]).wait()
     hot_ref[...] = jnp.where(x_ref[:, PIXELS:].astype(F32) == cls, 1.0, 0.0).astype(BF)
     feat_ref[:, D:] = jnp.ones((REAL, 128), BF)
-    pltpu.make_async_copy(w_ref, w_ref, sems.at[0]).wait()
-    save_w = pltpu.make_async_copy(w_ref, w_out, sems.at[2])
-    save_w.start()
+    patch_cols = w_ref.at[:, : 2 * 128]
+    pltpu.make_async_copy(patch_cols, patch_cols, sems.at[0]).wait()
     out_row = lax.broadcasted_iota(jnp.int32, (192, D), 0)
     in_row = lax.broadcasted_iota(jnp.int32, (192, D), 1)
 
@@ -213,6 +237,20 @@
     loop(3, decode, 3)
     save_wp = pltpu.make_async_copy(wp_ref, wp_out, sems.at[3])
     save_wp.start()
+
+    def embed(g):
+        at = mult(g * STEP, STEP)
+        x32 = x_ref[pl.ds(at, STEP), :PIXELS].astype(F32)
+        for t, e in enumerate(embed_rows(x32, wp_ref, tiles)):
+            e = e + posx_ref[...]
+            e_ref[g, 128 * t : 128 * t + 128] = e
+            n_ref[g, 128 * t : 128 * t + 128] = normalise(e)[0].astype(BF)
+
+    loop(groups, embed)
+    main_cols = w_ref.at[:, : 4 * D]
+    pltpu.make_async_copy(main_cols, main_cols, sems.at[4]).wait()
+    save_w = pltpu.make_async_copy(w_ref, w_out, sems.at[2])
+    save_w.start()
     low = low_half()
     bias = image_bias()
     ones = by_head(jnp.ones((128, 128), BF), low)
@@ -235,15 +273,10 @@
 
     def group(g):
         at = mult(g * STEP, STEP)
-        x32 = x_ref[pl.ds(at, STEP), :PIXELS].astype(F32)
-        for t, e in enumerate(embed_rows(x32, wp_ref, tiles)):
-            e = e + posx_ref[...]
-            e_ref[128 * t : 128 * t + 128] = e
-            n_ref[128 * t : 128 * t + 128] = normalise(e)[0].astype(BF)
-        qkv_product(n_ref, w_ref, qkv_ref, QKV_UNROLL)
+        qkv_product(n_ref.at[g], w_ref, qkv_ref, QKV_UNROLL)
         pipeline(6 * tiles, score, soften, weigh)
-        out_product(att_ref, w_ref, e_ref)
-        feats = [patch_sum(normalise(e_ref[128 * t : 128 * t + 128])[0]) for t in range(tiles)]
+        out_product(att_ref, w_ref, e_ref.at[g])
+        feats = [patch_sum(normalise(e_ref[g, 128 * t : 128 * t + 128])[0]) for t in range(tiles)]
         feat_ref[pl.ds(at, STEP), :D] = jnp.concatenate(feats, axis=0).astype(BF)
 
     loop(groups, group)
@@ -264,15 +297,15 @@
 
 
 def synth_kernel(
-    where_ref, mine_ref, theirs_ref, i0, i1, i2, i3, w_in, wp_in,
+    where_ref, mine_ref, theirs_ref, images_ref, w_in, wp_in,
     sum_ref, n_out, r1_out, qkv_out, p_out, xhat2_out, r2_out,
     n_ref, r1_ref, qkv_ref, p_ref, xhat2_ref, r2_ref,
     e_ref, att_ref, x_ref, posx_ref, w_ref, wp_ref, in_sems, sems,
 ):
     tiles = SYN // 8
     pairs = [
-        (ref.at[32:48, :PIXELS], x_ref.at[16 * k : 16 * k + 16])
-        for k, ref in enumerate((i0, i1, i2, i3))
+        (images_ref.at[k, 32:48, :PIXELS], x_ref.at[16 * k : 16 * k + 16])
+        for k in range(4)
     ]
     loads = copies_of(pairs + [(wp_in, wp_ref), (w_in, w_ref)], in_sems)
     saves = [
@@ -344,10 +377,10 @@
 
 
 def back_kernel(
-    g_ref, w_in, wp_in, n_in, r1_in, qkv_in, p_in, xhat2_in, r2_in,
-    out_ref,
+    where_ref, means_ref, own_ref, their_ref, w_in, wp_in, n_in, r1_in, qkv_in, p_in, xhat2_in, r2_in,
+    out0, out1, out2, out3,
     w_ref, wp_ref, n_ref, r1_ref, qkv_ref, p_ref, xhat2_ref, r2_ref,
-    dh_ref, dhb_ref, da_ref, dqkv_ref, dn_ref, spread_ref, px_ref, sems,
+    dh_ref, dhb_ref, da_ref, dqkv_ref, dn_ref, spread_ref, px_ref, grad_ref, sems,
 ):
     tiles = SYN // 8
     out_cols = pl.ds(OUT_AT, D)
@@ -365,7 +398,9 @@
     spread = jnp.zeros((SYN, D), F32)
     for s in range(4):
         mine = (image >= SLOT * s) & (image < SLOT * s + 5)
-        spread = jnp.where(mine, g_ref[s : s + 1], spread)
+        syn = (own_ref[s : s + 1] + their_ref[s : s + 1]) * (1.0 / IPC)
+        g = (syn - means_ref[s : s + 1]) * (2.0 / (IPC * TOKENS))
+        spread = jnp.where(mine, g, spread)
     spread_ref[...] = spread
     loads[0].wait()
     loads[1].wait()
@@ -443,9 +478,12 @@
 
     loop(tiles, first_norm, tiles)
     for j in range(8):
-        out_ref[:, 384 * j : 384 * j + 384] = jnp.concatenate(
-            [px_ref[t, 8 * j : 8 * j + 8] for t in range(tiles)], axis=0
-        ).astype(BF)
+        cols = slice(384 * j, 384 * j + 384)
+        all_rows = jnp.concatenate([px_ref[t, 8 * j : 8 * j + 8] for t in range(tiles)], axis=0)
+        for s in range(4):
+            grad_ref[8 * s : 8 * s + SLOT, cols] = all_rows[SLOT * s : SLOT * s + SLOT]
+    for at, out in zip(ring_order(where_ref[3]), (out0, out1, out2, out3)):
+        out[...] = grad_ref[pl.ds(mult(8 * at, 8), 8)][:5].astype(BF)
 
 
 SMEM_SPEC = pl.BlockSpec(memory_space=pltpu.SMEM)
@@ -461,7 +499,7 @@
     rows = STEP * TOKENS
     return pl.pallas_call(
         real_kernel,
-        in_specs=[SMEM_SPEC, VMEM_SPEC, VMEM_SPEC] + [ANY_SPEC] * 20,
+        in_specs=[SMEM_SPEC, VMEM_SPEC, VMEM_SPEC] + [ANY_SPEC] * 9,
         out_specs=[pl.BlockSpec((32, 4, D + 128), lambda: (0, 0, 0)), ANY_SPEC, ANY_SPEC],
         out_shape=[
             jax.ShapeDtypeStruct((32, 4, D + 128), BF),
@@ -469,8 +507,8 @@
             jax.ShapeDtypeStruct((2, 256, D), BF),
         ],
         scratch_shapes=[
-            buffer((rows, D), F32),
-            buffer((rows, D), BF),
+            buffer((REAL // STEP, rows, D), F32),
+            buffer((REAL // STEP, rows, D), BF),
             buffer((rows, 3 * D), BF),
             buffer((rows, D), BF),
             buffer((REAL, D + 128), BF),
@@ -479,14 +517,14 @@
             buffer((128, D), F32),
             buffer((D, 2 * COLS), BF),
             buffer((2, 256, D), BF),
-            pltpu.SemaphoreType.DMA((4,)),
+            pltpu.SemaphoreType.DMA((5,)),
         ],
         compiler_params=pltpu.CompilerParams(vmem_limit_bytes=VMEM_LIMIT),
         cost_estimate=pl.CostEstimate(
             flops=14_000_000_000, bytes_accessed=12_000_000, transcendentals=3_000_000
         ),
         name="real_forward",
-    )(place, mine_pos, their_pos, *images, *mine, *theirs)
+    )(place, mine_pos, their_pos, images, *mine, *theirs)
 
 
 SYN_ROWS = SYN * TOKENS
@@ -504,7 +542,7 @@
 def run_synth(place, mine_pos, their_pos, images, w, wp):
     return pl.pallas_call(
         synth_kernel,
-        in_specs=[SMEM_SPEC, VMEM_SPEC, VMEM_SPEC] + [ANY_SPEC] * 6,
+        in_specs=[SMEM_SPEC, VMEM_SPEC, VMEM_SPEC] + [ANY_SPEC] * 3,
         out_specs=[pl.BlockSpec((4, D), lambda: (0, 0))] + [ANY_SPEC] * 6,
         out_shape=[jax.ShapeDtypeStruct((4, D), F32)]
         + [jax.ShapeDtypeStruct(s, t) for s, t in SAVED],
@@ -522,15 +560,15 @@
             flops=3_000_000_000, bytes_accessed=12_000_000, transcendentals=600_000
         ),
         name="synth_forward",
-    )(place, mine_pos, their_pos, *images, w, wp)
-
-
-def run_back(g, w, wp, saved):
+    )(place, mine_pos, their_pos, images, w, wp)
+
+
+def run_back(place, means, own, their, w, wp, saved):
     return pl.pallas_call(
         back_kernel,
-        in_specs=[VMEM_SPEC] + [ANY_SPEC] * 8,
-        out_specs=pl.BlockSpec((SYN, PIXELS), lambda: (0, 0)),
-        out_shape=jax.ShapeDtypeStruct((SYN, PIXELS), BF),
+        in_specs=[SMEM_SPEC] + [VMEM_SPEC] * 3 + [ANY_SPEC] * 8,
+        out_specs=[pl.BlockSpec((5, PIXELS), lambda: (0, 0))] * 4,
+        out_shape=[jax.ShapeDtypeStruct((5, PIXELS), BF)] * 4,
         scratch_shapes=[buffer(s, t) for s, t in WEIGHTS + SAVED]
         + [
             buffer((SYN_ROWS, D), F32),
@@ -540,6 +578,7 @@
             buffer((SYN_ROWS, D), F32),
             buffer((SYN, D), F32),
             buffer((SYN // 8, 64, 384), F32),
+            buffer((32, PIXELS), F32),
             pltpu.SemaphoreType.DMA((9,)),
         ],
         compiler_params=pltpu.CompilerParams(vmem_limit_bytes=VMEM_LIMIT),
@@ -547,7 +586,7 @@
             flops=4_000_000_000, bytes_accessed=12_000_000, transcendentals=0
         ),
         name="synth_backward",
-    )(g, w, wp, *saved)
+    )(place, means, own, their, w, wp, *saved)
 
 
 def gather_weights(core, x, patch_weight, qkv_weight, out_weight, images):
@@ -572,13 +611,13 @@
         jnp.stack([ring, from_first(ring, 1)]),
         jnp.stack([from_first(ring, 2), from_first(ring, 3)]),
     )
-    next_near, last_far = from_second(near, 1), from_second(far, 3)
-    next_far, last_near = from_second(far, 1), from_second(near, 3)
-    over_near, over_far = from_second(next_near, 1), from_second(last_far, 3)
-    over_far, *images = lax.optimization_barrier((over_far, *images))
-    mine = [near, far, next_near, next_far, over_near, over_far, last_near, last_far]
+    near = jnp.stack([near, other_second(near)])
+    far = jnp.stack([far, across_second(far)])
+    near_across, far_other = across_second(near), other_second(far)
+    near_across, images, their_pos = lax.optimization_barrier((near_across, *images))
+    mine = [near, near_across, far, far_other]
     theirs = [swap_cores(a) for a in mine]
-    return mine, theirs, images
+    return mine, theirs, images, their_pos
 
 
 def local(
@@ -598,11 +637,12 @@
         [lax.dynamic_slice_in_dim(tagged, 32 * core, 32, 0), jnp.pad(syn, ((0, 11), (0, 128)))],
         axis=0,
     )
-    after = from_x(images, 1)
-    images = [images, after, from_x(after, 1), from_x(images, 3)]
-    their_pos = swap_cores(position)
-
-    mine, theirs, images = gather_weights(
+    rings = [[flat(c, yz // 4, yz % 4, xx) for xx in range(4)] for c in range(2) for yz in range(16)]
+    images = lax.all_to_all(
+        jnp.broadcast_to(images[None], (4, 48, PIXELS + 128)), AXES, 0, 0, axis_index_groups=rings
+    )
+    images = (images, swap_cores(position))
+    mine, theirs, images, their_pos = gather_weights(
         core, x, patch_weight, qkv_weight, out_weight, images
     )
     csum, w, wp = run_real(place, position, their_pos, images, mine, theirs)
@@ -613,10 +653,9 @@
     means = total[:, :D] / jnp.maximum(total[:, D : D + 1], 1.0)
 
     own, *saved = run_synth(place, position, their_pos, images, w, wp)
-    syn_mean = (own + swap_cores(own)) * (1.0 / IPC)
-    g = (syn_mean - jnp.roll(means, -x, axis=0)) * (2.0 / (IPC * TOKENS))
-    grads = run_back(g, w, wp, saved)
-
+    grads = run_back(place, means, own, swap_cores(own), w, wp, saved)
+
+    means, grads = lax.optimization_barrier((means, grads))
     sent = []
     for m in range(2):
         row = lax.dynamic_index_in_dim(means, (x - m) % 2 + 2 * core, 0, keepdims=True)
@@ -627,11 +666,8 @@
     second = jnp.where(x % 2 == 0, sent[1], sent[0])
     real_means = jnp.stack([first, second])
 
-    grads = grads.reshape(4, SLOT, PIXELS)
-    pixel = grads[0].astype(F32)
-    for k in (1, 2, 3):
-        pixel = pixel + from_x(grads[k], -k).astype(F32)
-    pixel = pixel[:5]
+    pixel = grads[0].astype(F32) + other_x(grads[1]).astype(F32)
+    pixel = pixel + across_x(grads[2]).astype(F32) + from_x(grads[3], 2).astype(F32)
     other = swap_cores(pixel)
     pixel_grad = jnp.concatenate(
         [jnp.where(core == 0, pixel, other), jnp.where(core == 0, other, pixel)], axis=0

time: 125 us -> 121 us (0.968)
  starting transfers between devices: 45 us -> 39.6 us
  other arithmetic: 5.07 us -> 7.04 us
  Pallas kernels: 42.7 us -> 41.4 us
    ppermute x32 -> x23, waiting for transfers between devices: 27.7 us -> 14.2 us  [permute(): lax.ppermute(a, AXES, [(flat(*p), flat(*target(*p))) for p in PLACES])]
    all_to_all x0 -> x1, waiting for transfers between devices: none -> 12.8 us  [local(): lax.all_to_all(jnp.broadcast_to(images[None], (4, 48, PIXELS + 128)), AXE...]
    ppermute x32 -> x23, starting transfers between devices: 38.2 us -> 31.1 us  [permute(): lax.ppermute(a, AXES, [(flat(*p), flat(*target(*p))) for p in PLACES])]
    all_to_all x0 -> x1, starting transfers between devices: none -> 3.53 us  [local(): lax.all_to_all(jnp.broadcast_to(images[None], (4, 48, PIXELS + 128)), AXE...]
    another operation x2 -> x4, other arithmetic: 0.07 us -> 1.93 us  [the longest x2 1.09 us: gather_weights(): near = jnp.stack([near, other_second(near)])]
    all_to_all x1, starting transfers between devices: 6.74 us -> 4.99 us  [local(): got = lax.all_to_all(csum, AXES, 0, 0, axis_index_groups=groups)]
    pallas_call x1, Pallas kernels: 24 us -> 22.6 us  [run_real(): pl.pallas_call(real_kernel, in_specs=[SMEM_SPEC, VMEM_SPEC, VMEM_SPEC] +...]
    mul x1 -> x0, other arithmetic: 1.33 us -> none  [local(): g = (syn_mean - jnp.roll(means, -x, axis=0)) * (2.0 / (IPC * TOKENS))]
  transfers between devices with their start and end apart: 33 -> 25, of which waited for: 14 -> 13; matrix products, arithmetic and copies ran while one was open for 3% -> 5% of each run, Pallas kernels for 15% -> 8%
where the time goes in v3:
time: 121 us; the launch traced here: 120 us
  Pallas kernels  41.4 us (34%)
  starting transfers between devices  39.6 us (33%)
  waiting for transfers between devices  27 us (22%)
  other arithmetic  7.04 us (6%)
  local copies, waits for them, and re-layouts  3.7 us (3%)
  between operations  1.27 us (1%)
    ppermute x23, starting transfers between devices, permute(): lax.ppermute(a, AXES, [(flat(*p), flat(*target(*p))) for p in PLACES])  31.1 us
    pallas_call x1, Pallas kernels, run_real(): pl.pallas_call(real_kernel, in_specs=[SMEM_SPEC, VMEM_SPEC, VMEM_SPEC] +...  22.6 us
    ppermute x23, waiting for transfers between devices, permute(): lax.ppermute(a, AXES, [(flat(*p), flat(*target(*p))) for p in PLACES])  14.2 us
    all_to_all x1, waiting for transfers between devices, local(): lax.all_to_all(jnp.broadcast_to(images[None], (4, 48, PIXELS + 128)), AXE...  12.8 us
    pallas_call x1, Pallas kernels, run_back(): pl.pallas_call(back_kernel, in_specs=[SMEM_SPEC] + [VMEM_SPEC] * 3 + [ANY...  9.77 us
    pallas_call x1, Pallas kernels, run_synth(): pl.pallas_call(synth_kernel, in_specs=[SMEM_SPEC, VMEM_SPEC, VMEM_SPEC] +...  9.09 us
    all_to_all x1, starting transfers between devices, local(): got = lax.all_to_all(csum, AXES, 0, 0, axis_index_groups=groups)  4.99 us
    all_to_all x1, starting transfers between devices, local(): lax.all_to_all(jnp.broadcast_to(images[None], (4, 48, PIXELS + 128)), AXE...  3.53 us
  transfers between devices with their start and end apart: 25, of which 13 were waited for; matrix products, arithmetic and copies ran while one was open for 5% of the time, Pallas kernels for 8%

profile of v3, /device:TPU:1, one launch (start us, length us, event | category | flops | bytes accessed | tf_op | source)
XLA Modules:
  0.0 120.1 jit_solution(9090285863386177015)
XLA Ops:
  0.9 0.7 reshape.24
  1.7 1.1 pad_maximum_fusion.5
  2.8 0.1 maximum_bitcast_fusion
  3.1 3.4 %collective-permute-start.3 = (bf16[12,1664]{1,0:T(8,128)(2,1)S(1)}, bf16[12,1664]{1,0:T(8,128)(2,1)S(1)}, u32[]{:S(2)}, u32[]{:S(2)}) collective-permute-start(bf16[12,1664]{1,0:T(8,128)(2,1)S(1)} %get-tuple-element.50), channel_id=1, source_target_pairs={{0,1},{1,64},{2,65},{3,0},{4,5},{5,68},{6,69},{7,4},{8,9},{9,72},{... | collective-permute-start | bytes 119816 | tf_op jit(solution)/shard_map/ppermute | solution.py:35
  6.4 2.7 %collective-permute-start.2 = (bf16[12,1664]{1,0:T(8,128)(2,1)S(1)}, bf16[12,1664]{1,0:T(8,128)(2,1)S(1)}, u32[]{:S(2)}, u32[]{:S(2)}) collective-permute-start(bf16[12,1664]{1,0:T(8,128)(2,1)S(1)} %get-tuple-element.51), channel_id=1, source_target_pairs={{0,64},{1,65},{2,0},{3,1},{4,68},{5,69},{6,4},{7,5},{8,72},{9,73},... | collective-permute-start | bytes 119816 | tf_op jit(solution)/shard_map/ppermute | solution.py:35
  9.2 1.2 %collective-permute-start.1 = (bf16[12,1664]{1,0:T(8,128)(2,1)S(1)}, bf16[12,1664]{1,0:T(8,128)(2,1)S(1)}, u32[]{:S(2)}, u32[]{:S(2)}) collective-permute-start(bf16[12,1664]{1,0:T(8,128)(2,1)S(1)} %get-tuple-element.52), channel_id=1, source_target_pairs={{0,65},{1,0},{2,1},{3,64},{4,69},{5,4},{6,5},{7,68},{8,73},{9,8},{... | collective-permute-start | bytes 119816 | tf_op jit(solution)/shard_map/ppermute | solution.py:35
  10.4 1.9 %collective-permute-start = (bf16[12,1664]{1,0:T(8,128)(2,1)S(1)}, bf16[12,1664]{1,0:T(8,128)(2,1)S(1)}, u32[]{:S(2)}, u32[]{:S(2)}) collective-permute-start(bf16[12,1664]{1,0:T(8,128)(2,1)S(1)} %get-tuple-element.53), channel_id=1, source_target_pairs={{0,0},{1,1},{2,64},{3,65},{4,4},{5,5},{6,68},{7,69},{8,8},{9,9},{1... | collective-permute-start | bytes 119816 | tf_op jit(solution)/shard_map/ppermute | solution.py:35
  12.4 0.2 select_reduce_fusion
  12.7 4.7 %collective-permute-done = bf16[12,1664]{1,0:T(8,128)(2,1)S(1)} collective-permute-done((bf16[12,1664]{1,0:T(8,128)(2,1)S(1)}, bf16[12,1664]{1,0:T(8,128)(2,1)S(1)}, u32[]{:S(2)}, u32[]{:S(2)}) %collective-permute-start) | collective-permute-done | bytes 39968 | tf_op jit(solution)/shard_map/ppermute | solution.py:35
  17.6 1.7 %collective-permute-start.9 = (bf16[48,1664]{1,0:T(8,128)(2,1)S(1)}, bf16[48,1664]{1,0:T(8,128)(2,1)S(1)}, u32[]{:S(2)}, u32[]{:S(2)}) collective-permute-start(bf16[48,1664]{1,0:T(8,128)(2,1)S(1)} %reshape.27), channel_id=1, source_target_pairs={{0,16},{1,17},{2,18},{3,19},{4,20},{5,21},{6,22},{7,23},{8,24},{9,... | collective-permute-start | bytes 479240 | tf_op jit(solution)/shard_map/ppermute | solution.py:35
  19.3 3.3 %collective-permute-start.8 = (bf16[48,1664]{1,0:T(8,128)(2,1)S(1)}, bf16[48,1664]{1,0:T(8,128)(2,1)S(1)}, u32[]{:S(2)}, u32[]{:S(2)}) collective-permute-start(bf16[48,1664]{1,0:T(8,128)(2,1)S(1)} %reshape.27), channel_id=1, source_target_pairs={{0,32},{1,33},{2,34},{3,35},{4,36},{5,37},{6,38},{7,39},{8,40},{9,... | collective-permute-start | bytes 479240 | tf_op jit(solution)/shard_map/ppermute | solution.py:35
  22.7 0.8 collective-permute-start.4
  23.5 0.6 collective-permute-done.9
  24.1 2.9 %collective-permute-done.8 = bf16[48,1664]{1,0:T(8,128)(2,1)S(1)} collective-permute-done((bf16[48,1664]{1,0:T(8,128)(2,1)S(1)}, bf16[48,1664]{1,0:T(8,128)(2,1)S(1)}, u32[]{:S(2)}, u32[]{:S(2)}) %collective-permute-start.8) | collective-permute-done | bytes 159776 | tf_op jit(solution)/shard_map/ppermute | solution.py:35
  27.0 0.8 fusion.6
  27.7 2.8 %collective-permute-start.10 = (bf16[2,48,1664]{2,1,0:T(8,128)(2,1)}, bf16[2,48,1664]{2,1,0:T(8,128)(2,1)S(1)}, u32[]{:S(2)}, u32[]{:S(2)}) collective-permute-start(bf16[2,48,1664]{2,1,0:T(8,128)(2,1)} %get-tuple-element.47), channel_id=1, source_target_pairs={{0,12},{1,13},{2,14},{3,15},{4,8},{5,9},{6,10},{7,11},{8,4},{9,5},... | collective-permute-start | bytes 958472 | tf_op jit(solution)/shard_map/ppermute | solution.py:35
  30.7 1.1 broadcast_in_dim.30
  31.8 3.5 %all-to-all-start = ((bf16[4,48,3200]{2,1,0:T(8,128)(2,1)}), bf16[4,48,3200]{2,1,0:T(8,128)(2,1)S(1)}, u32[]{:S(2)}, u32[]{:S(2)}) async-start(bf16[4,48,3200]{2,1,0:T(8,128)(2,1)} %broadcast_in_dim.30), calls=%async_computation | async-start | bytes 2457600 | tf_op jit(solution)/shard_map/all_to_all | solution.py:641
  35.3 1.1 collective-permute-done.5
  36.5 0.7 copy-done.5
  37.2 1.0 pad_maximum_fusion.l0
  38.5 0.4 collective-permute-start.11
  38.9 0.5 collective-permute-start.12
  39.4 0.7 collective-permute-done.7.theirs_ref
  40.1 12.8 %all-to-all-done.images_ref = bf16[4,48,3200]{2,1,0:T(8,128)(2,1)S(1)} async-done(((bf16[4,48,3200]{2,1,0:T(8,128)(2,1)}), bf16[4,48,3200]{2,1,0:T(8,128)(2,1)S(1)}, u32[]{:S(2)}, u32[]{:S(2)}) %all-to-all-start) | async-done | bytes 1228832 | tf_op jit(solution)/shard_map/all_to_all | solution.py:641
  52.9 0.5 collective-permute-start.15
  53.4 0.3 collective-permute-start.13
  53.6 0.6 pad_add_fusion.where_ref
  54.3 0.9 collective-permute-done.15.o3
  55.2 1.1 collective-permute-done.13.o1
  56.3 22.6 %real_forward.1 = (bf16[32,4,896]{2,1,0:T(4,128)(2,1)}, bf16[768,3328]{1,0:T(8,128)(2,1)}, bf16[2,256,768]{2,1,0:T(8,128)(2,1)}) custom-call(s32[4]{0:T(128)} %pad_add_fusion.where_ref, bf16[2,16,768]{2,1,0:T(8,128)(2,1)} %mine_ref.3, bf16[2,16,768]{2,1,0:T(8,128)(2,1)} %copy-done.9, bf16[4,48,3200]{2,1,0:T(8,128)(2,1)} %copy-done.1, ...), custom_call_target="tpu_custom_call" | custom-call | flops 14000000000 | bytes 12000000 | tf_op jit(solution)/shard_map/real_forward/pallas_call | solution.py:500
  78.9 5.0 %all-to-all-start.1 = ((bf16[32,4,896]{2,1,0:T(4,128)(2,1)}), bf16[32,4,896]{2,1,0:T(4,128)(2,1)S(1)}, u32[]{:S(2)}, u32[]{:S(2)}) async-start(bf16[32,4,896]{2,1,0:T(4,128)(2,1)} %get-tuple-element.27), calls=%async_computation.1 | async-start | bytes 458752 | tf_op jit(solution)/shard_map/all_to_all | solution.py:651
  83.9 9.1 %synth_forward.1 = (f32[4,768]{1,0:T(4,128)}, bf16[384,768]{1,0:T(8,128)(2,1)}, f32[384,128]{1,0:T(8,128)}, bf16[384,2304]{1,0:T(8,128)(2,1)}, bf16[384,1536]{1,...) custom-call(s32[4]{0:T(128)} %pad_add_fusion.where_ref, bf16[2,16,768]{2,1,0:T(8,128)(2,1)} %mine_ref.3, ...), custom_call_target="tpu_custom_call" | custom-call | flops 3000000000 | bytes 12000000 | tf_op jit(solution)/shard_map/synth_forward/pallas_call | solution.py:543
  93.0 0.5 collective-permute-start.16
  93.8 0.7 slice_divide_fusion.means_ref
  94.6 0.6 copy-done.10
  95.2 9.8 %synth_backward.1 = (bf16[5,3072]{1,0:T(8,128)(2,1)}, bf16[5,3072]{1,0:T(8,128)(2,1)}, bf16[5,3072]{1,0:T(8,128)(2,1)}, bf16[5,3072]{1,0:T(8,128)(2,1)}) custom-call(s32[4]{0:T(128)} %pad_add_fusion.where_ref, f32[4,768]{1,0:T(4,128)} %slice_divide_fusion.means_ref, f32[4,768]{1,0:T(4,128)} %get-tuple-element.30.own_ref, f32[4,768]{1,0:T(4,128)} %copy-done.10, ...), custom_call_target="tpu_custom_call" | custom-call | flops 4000000000 | bytes 12000000 | tf_op jit(solution)/shard_map/synth_backward/pallas_call | solution.py:567
  105.0 2.4 %collective-permute-start.17 = (f32[1,768]{1,0:T(1,128)S(1)}, f32[1,768]{1,0:T(1,128)S(1)}, u32[]{:S(2)}, u32[]{:S(2)}) collective-permute-start(f32[1,768]{1,0:T(1,128)S(1)} %get-tuple-element.56), channel_id=1, source_target_pairs={{0,0},{1,1},{2,64},{3,65},{4,4},{5,5},{6,68},{7,69},{8,8},{9,9},{1... | collective-permute-start | bytes 9224 | tf_op jit(solution)/shard_map/ppermute | solution.py:35
  107.4 2.5 %collective-permute-start.18 = (f32[1,768]{1,0:T(1,128)S(1)}, f32[1,768]{1,0:T(1,128)S(1)}, u32[]{:S(2)}, u32[]{:S(2)}) collective-permute-start(f32[1,768]{1,0:T(1,128)S(1)} %get-tuple-element.57), channel_id=1, source_target_pairs={{0,1},{1,0},{2,65},{3,64},{4,5},{5,4},{6,69},{7,68},{8,9},{9,8},{1... | collective-permute-start | bytes 9224 | tf_op jit(solution)/shard_map/ppermute | solution.py:35
  110.0 3.2 %collective-permute-start.21 = (bf16[5,3072]{1,0:T(8,128)(2,1)}, bf16[5,3072]{1,0:T(8,128)(2,1)S(1)}, u32[]{:S(2)}, u32[]{:S(2)}) collective-permute-start(bf16[5,3072]{1,0:T(8,128)(2,1)} %get-tuple-element.45), channel_id=1, source_target_pairs={{0,2},{1,3},{2,0},{3,1},{4,6},{5,7},{6,4},{7,5},{8,10},{9,11},{10,... | collective-permute-start | bytes 92168 | tf_op jit(solution)/shard_map/ppermute | solution.py:35
  113.2 0.2 collective-permute-done.19
  113.4 0.9 collective-permute-done.20
  114.3 0.6 collective-permute-done.21
  114.9 0.8 convert_add_fusion
  115.7 2.7 %collective-permute-start.22 = (f32[5,3072]{1,0:T(8,128)S(1)}, f32[5,3072]{1,0:T(8,128)S(1)}, u32[]{:S(2)}, u32[]{:S(2)}) collective-permute-start(f32[5,3072]{1,0:T(8,128)S(1)} %convert_add_fusion), channel_id=1, source_target_pairs={{0,64},{1,65},{2,66},{3,67},{4,68},{5,69},{6,70},{7,71},{8,72},{9,... | collective-permute-start | bytes 184328 | tf_op jit(solution)/shard_map/ppermute | solution.py:35
  118.4 0.6 pad_maximum_fusion.6
  119.0 0.3 collective-permute-done.22
  119.4 0.7 pad_maximum_fusion.4
  (70 shorter events, 1.4 us)
Async XLA Ops:
  0.6 22.0 %copy-start = (f32[10,3072]{1,0:T(8,128)S(1)}, f32[10,3072]{1,0:T(8,128)}, u32[]{:S(2)}) copy-start(f32[10,3072]{1,0:T(8,128)} %param.11) | copy-start | bytes 368644
  0.6 11.7 %copy-start.11 = (s32[64]{0:T(128)S(1)}, s32[64]{0:T(128)}, u32[]{:S(2)}) copy-start(s32[64]{0:T(128)} %param.10) | copy-start | bytes 772
  0.7 11.7 %copy-start.12 = (s32[64]{0:T(128)S(1)}, s32[64]{0:T(128)}, u32[]{:S(2)}) copy-start(s32[64]{0:T(128)} %param.9) | copy-start | bytes 772
  0.7 11.9 %copy-start.4 = (bf16[64,3072]{1,0:T(8,128)(2,1)S(1)}, bf16[64,3072]{1,0:T(8,128)(2,1)}, u32[]{:S(2)}) copy-start(bf16[64,3072]{1,0:T(8,128)(2,1)} %param.8) | copy-start | bytes 1179652
  3.1 14.4 %collective-permute-start.3 = (bf16[12,1664]{1,0:T(8,128)(2,1)S(1)}, bf16[12,1664]{1,0:T(8,128)(2,1)S(1)}, u32[]{:S(2)}, u32[]{:S(2)}) collective-permute-start(bf16[12,1664]{1,0:T(8,128)(2,1)S(1)} %get-tuple-element.50), channel_id=1, source_target_pairs={{0,1},{1,64},{2,65},{3,0},{4,5},{5,68},{6,69},{7,4},{8,9},{9,72},{... | collective-permute-start | bytes 119816 | tf_op jit(solution)/shard_map/ppermute | solution.py:35
  6.4 10.9 %collective-permute-start.2 = (bf16[12,1664]{1,0:T(8,128)(2,1)S(1)}, bf16[12,1664]{1,0:T(8,128)(2,1)S(1)}, u32[]{:S(2)}, u32[]{:S(2)}) collective-permute-start(bf16[12,1664]{1,0:T(8,128)(2,1)S(1)} %get-tuple-element.51), channel_id=1, source_target_pairs={{0,64},{1,65},{2,0},{3,1},{4,68},{5,69},{6,4},{7,5},{8,72},{9,73},... | collective-permute-start | bytes 119816 | tf_op jit(solution)/shard_map/ppermute | solution.py:35
  9.2 8.2 %collective-permute-start.1 = (bf16[12,1664]{1,0:T(8,128)(2,1)S(1)}, bf16[12,1664]{1,0:T(8,128)(2,1)S(1)}, u32[]{:S(2)}, u32[]{:S(2)}) collective-permute-start(bf16[12,1664]{1,0:T(8,128)(2,1)S(1)} %get-tuple-element.52), channel_id=1, source_target_pairs={{0,65},{1,0},{2,1},{3,64},{4,69},{5,4},{6,5},{7,68},{8,73},{9,8},{... | collective-permute-start | bytes 119816 | tf_op jit(solution)/shard_map/ppermute | solution.py:35
  10.4 6.9 %collective-permute-start = (bf16[12,1664]{1,0:T(8,128)(2,1)S(1)}, bf16[12,1664]{1,0:T(8,128)(2,1)S(1)}, u32[]{:S(2)}, u32[]{:S(2)}) collective-permute-start(bf16[12,1664]{1,0:T(8,128)(2,1)S(1)} %get-tuple-element.53), channel_id=1, source_target_pairs={{0,0},{1,1},{2,64},{3,65},{4,4},{5,5},{6,68},{7,69},{8,8},{9,9},{1... | collective-permute-start | bytes 119816 | tf_op jit(solution)/shard_map/ppermute | solution.py:35
  17.6 6.5 %collective-permute-start.9 = (bf16[48,1664]{1,0:T(8,128)(2,1)S(1)}, bf16[48,1664]{1,0:T(8,128)(2,1)S(1)}, u32[]{:S(2)}, u32[]{:S(2)}) collective-permute-start(bf16[48,1664]{1,0:T(8,128)(2,1)S(1)} %reshape.27), channel_id=1, source_target_pairs={{0,16},{1,17},{2,18},{3,19},{4,20},{5,21},{6,22},{7,23},{8,24},{9,... | collective-permute-start | bytes 479240 | tf_op jit(solution)/shard_map/ppermute | solution.py:35
  19.3 7.7 %collective-permute-start.8 = (bf16[48,1664]{1,0:T(8,128)(2,1)S(1)}, bf16[48,1664]{1,0:T(8,128)(2,1)S(1)}, u32[]{:S(2)}, u32[]{:S(2)}) collective-permute-start(bf16[48,1664]{1,0:T(8,128)(2,1)S(1)} %reshape.27), channel_id=1, source_target_pairs={{0,32},{1,33},{2,34},{3,35},{4,36},{5,37},{6,38},{7,39},{8,40},{9,... | collective-permute-start | bytes 479240 | tf_op jit(solution)/shard_map/ppermute | solution.py:35
  22.7 7.8 %collective-permute-start.4 = (bf16[48,1664]{1,0:T(8,128)(2,1)S(1)}, bf16[48,1664]{1,0:T(8,128)(2,1)S(1)}, u32[]{:S(2)}, u32[]{:S(2)}) collective-permute-start(bf16[48,1664]{1,0:T(8,128)(2,1)S(1)} %reshape.27), channel_id=1, source_target_pairs={{0,48},{1,49},{2,50},{3,51},{4,52},{5,53},{6,54},{7,55},{8,56},{9,... | collective-permute-start | bytes 479240 | tf_op jit(solution)/shard_map/ppermute | solution.py:35
  27.7 10.6 %collective-permute-start.10 = (bf16[2,48,1664]{2,1,0:T(8,128)(2,1)}, bf16[2,48,1664]{2,1,0:T(8,128)(2,1)S(1)}, u32[]{:S(2)}, u32[]{:S(2)}) collective-permute-start(bf16[2,48,1664]{2,1,0:T(8,128)(2,1)} %get-tuple-element.47), channel_id=1, source_target_pairs={{0,12},{1,13},{2,14},{3,15},{4,8},{5,9},{6,10},{7,11},{8,4},{9,5},... | collective-permute-start | bytes 958472 | tf_op jit(solution)/shard_map/ppermute | solution.py:35
  30.5 5.9 %collective-permute-start.5 = (bf16[2,48,1664]{2,1,0:T(8,128)(2,1)S(1)}, bf16[2,48,1664]{2,1,0:T(8,128)(2,1)S(1)}, u32[]{:S(2)}, u32[]{:S(2)}) collective-permute-start(bf16[2,48,1664]{2,1,0:T(8,128)(2,1)S(1)} %get-tuple-element.49), channel_id=1, source_target_pairs={{0,4},{1,5},{2,6},{3,7},{4,0},{5,1},{6,2},{7,3},{8,12},{9,13},{10,... | collective-permute-start | bytes 958472 | tf_op jit(solution)/shard_map/ppermute | solution.py:35
  31.8 21.1 %all-to-all-start = ((bf16[4,48,3200]{2,1,0:T(8,128)(2,1)}), bf16[4,48,3200]{2,1,0:T(8,128)(2,1)S(1)}, u32[]{:S(2)}, u32[]{:S(2)}) async-start(bf16[4,48,3200]{2,1,0:T(8,128)(2,1)} %broadcast_in_dim.30), calls=%async_computation | async-start | bytes 2457600 | tf_op jit(solution)/shard_map/all_to_all | solution.py:641
  36.5 0.7 copy-start.5
  37.2 1.6 %copy-start.8 = (bf16[2,16,768]{2,1,0:T(8,128)(2,1)S(1)}, bf16[2,16,768]{2,1,0:T(8,128)(2,1)}, u32[]{:S(2)}) copy-start(bf16[2,16,768]{2,1,0:T(8,128)(2,1)} %mine_ref.3) | copy-start | bytes 147460
  38.3 18.1 %copy-start.2 = (bf16[2,2,48,1664]{3,2,1,0:T(8,128)(2,1)}, bf16[2,2,48,1664]{3,2,1,0:T(8,128)(2,1)S(1)}, u32[]{:S(2)}) copy-start(bf16[2,2,48,1664]{3,2,1,0:T(8,128)(2,1)S(1)} %pad_maximum_fusion.l0) | copy-start | bytes 1916932
  38.3 14.6 %collective-permute-start.6 = (bf16[2,2,48,1664]{3,2,1,0:T(8,128)(2,1)S(1)}, bf16[2,2,48,1664]{3,2,1,0:T(8,128)(2,1)}, u32[]{:S(2)}, u32[]{:S(2)}) collective-permute-start(bf16[2,2,48,1664]{3,2,1,0:T(8,128)(2,1)S(1)} %pad_maximum_fusion.l0), channel_id=1, source_target_pairs={{0,12},{1,13},{2,14},{3,15},{4,8},{5,9},{6,10},{7,11},{8,4},{9,5},... | collective-permute-start | bytes 1916936 | tf_op jit(solution)/shard_map/ppermute | solution.py:35
  38.4 17.9 %copy-start.3 = (bf16[2,2,48,1664]{3,2,1,0:T(8,128)(2,1)}, bf16[2,2,48,1664]{3,2,1,0:T(8,128)(2,1)S(1)}, u32[]{:S(2)}) copy-start(bf16[2,2,48,1664]{3,2,1,0:T(8,128)(2,1)S(1)} %pad_maximum_fusion.1.l2) | copy-start | bytes 1916932
  38.5 14.4 %collective-permute-start.11 = (bf16[2,2,48,1664]{3,2,1,0:T(8,128)(2,1)S(1)}, bf16[2,2,48,1664]{3,2,1,0:T(8,128)(2,1)S(1)}, u32[]{:S(2)}, u32[]{:S(2)}) collective-permute-start(bf16[2,2,48,1664]{3,2,1,0:T(8,128)(2,1)S(1)} %pad_maximum_fusion.1.l2), channel_id=1, source_target_pairs={{0,4},{1,5},{2,6},{3,7},{4,0},{5,1},{6,2},{7,3},{8,12},{9,13},{10,... | collective-permute-start | bytes 1916936 | tf_op jit(solution)/shard_map/ppermute | solution.py:35
  38.8 1.2 %collective-permute-start.7 = (bf16[2,16,768]{2,1,0:T(8,128)(2,1)S(1)}, bf16[2,16,768]{2,1,0:T(8,128)(2,1)S(1)}, u32[]{:S(2)}, u32[]{:S(2)}) collective-permute-start(bf16[2,16,768]{2,1,0:T(8,128)(2,1)S(1)} %copy-done.8), channel_id=1, source_target_pairs={{0,64},{1,65},{2,66},{3,67},{4,68},{5,69},{6,70},{7,71},{8,72},{9,... | collective-permute-start | bytes 147464 | tf_op jit(solution)/shard_map/ppermute | solution.py:35
  38.9 15.3 %collective-permute-start.12 = (bf16[2,2,48,1664]{3,2,1,0:T(8,128)(2,1)S(1)}, bf16[2,2,48,1664]{3,2,1,0:T(8,128)(2,1)}, u32[]{:S(2)}, u32[]{:S(2)}) collective-permute-start(bf16[2,2,48,1664]{3,2,1,0:T(8,128)(2,1)S(1)} %pad_maximum_fusion.l0), channel_id=1, source_target_pairs={{0,64},{1,65},{2,66},{3,67},{4,68},{5,69},{6,70},{7,71},{8,72},{9,... | collective-permute-start | bytes 1916936 | tf_op jit(solution)/shard_map/ppermute | solution.py:35
  39.4 14.9 %collective-permute-start.14 = (bf16[2,2,48,1664]{3,2,1,0:T(8,128)(2,1)S(1)}, bf16[2,2,48,1664]{3,2,1,0:T(8,128)(2,1)}, u32[]{:S(2)}, u32[]{:S(2)}) collective-permute-start(bf16[2,2,48,1664]{3,2,1,0:T(8,128)(2,1)S(1)} %pad_maximum_fusion.1.l2), channel_id=1, source_target_pairs={{0,64},{1,65},{2,66},{3,67},{4,68},{5,69},{6,70},{7,71},{8,72},{9,... | collective-permute-start | bytes 1916936 | tf_op jit(solution)/shard_map/ppermute | solution.py:35
  40.1 16.2 %copy-start.9 = (bf16[2,16,768]{2,1,0:T(8,128)(2,1)}, bf16[2,16,768]{2,1,0:T(8,128)(2,1)S(1)}, u32[]{:S(2)}) copy-start(bf16[2,16,768]{2,1,0:T(8,128)(2,1)S(1)} %collective-permute-done.7.theirs_ref) | copy-start | bytes 147460
  52.9 3.5 %copy-start.1 = (bf16[4,48,3200]{2,1,0:T(8,128)(2,1)}, bf16[4,48,3200]{2,1,0:T(8,128)(2,1)S(1)}, u32[]{:S(2)}) copy-start(bf16[4,48,3200]{2,1,0:T(8,128)(2,1)S(1)} %all-to-all-done.images_ref) | copy-start | bytes 3686404
  52.9 3.5 %copy-start.7 = (bf16[2,2,48,1664]{3,2,1,0:T(8,128)(2,1)}, bf16[2,2,48,1664]{3,2,1,0:T(8,128)(2,1)S(1)}, u32[]{:S(2)}) copy-start(bf16[2,2,48,1664]{3,2,1,0:T(8,128)(2,1)S(1)} %collective-permute-done.11.l3) | copy-start | bytes 1916932
  52.9 2.3 %collective-permute-start.15 = (bf16[2,2,48,1664]{3,2,1,0:T(8,128)(2,1)S(1)}, bf16[2,2,48,1664]{3,2,1,0:T(8,128)(2,1)}, u32[]{:S(2)}, u32[]{:S(2)}) collective-permute-start(bf16[2,2,48,1664]{3,2,1,0:T(8,128)(2,1)S(1)} %collective-permute-done.11.l3), channel_id=1, source_target_pairs={{0,64},{1,65},{2,66},{3,67},{4,68},{5,69},{6,70},{7,71},{8,72},{9,... | collective-permute-start | bytes 1916936 | tf_op jit(solution)/shard_map/ppermute | solution.py:35
  53.4 3.0 %collective-permute-start.13 = (bf16[2,2,48,1664]{3,2,1,0:T(8,128)(2,1)}, bf16[2,2,48,1664]{3,2,1,0:T(8,128)(2,1)}, u32[]{:S(2)}, u32[]{:S(2)}) collective-permute-start(bf16[2,2,48,1664]{3,2,1,0:T(8,128)(2,1)} %collective-permute-done.6.l1), channel_id=1, source_target_pairs={{0,64},{1,65},{2,66},{3,67},{4,68},{5,69},{6,70},{7,71},{8,72},{9,... | collective-permute-start | bytes 1916936 | tf_op jit(solution)/shard_map/ppermute | solution.py:35
  78.9 14.6 %all-to-all-start.1 = ((bf16[32,4,896]{2,1,0:T(4,128)(2,1)}), bf16[32,4,896]{2,1,0:T(4,128)(2,1)S(1)}, u32[]{:S(2)}, u32[]{:S(2)}) async-start(bf16[32,4,896]{2,1,0:T(4,128)(2,1)} %get-tuple-element.27), calls=%async_computation.1 | async-start | bytes 458752 | tf_op jit(solution)/shard_map/all_to_all | solution.py:651
  93.0 1.6 %collective-permute-start.16 = (f32[4,768]{1,0:T(4,128)}, f32[4,768]{1,0:T(4,128)S(1)}, u32[]{:S(2)}, u32[]{:S(2)}) collective-permute-start(f32[4,768]{1,0:T(4,128)} %get-tuple-element.30.own_ref), channel_id=1, source_target_pairs={{0,64},{1,65},{2,66},{3,67},{4,68},{5,69},{6,70},{7,71},{8,72},{9,... | collective-permute-start | bytes 36872 | tf_op jit(solution)/shard_map/ppermute | solution.py:35
  94.6 0.6 copy-start.10
  95.2 9.8 %copy-start.6 = (f32[4,768]{1,0:T(4,128)S(1)}, f32[4,768]{1,0:T(4,128)}, u32[]{:S(2)}) copy-start(f32[4,768]{1,0:T(4,128)} %slice_divide_fusion.means_ref) | copy-start | bytes 36868
  105.0 8.2 %collective-permute-start.17 = (f32[1,768]{1,0:T(1,128)S(1)}, f32[1,768]{1,0:T(1,128)S(1)}, u32[]{:S(2)}, u32[]{:S(2)}) collective-permute-start(f32[1,768]{1,0:T(1,128)S(1)} %get-tuple-element.56), channel_id=1, source_target_pairs={{0,0},{1,1},{2,64},{3,65},{4,4},{5,5},{6,68},{7,69},{8,8},{9,9},{1... | collective-permute-start | bytes 9224 | tf_op jit(solution)/shard_map/ppermute | solution.py:35
  107.4 5.8 %collective-permute-start.18 = (f32[1,768]{1,0:T(1,128)S(1)}, f32[1,768]{1,0:T(1,128)S(1)}, u32[]{:S(2)}, u32[]{:S(2)}) collective-permute-start(f32[1,768]{1,0:T(1,128)S(1)} %get-tuple-element.57), channel_id=1, source_target_pairs={{0,1},{1,0},{2,65},{3,64},{4,5},{5,4},{6,69},{7,68},{8,9},{9,8},{1... | collective-permute-start | bytes 9224 | tf_op jit(solution)/shard_map/ppermute | solution.py:35
  110.0 3.4 %collective-permute-start.19 = (bf16[5,3072]{1,0:T(8,128)(2,1)}, bf16[5,3072]{1,0:T(8,128)(2,1)S(1)}, u32[]{:S(2)}, u32[]{:S(2)}) collective-permute-start(bf16[5,3072]{1,0:T(8,128)(2,1)} %get-tuple-element.43), channel_id=1, source_target_pairs={{0,1},{1,0},{2,3},{3,2},{4,5},{5,4},{6,7},{7,6},{8,9},{9,8},{10,11... | collective-permute-start | bytes 92168 | tf_op jit(solution)/shard_map/ppermute | solution.py:35
  110.0 4.4 %collective-permute-start.20 = (bf16[5,3072]{1,0:T(8,128)(2,1)}, bf16[5,3072]{1,0:T(8,128)(2,1)S(1)}, u32[]{:S(2)}, u32[]{:S(2)}) collective-permute-start(bf16[5,3072]{1,0:T(8,128)(2,1)} %get-tuple-element.44), channel_id=1, source_target_pairs={{0,3},{1,2},{2,1},{3,0},{4,7},{5,6},{6,5},{7,4},{8,11},{9,10},{10,... | collective-permute-start | bytes 92168 | tf_op jit(solution)/shard_map/ppermute | solution.py:35
  110.0 4.9 %collective-permute-start.21 = (bf16[5,3072]{1,0:T(8,128)(2,1)}, bf16[5,3072]{1,0:T(8,128)(2,1)S(1)}, u32[]{:S(2)}, u32[]{:S(2)}) collective-permute-start(bf16[5,3072]{1,0:T(8,128)(2,1)} %get-tuple-element.45), channel_id=1, source_target_pairs={{0,2},{1,3},{2,0},{3,1},{4,6},{5,7},{6,4},{7,5},{8,10},{9,11},{10,... | collective-permute-start | bytes 92168 | tf_op jit(solution)/shard_map/ppermute | solution.py:35
  115.7 3.6 %collective-permute-start.22 = (f32[5,3072]{1,0:T(8,128)S(1)}, f32[5,3072]{1,0:T(8,128)S(1)}, u32[]{:S(2)}, u32[]{:S(2)}) collective-permute-start(f32[5,3072]{1,0:T(8,128)S(1)} %convert_add_fusion), channel_id=1, source_target_pairs={{0,64},{1,65},{2,66},{3,67},{4,68},{5,69},{6,70},{7,71},{8,72},{9,... | collective-permute-start | bytes 184328 | tf_op jit(solution)/shard_map/ppermute | solution.py:35

commit v4 on v3

--- a/solution.py
+++ b/solution.py
@@ -11,6 +11,7 @@
 D = 768
 PIXELS = 3072
 IPC = 10
+SYN_AT = PIXELS + 128
 SLOT = 6
 SYN = 4 * SLOT
 BLOCK_ROWS = 48
@@ -195,7 +196,7 @@
 
     for k in range(4):
         pltpu.make_async_copy(
-            images_ref.at[k, 0:32], x_ref.at[32 * k : 32 * k + 32], sems.at[1]
+            images_ref.at[k, :, :SYN_AT], x_ref.at[32 * k : 32 * k + 32], sems.at[1]
         ).start()
     near_block = ((0, 0), (0, 1), (1, 0), (1, 1))
     far_block = ((2, 0), (3, 0), (2, 1), (3, 1))
@@ -300,12 +301,11 @@
     where_ref, mine_ref, theirs_ref, images_ref, w_in, wp_in,
     sum_ref, n_out, r1_out, qkv_out, p_out, xhat2_out, r2_out,
     n_ref, r1_ref, qkv_ref, p_ref, xhat2_ref, r2_ref,
-    e_ref, att_ref, x_ref, posx_ref, w_ref, wp_ref, in_sems, sems,
+    e_ref, att_ref, x_ref, x32_ref, pixels_ref, posx_ref, w_ref, wp_ref, in_sems, sems,
 ):
     tiles = SYN // 8
     pairs = [
-        (images_ref.at[k, 32:48, :PIXELS], x_ref.at[16 * k : 16 * k + 16])
-        for k in range(4)
+        (images_ref.at[k, :, SYN_AT:], x_ref.at[32 * k : 32 * k + 32]) for k in range(4)
     ]
     loads = copies_of(pairs + [(wp_in, wp_ref), (w_in, w_ref)], in_sems)
     saves = [
@@ -320,7 +320,15 @@
     spread_position(where_ref, mine_ref, theirs_ref, posx_ref)
     for copy in loads[:5]:
         copy.wait()
-    x32 = jnp.concatenate([x_ref[16 * k : 16 * k + 16].astype(F32)[:SLOT] for k in range(4)], axis=0)
+    x32_ref[...] = x_ref[...].astype(F32).reshape(4, 32, 512)
+    pixels_ref[...] = jnp.zeros_like(pixels_ref)
+    for k in range(4):
+        for m in range(6):
+            for i in range(5):
+                pixels_ref[SLOT * k + i : SLOT * k + i + 1, 512 * m : 512 * m + 512] = x32_ref[
+                    k, 6 * i + m : 6 * i + m + 1
+                ]
+    x32 = pixels_ref[...]
     for t, e in enumerate(embed_rows(x32, wp_ref, tiles)):
         rows = slice(128 * t, 128 * t + 128)
         e = e + posx_ref[...]
@@ -550,7 +558,9 @@
         + [
             buffer((SYN_ROWS, D), F32),
             buffer((SYN_ROWS, D), BF),
-            buffer((64, PIXELS), BF),
+            buffer((128, 512), BF),
+            buffer((4, 32, 512), F32),
+            buffer((SYN, PIXELS), F32),
             buffer((128, D), F32),
         ]
         + [buffer(s, t) for s, t in WEIGHTS]
@@ -632,14 +642,14 @@
     tagged = jnp.concatenate(
         [real_images, jnp.broadcast_to(index[:, None], (64, 128)).astype(BF)], axis=1
     )
-    syn = lax.dynamic_slice_in_dim(synthetic, 5 * core, 5, 0).astype(BF)
+    syn = lax.dynamic_slice_in_dim(synthetic, 5 * core, 5, 0).astype(BF).reshape(30, 512)
     images = jnp.concatenate(
-        [lax.dynamic_slice_in_dim(tagged, 32 * core, 32, 0), jnp.pad(syn, ((0, 11), (0, 128)))],
-        axis=0,
+        [lax.dynamic_slice_in_dim(tagged, 32 * core, 32, 0), jnp.pad(syn, ((0, 2), (0, 0)))],
+        axis=1,
     )
     rings = [[flat(c, yz // 4, yz % 4, xx) for xx in range(4)] for c in range(2) for yz in range(16)]
     images = lax.all_to_all(
-        jnp.broadcast_to(images[None], (4, 48, PIXELS + 128)), AXES, 0, 0, axis_index_groups=rings
+        jnp.broadcast_to(images[None], (4, 32, SYN_AT + 512)), AXES, 0, 0, axis_index_groups=rings
     )
     images = (images, swap_cores(position))
     mine, theirs, images, their_pos = gather_weights(
@@ -655,7 +665,7 @@
     own, *saved = run_synth(place, position, their_pos, images, w, wp)
     grads = run_back(place, means, own, swap_cores(own), w, wp, saved)
 
-    means, grads = lax.optimization_barrier((means, grads))
+    beside, means = lax.optimization_barrier((other_x(grads[1]), means))
     sent = []
     for m in range(2):
         row = lax.dynamic_index_in_dim(means, (x - m) % 2 + 2 * core, 0, keepdims=True)
@@ -666,7 +676,7 @@
     second = jnp.where(x % 2 == 0, sent[1], sent[0])
     real_means = jnp.stack([first, second])
 
-    pixel = grads[0].astype(F32) + other_x(grads[1]).astype(F32)
+    pixel = grads[0].astype(F32) + beside.astype(F32)
     pixel = pixel + across_x(grads[2]).astype(F32) + from_x(grads[3], 2).astype(F32)
     other = swap_cores(pixel)
     pixel_grad = jnp.concatenate(

time: 121 us -> 115 us (0.950)
  starting transfers between devices: 39.6 us -> 37.8 us
  other arithmetic: 7.04 us -> 5.37 us
  waiting for transfers between devices: 27 us -> 25.6 us
    ppermute x23, starting transfers between devices: 31.1 us -> 28.8 us  [permute(): lax.ppermute(a, AXES, [(flat(*p), flat(*target(*p))) for p in PLACES])]
    all_to_all x1, waiting for transfers between devices: 12.8 us -> 11.4 us  [local(): lax.all_to_all(jnp.broadcast_to(images[None], (4, 32, SYN_AT + 512)), AXE...]
  transfers between devices with their start and end apart: 25 -> 25, of which waited for: 13 -> 11; matrix products, arithmetic and copies ran while one was open for 5% -> 4% of each run, Pallas kernels for 8% -> 8%
where the time goes in v4:
time: 115 us; the launch traced here: 114 us
  Pallas kernels  41.3 us (36%)
  starting transfers between devices  37.8 us (33%)
  waiting for transfers between devices  25.6 us (22%)
  other arithmetic  5.37 us (5%)
  local copies, waits for them, and re-layouts  2.93 us (3%)
  between operations  1.26 us (1%)
    ppermute x23, starting transfers between devices, permute(): lax.ppermute(a, AXES, [(flat(*p), flat(*target(*p))) for p in PLACES])  28.8 us
    pallas_call x1, Pallas kernels, run_real(): pl.pallas_call(real_kernel, in_specs=[SMEM_SPEC, VMEM_SPEC, VMEM_SPEC] +...  22.6 us
    ppermute x23, waiting for transfers between devices, permute(): lax.ppermute(a, AXES, [(flat(*p), flat(*target(*p))) for p in PLACES])  14.2 us
    all_to_all x1, waiting for transfers between devices, local(): lax.all_to_all(jnp.broadcast_to(images[None], (4, 32, SYN_AT + 512)), AXE...  11.4 us
    pallas_call x1, Pallas kernels, run_back(): pl.pallas_call(back_kernel, in_specs=[SMEM_SPEC] + [VMEM_SPEC] * 3 + [ANY...  9.76 us
    pallas_call x1, Pallas kernels, run_synth(): pl.pallas_call(synth_kernel, in_specs=[SMEM_SPEC, VMEM_SPEC, VMEM_SPEC] +...  8.93 us
    all_to_all x1, starting transfers between devices, local(): got = lax.all_to_all(csum, AXES, 0, 0, axis_index_groups=groups)  5.36 us
    all_to_all x1, starting transfers between devices, local(): lax.all_to_all(jnp.broadcast_to(images[None], (4, 32, SYN_AT + 512)), AXE...  3.64 us
  transfers between devices with their start and end apart: 25, of which 11 were waited for; matrix products, arithmetic and copies ran while one was open for 4% of the time, Pallas kernels for 8%

profile of v4, /device:TPU:1, one launch (start us, length us, event | category | flops | bytes accessed | tf_op | source)
XLA Modules:
  0.0 114.2 jit_solution(17436843074499814324)
XLA Ops:
  0.9 0.7 reshape.27
  1.7 1.1 pad_maximum_fusion.5
  2.8 0.1 maximum_bitcast_fusion
  3.1 3.4 %collective-permute-start.3 = (bf16[12,1664]{1,0:T(8,128)(2,1)S(1)}, bf16[12,1664]{1,0:T(8,128)(2,1)S(1)}, u32[]{:S(2)}, u32[]{:S(2)}) collective-permute-start(bf16[12,1664]{1,0:T(8,128)(2,1)S(1)} %get-tuple-element.44), channel_id=1, source_target_pairs={{0,1},{1,64},{2,65},{3,0},{4,5},{5,68},{6,69},{7,4},{8,9},{9,72},{... | collective-permute-start | bytes 119816 | tf_op jit(solution)/shard_map/ppermute | solution.py:36
  6.4 2.7 %collective-permute-start.2 = (bf16[12,1664]{1,0:T(8,128)(2,1)S(1)}, bf16[12,1664]{1,0:T(8,128)(2,1)S(1)}, u32[]{:S(2)}, u32[]{:S(2)}) collective-permute-start(bf16[12,1664]{1,0:T(8,128)(2,1)S(1)} %get-tuple-element.45), channel_id=1, source_target_pairs={{0,64},{1,65},{2,0},{3,1},{4,68},{5,69},{6,4},{7,5},{8,72},{9,73},... | collective-permute-start | bytes 119816 | tf_op jit(solution)/shard_map/ppermute | solution.py:36
  9.2 1.2 %collective-permute-start.1 = (bf16[12,1664]{1,0:T(8,128)(2,1)S(1)}, bf16[12,1664]{1,0:T(8,128)(2,1)S(1)}, u32[]{:S(2)}, u32[]{:S(2)}) collective-permute-start(bf16[12,1664]{1,0:T(8,128)(2,1)S(1)} %get-tuple-element.46), channel_id=1, source_target_pairs={{0,65},{1,0},{2,1},{3,64},{4,69},{5,4},{6,5},{7,68},{8,73},{9,8},{... | collective-permute-start | bytes 119816 | tf_op jit(solution)/shard_map/ppermute | solution.py:36
  10.4 1.9 %collective-permute-start = (bf16[12,1664]{1,0:T(8,128)(2,1)S(1)}, bf16[12,1664]{1,0:T(8,128)(2,1)S(1)}, u32[]{:S(2)}, u32[]{:S(2)}) collective-permute-start(bf16[12,1664]{1,0:T(8,128)(2,1)S(1)} %get-tuple-element.47), channel_id=1, source_target_pairs={{0,0},{1,1},{2,64},{3,65},{4,4},{5,5},{6,68},{7,69},{8,8},{9,9},{1... | collective-permute-start | bytes 119816 | tf_op jit(solution)/shard_map/ppermute | solution.py:36
  12.4 0.2 select_reduce_fusion
  12.7 4.7 %collective-permute-done = bf16[12,1664]{1,0:T(8,128)(2,1)S(1)} collective-permute-done((bf16[12,1664]{1,0:T(8,128)(2,1)S(1)}, bf16[12,1664]{1,0:T(8,128)(2,1)S(1)}, u32[]{:S(2)}, u32[]{:S(2)}) %collective-permute-start) | collective-permute-done | bytes 39968 | tf_op jit(solution)/shard_map/ppermute | solution.py:36
  17.6 1.7 %collective-permute-start.9 = (bf16[48,1664]{1,0:T(8,128)(2,1)S(1)}, bf16[48,1664]{1,0:T(8,128)(2,1)S(1)}, u32[]{:S(2)}, u32[]{:S(2)}) collective-permute-start(bf16[48,1664]{1,0:T(8,128)(2,1)S(1)} %reshape.30), channel_id=1, source_target_pairs={{0,16},{1,17},{2,18},{3,19},{4,20},{5,21},{6,22},{7,23},{8,24},{9,... | collective-permute-start | bytes 479240 | tf_op jit(solution)/shard_map/ppermute | solution.py:36
  19.3 3.3 %collective-permute-start.8 = (bf16[48,1664]{1,0:T(8,128)(2,1)S(1)}, bf16[48,1664]{1,0:T(8,128)(2,1)S(1)}, u32[]{:S(2)}, u32[]{:S(2)}) collective-permute-start(bf16[48,1664]{1,0:T(8,128)(2,1)S(1)} %reshape.30), channel_id=1, source_target_pairs={{0,32},{1,33},{2,34},{3,35},{4,36},{5,37},{6,38},{7,39},{8,40},{9,... | collective-permute-start | bytes 479240 | tf_op jit(solution)/shard_map/ppermute | solution.py:36
  22.7 0.8 collective-permute-start.4
  23.5 0.6 collective-permute-done.9
  24.1 2.9 %collective-permute-done.8 = bf16[48,1664]{1,0:T(8,128)(2,1)S(1)} collective-permute-done((bf16[48,1664]{1,0:T(8,128)(2,1)S(1)}, bf16[48,1664]{1,0:T(8,128)(2,1)S(1)}, u32[]{:S(2)}, u32[]{:S(2)}) %collective-permute-start.8) | collective-permute-done | bytes 159776 | tf_op jit(solution)/shard_map/ppermute | solution.py:36
  27.0 2.9 %collective-permute-start.10 = (bf16[2,48,1664]{2,1,0:T(8,128)(2,1)S(1)}, bf16[2,48,1664]{2,1,0:T(8,128)(2,1)S(1)}, u32[]{:S(2)}, u32[]{:S(2)}) collective-permute-start(bf16[2,48,1664]{2,1,0:T(8,128)(2,1)S(1)} %get-tuple-element.41), channel_id=1, source_target_pairs={{0,12},{1,13},{2,14},{3,15},{4,8},{5,9},{6,10},{7,11},{8,4},{9,5},... | collective-permute-start | bytes 958472 | tf_op jit(solution)/shard_map/ppermute | solution.py:36
  30.1 1.0 broadcast_in_dim.30
  31.2 3.6 %all-to-all-start = ((bf16[4,32,3712]{2,1,0:T(8,128)(2,1)}), bf16[4,32,3712]{2,1,0:T(8,128)(2,1)S(1)}, u32[]{:S(2)}, u32[]{:S(2)}) async-start(bf16[4,32,3712]{2,1,0:T(8,128)(2,1)} %broadcast_in_dim.30), calls=%async_computation | async-start | bytes 1900544 | tf_op jit(solution)/shard_map/all_to_all | solution.py:651
  34.8 1.1 collective-permute-done.5
  36.0 0.1 collective-permute-start.6
  36.2 0.4 collective-permute-start.11
  36.6 0.5 collective-permute-start.12
  37.1 0.7 collective-permute-done.7.theirs_ref
  37.9 11.4 %all-to-all-done.images_ref = bf16[4,32,3712]{2,1,0:T(8,128)(2,1)S(1)} async-done(((bf16[4,32,3712]{2,1,0:T(8,128)(2,1)}), bf16[4,32,3712]{2,1,0:T(8,128)(2,1)S(1)}, u32[]{:S(2)}, u32[]{:S(2)}) %all-to-all-start) | async-done | bytes 950304 | tf_op jit(solution)/shard_map/all_to_all | solution.py:651
  49.3 0.5 collective-permute-start.15
  49.7 0.3 collective-permute-start.13
  50.0 0.6 pad_add_fusion.where_ref
  50.7 0.9 collective-permute-done.15.o3
  51.6 1.1 collective-permute-done.13.o1
  52.7 22.6 %real_forward.1 = (bf16[32,4,896]{2,1,0:T(4,128)(2,1)}, bf16[768,3328]{1,0:T(8,128)(2,1)}, bf16[2,256,768]{2,1,0:T(8,128)(2,1)}) custom-call(s32[4]{0:T(128)} %pad_add_fusion.where_ref, bf16[2,16,768]{2,1,0:T(8,128)(2,1)} %mine_ref.3, bf16[2,16,768]{2,1,0:T(8,128)(2,1)} %copy-done.8, bf16[4,32,3712]{2,1,0:T(8,128)(2,1)} %copy-done.1, ...), custom_call_target="tpu_custom_call" | custom-call | flops 14000000000 | bytes 12000000 | tf_op jit(solution)/shard_map/real_forward/pallas_call | solution.py:508
  75.3 5.4 %all-to-all-start.1 = ((bf16[32,4,896]{2,1,0:T(4,128)(2,1)}), bf16[32,4,896]{2,1,0:T(4,128)(2,1)S(1)}, u32[]{:S(2)}, u32[]{:S(2)}) async-start(bf16[32,4,896]{2,1,0:T(4,128)(2,1)} %get-tuple-element.24), calls=%async_computation.1 | async-start | bytes 458752 | tf_op jit(solution)/shard_map/all_to_all | solution.py:661
  80.7 8.9 %synth_forward.1 = (f32[4,768]{1,0:T(4,128)}, bf16[384,768]{1,0:T(8,128)(2,1)}, f32[384,128]{1,0:T(8,128)}, bf16[384,2304]{1,0:T(8,128)(2,1)}, bf16[384,1536]{1,...) custom-call(s32[4]{0:T(128)} %pad_add_fusion.where_ref, bf16[2,16,768]{2,1,0:T(8,128)(2,1)} %mine_ref.3, ...), custom_call_target="tpu_custom_call" | custom-call | flops 3000000000 | bytes 12000000 | tf_op jit(solution)/shard_map/synth_forward/pallas_call | solution.py:551
  89.6 0.5 collective-permute-start.16
  90.1 0.1 convert_reduce_fusion
  90.2 0.1 fusion.5
  90.4 0.7 slice_divide_fusion.means_ref
  91.0 0.1 collective-permute-done.16.their_ref
  91.2 0.6 copy-done.9
  91.8 9.8 %synth_backward.1 = (bf16[5,3072]{1,0:T(8,128)(2,1)}, bf16[5,3072]{1,0:T(8,128)(2,1)}, bf16[5,3072]{1,0:T(8,128)(2,1)}, bf16[5,3072]{1,0:T(8,128)(2,1)}) custom-call(s32[4]{0:T(128)} %pad_add_fusion.where_ref, f32[4,768]{1,0:T(4,128)} %slice_divide_fusion.means_ref, f32[4,768]{1,0:T(4,128)} %get-tuple-element.27.own_ref, f32[4,768]{1,0:T(4,128)} %copy-done.9, ...), custom_call_target="tpu_custom_call" | custom-call | flops 4000000000 | bytes 12000000 | tf_op jit(solution)/shard_map/synth_backward/pallas_call | solution.py:577
  101.5 0.4 collective-permute-start.17
  101.9 0.7 collective-permute-start.20
  102.7 2.2 %collective-permute-start.21 = (bf16[5,3072]{1,0:T(8,128)(2,1)}, bf16[5,3072]{1,0:T(8,128)(2,1)S(1)}, u32[]{:S(2)}, u32[]{:S(2)}) collective-permute-start(bf16[5,3072]{1,0:T(8,128)(2,1)} %get-tuple-element.39), channel_id=1, source_target_pairs={{0,2},{1,3},{2,0},{3,1},{4,6},{5,7},{6,4},{7,5},{8,10},{9,11},{10,... | collective-permute-start | bytes 92168 | tf_op jit(solution)/shard_map/ppermute | solution.py:36
  104.9 3.6 %collective-permute-start.18 = (f32[1,768]{1,0:T(1,128)S(1)}, f32[1,768]{1,0:T(1,128)S(1)}, u32[]{:S(2)}, u32[]{:S(2)}) collective-permute-start(f32[1,768]{1,0:T(1,128)S(1)} %get-tuple-element.50), channel_id=1, source_target_pairs={{0,0},{1,1},{2,64},{3,65},{4,4},{5,5},{6,68},{7,69},{8,8},{9,9},{1... | collective-permute-start | bytes 9224 | tf_op jit(solution)/shard_map/ppermute | solution.py:36
  108.5 1.3 %collective-permute-start.19 = (f32[1,768]{1,0:T(1,128)S(1)}, f32[1,768]{1,0:T(1,128)S(1)}, u32[]{:S(2)}, u32[]{:S(2)}) collective-permute-start(f32[1,768]{1,0:T(1,128)S(1)} %get-tuple-element.51), channel_id=1, source_target_pairs={{0,1},{1,0},{2,65},{3,64},{4,5},{5,4},{6,69},{7,68},{8,9},{9,8},{1... | collective-permute-start | bytes 9224 | tf_op jit(solution)/shard_map/ppermute | solution.py:36
  109.9 0.8 convert_add_fusion
  110.8 0.5 collective-permute-done.18
  111.3 1.5 %collective-permute-done.19 = f32[1,768]{1,0:T(1,128)S(1)} collective-permute-done((f32[1,768]{1,0:T(1,128)S(1)}, f32[1,768]{1,0:T(1,128)S(1)}, u32[]{:S(2)}, u32[]{:S(2)}) %collective-permute-start.19) | collective-permute-done | bytes 3104 | tf_op jit(solution)/shard_map/ppermute | solution.py:36
  112.9 0.6 pad_maximum_fusion.6
  113.5 0.7 pad_maximum_fusion.4
  (69 shorter events, 1.1 us)
Async XLA Ops:
  0.6 22.0 %copy-start = (f32[10,3072]{1,0:T(8,128)S(1)}, f32[10,3072]{1,0:T(8,128)}, u32[]{:S(2)}) copy-start(f32[10,3072]{1,0:T(8,128)} %param.11) | copy-start | bytes 368644
  0.6 11.7 %copy-start.10 = (s32[64]{0:T(128)S(1)}, s32[64]{0:T(128)}, u32[]{:S(2)}) copy-start(s32[64]{0:T(128)} %param.10) | copy-start | bytes 772
  0.7 11.7 %copy-start.11 = (s32[64]{0:T(128)S(1)}, s32[64]{0:T(128)}, u32[]{:S(2)}) copy-start(s32[64]{0:T(128)} %param.9) | copy-start | bytes 772
  0.7 11.9 %copy-start.4 = (bf16[64,3072]{1,0:T(8,128)(2,1)S(1)}, bf16[64,3072]{1,0:T(8,128)(2,1)}, u32[]{:S(2)}) copy-start(bf16[64,3072]{1,0:T(8,128)(2,1)} %param.8) | copy-start | bytes 1179652
  3.1 14.4 %collective-permute-start.3 = (bf16[12,1664]{1,0:T(8,128)(2,1)S(1)}, bf16[12,1664]{1,0:T(8,128)(2,1)S(1)}, u32[]{:S(2)}, u32[]{:S(2)}) collective-permute-start(bf16[12,1664]{1,0:T(8,128)(2,1)S(1)} %get-tuple-element.44), channel_id=1, source_target_pairs={{0,1},{1,64},{2,65},{3,0},{4,5},{5,68},{6,69},{7,4},{8,9},{9,72},{... | collective-permute-start | bytes 119816 | tf_op jit(solution)/shard_map/ppermute | solution.py:36
  6.4 10.9 %collective-permute-start.2 = (bf16[12,1664]{1,0:T(8,128)(2,1)S(1)}, bf16[12,1664]{1,0:T(8,128)(2,1)S(1)}, u32[]{:S(2)}, u32[]{:S(2)}) collective-permute-start(bf16[12,1664]{1,0:T(8,128)(2,1)S(1)} %get-tuple-element.45), channel_id=1, source_target_pairs={{0,64},{1,65},{2,0},{3,1},{4,68},{5,69},{6,4},{7,5},{8,72},{9,73},... | collective-permute-start | bytes 119816 | tf_op jit(solution)/shard_map/ppermute | solution.py:36
  9.2 8.2 %collective-permute-start.1 = (bf16[12,1664]{1,0:T(8,128)(2,1)S(1)}, bf16[12,1664]{1,0:T(8,128)(2,1)S(1)}, u32[]{:S(2)}, u32[]{:S(2)}) collective-permute-start(bf16[12,1664]{1,0:T(8,128)(2,1)S(1)} %get-tuple-element.46), channel_id=1, source_target_pairs={{0,65},{1,0},{2,1},{3,64},{4,69},{5,4},{6,5},{7,68},{8,73},{9,8},{... | collective-permute-start | bytes 119816 | tf_op jit(solution)/shard_map/ppermute | solution.py:36
  10.4 6.9 %collective-permute-start = (bf16[12,1664]{1,0:T(8,128)(2,1)S(1)}, bf16[12,1664]{1,0:T(8,128)(2,1)S(1)}, u32[]{:S(2)}, u32[]{:S(2)}) collective-permute-start(bf16[12,1664]{1,0:T(8,128)(2,1)S(1)} %get-tuple-element.47), channel_id=1, source_target_pairs={{0,0},{1,1},{2,64},{3,65},{4,4},{5,5},{6,68},{7,69},{8,8},{9,9},{1... | collective-permute-start | bytes 119816 | tf_op jit(solution)/shard_map/ppermute | solution.py:36
  17.6 6.5 %collective-permute-start.9 = (bf16[48,1664]{1,0:T(8,128)(2,1)S(1)}, bf16[48,1664]{1,0:T(8,128)(2,1)S(1)}, u32[]{:S(2)}, u32[]{:S(2)}) collective-permute-start(bf16[48,1664]{1,0:T(8,128)(2,1)S(1)} %reshape.30), channel_id=1, source_target_pairs={{0,16},{1,17},{2,18},{3,19},{4,20},{5,21},{6,22},{7,23},{8,24},{9,... | collective-permute-start | bytes 479240 | tf_op jit(solution)/shard_map/ppermute | solution.py:36
  19.3 7.7 %collective-permute-start.8 = (bf16[48,1664]{1,0:T(8,128)(2,1)S(1)}, bf16[48,1664]{1,0:T(8,128)(2,1)S(1)}, u32[]{:S(2)}, u32[]{:S(2)}) collective-permute-start(bf16[48,1664]{1,0:T(8,128)(2,1)S(1)} %reshape.30), channel_id=1, source_target_pairs={{0,32},{1,33},{2,34},{3,35},{4,36},{5,37},{6,38},{7,39},{8,40},{9,... | collective-permute-start | bytes 479240 | tf_op jit(solution)/shard_map/ppermute | solution.py:36
  22.7 7.2 %collective-permute-start.4 = (bf16[48,1664]{1,0:T(8,128)(2,1)S(1)}, bf16[48,1664]{1,0:T(8,128)(2,1)S(1)}, u32[]{:S(2)}, u32[]{:S(2)}) collective-permute-start(bf16[48,1664]{1,0:T(8,128)(2,1)S(1)} %reshape.30), channel_id=1, source_target_pairs={{0,48},{1,49},{2,50},{3,51},{4,52},{5,53},{6,54},{7,55},{8,56},{9,... | collective-permute-start | bytes 479240 | tf_op jit(solution)/shard_map/ppermute | solution.py:36
  27.0 9.1 %collective-permute-start.10 = (bf16[2,48,1664]{2,1,0:T(8,128)(2,1)S(1)}, bf16[2,48,1664]{2,1,0:T(8,128)(2,1)S(1)}, u32[]{:S(2)}, u32[]{:S(2)}) collective-permute-start(bf16[2,48,1664]{2,1,0:T(8,128)(2,1)S(1)} %get-tuple-element.41), channel_id=1, source_target_pairs={{0,12},{1,13},{2,14},{3,15},{4,8},{5,9},{6,10},{7,11},{8,4},{9,5},... | collective-permute-start | bytes 958472 | tf_op jit(solution)/shard_map/ppermute | solution.py:36
  30.0 5.9 %collective-permute-start.5 = (bf16[2,48,1664]{2,1,0:T(8,128)(2,1)S(1)}, bf16[2,48,1664]{2,1,0:T(8,128)(2,1)S(1)}, u32[]{:S(2)}, u32[]{:S(2)}) collective-permute-start(bf16[2,48,1664]{2,1,0:T(8,128)(2,1)S(1)} %get-tuple-element.43), channel_id=1, source_target_pairs={{0,4},{1,5},{2,6},{3,7},{4,0},{5,1},{6,2},{7,3},{8,12},{9,13},{10,... | collective-permute-start | bytes 958472 | tf_op jit(solution)/shard_map/ppermute | solution.py:36
  31.2 5.5 %copy-start.7 = (bf16[2,16,768]{2,1,0:T(8,128)(2,1)S(1)}, bf16[2,16,768]{2,1,0:T(8,128)(2,1)}, u32[]{:S(2)}) copy-start(bf16[2,16,768]{2,1,0:T(8,128)(2,1)} %mine_ref.3) | copy-start | bytes 147460
  31.2 18.1 %all-to-all-start = ((bf16[4,32,3712]{2,1,0:T(8,128)(2,1)}), bf16[4,32,3712]{2,1,0:T(8,128)(2,1)S(1)}, u32[]{:S(2)}, u32[]{:S(2)}) async-start(bf16[4,32,3712]{2,1,0:T(8,128)(2,1)} %broadcast_in_dim.30), calls=%async_computation | async-start | bytes 1900544 | tf_op jit(solution)/shard_map/all_to_all | solution.py:651
  36.0 16.7 %copy-start.2 = (bf16[2,2,48,1664]{3,2,1,0:T(8,128)(2,1)}, bf16[2,2,48,1664]{3,2,1,0:T(8,128)(2,1)S(1)}, u32[]{:S(2)}) copy-start(bf16[2,2,48,1664]{3,2,1,0:T(8,128)(2,1)S(1)} %pad_maximum_fusion.l0) | copy-start | bytes 1916932
  36.0 13.3 %collective-permute-start.6 = (bf16[2,2,48,1664]{3,2,1,0:T(8,128)(2,1)S(1)}, bf16[2,2,48,1664]{3,2,1,0:T(8,128)(2,1)}, u32[]{:S(2)}, u32[]{:S(2)}) collective-permute-start(bf16[2,2,48,1664]{3,2,1,0:T(8,128)(2,1)S(1)} %pad_maximum_fusion.l0), channel_id=1, source_target_pairs={{0,12},{1,13},{2,14},{3,15},{4,8},{5,9},{6,10},{7,11},{8,4},{9,5},... | collective-permute-start | bytes 1916936 | tf_op jit(solution)/shard_map/ppermute | solution.py:36
  36.2 16.5 %copy-start.3 = (bf16[2,2,48,1664]{3,2,1,0:T(8,128)(2,1)}, bf16[2,2,48,1664]{3,2,1,0:T(8,128)(2,1)S(1)}, u32[]{:S(2)}) copy-start(bf16[2,2,48,1664]{3,2,1,0:T(8,128)(2,1)S(1)} %pad_maximum_fusion.1.l2) | copy-start | bytes 1916932
  36.2 13.1 %collective-permute-start.11 = (bf16[2,2,48,1664]{3,2,1,0:T(8,128)(2,1)S(1)}, bf16[2,2,48,1664]{3,2,1,0:T(8,128)(2,1)S(1)}, u32[]{:S(2)}, u32[]{:S(2)}) collective-permute-start(bf16[2,2,48,1664]{3,2,1,0:T(8,128)(2,1)S(1)} %pad_maximum_fusion.1.l2), channel_id=1, source_target_pairs={{0,4},{1,5},{2,6},{3,7},{4,0},{5,1},{6,2},{7,3},{8,12},{9,13},{10,... | collective-permute-start | bytes 1916936 | tf_op jit(solution)/shard_map/ppermute | solution.py:36
  36.6 1.3 %collective-permute-start.7 = (bf16[2,16,768]{2,1,0:T(8,128)(2,1)S(1)}, bf16[2,16,768]{2,1,0:T(8,128)(2,1)S(1)}, u32[]{:S(2)}, u32[]{:S(2)}) collective-permute-start(bf16[2,16,768]{2,1,0:T(8,128)(2,1)S(1)} %copy-done.7), channel_id=1, source_target_pairs={{0,64},{1,65},{2,66},{3,67},{4,68},{5,69},{6,70},{7,71},{8,72},{9,... | collective-permute-start | bytes 147464 | tf_op jit(solution)/shard_map/ppermute | solution.py:36
  36.6 14.0 %collective-permute-start.12 = (bf16[2,2,48,1664]{3,2,1,0:T(8,128)(2,1)S(1)}, bf16[2,2,48,1664]{3,2,1,0:T(8,128)(2,1)}, u32[]{:S(2)}, u32[]{:S(2)}) collective-permute-start(bf16[2,2,48,1664]{3,2,1,0:T(8,128)(2,1)S(1)} %pad_maximum_fusion.l0), channel_id=1, source_target_pairs={{0,64},{1,65},{2,66},{3,67},{4,68},{5,69},{6,70},{7,71},{8,72},{9,... | collective-permute-start | bytes 1916936 | tf_op jit(solution)/shard_map/ppermute | solution.py:36
  37.1 13.5 %collective-permute-start.14 = (bf16[2,2,48,1664]{3,2,1,0:T(8,128)(2,1)S(1)}, bf16[2,2,48,1664]{3,2,1,0:T(8,128)(2,1)}, u32[]{:S(2)}, u32[]{:S(2)}) collective-permute-start(bf16[2,2,48,1664]{3,2,1,0:T(8,128)(2,1)S(1)} %pad_maximum_fusion.1.l2), channel_id=1, source_target_pairs={{0,64},{1,65},{2,66},{3,67},{4,68},{5,69},{6,70},{7,71},{8,72},{9,... | collective-permute-start | bytes 1916936 | tf_op jit(solution)/shard_map/ppermute | solution.py:36
  37.9 14.8 %copy-start.8 = (bf16[2,16,768]{2,1,0:T(8,128)(2,1)}, bf16[2,16,768]{2,1,0:T(8,128)(2,1)S(1)}, u32[]{:S(2)}) copy-start(bf16[2,16,768]{2,1,0:T(8,128)(2,1)S(1)} %collective-permute-done.7.theirs_ref) | copy-start | bytes 147460
  49.2 3.5 %copy-start.1 = (bf16[4,32,3712]{2,1,0:T(8,128)(2,1)}, bf16[4,32,3712]{2,1,0:T(8,128)(2,1)S(1)}, u32[]{:S(2)}) copy-start(bf16[4,32,3712]{2,1,0:T(8,128)(2,1)S(1)} %all-to-all-done.images_ref) | copy-start | bytes 2850820
  49.3 3.5 %copy-start.6 = (bf16[2,2,48,1664]{3,2,1,0:T(8,128)(2,1)}, bf16[2,2,48,1664]{3,2,1,0:T(8,128)(2,1)S(1)}, u32[]{:S(2)}) copy-start(bf16[2,2,48,1664]{3,2,1,0:T(8,128)(2,1)S(1)} %collective-permute-done.11.l3) | copy-start | bytes 1916932
  49.3 2.3 %collective-permute-start.15 = (bf16[2,2,48,1664]{3,2,1,0:T(8,128)(2,1)S(1)}, bf16[2,2,48,1664]{3,2,1,0:T(8,128)(2,1)}, u32[]{:S(2)}, u32[]{:S(2)}) collective-permute-start(bf16[2,2,48,1664]{3,2,1,0:T(8,128)(2,1)S(1)} %collective-permute-done.11.l3), channel_id=1, source_target_pairs={{0,64},{1,65},{2,66},{3,67},{4,68},{5,69},{6,70},{7,71},{8,72},{9,... | collective-permute-start | bytes 1916936 | tf_op jit(solution)/shard_map/ppermute | solution.py:36
  49.7 3.0 %collective-permute-start.13 = (bf16[2,2,48,1664]{3,2,1,0:T(8,128)(2,1)}, bf16[2,2,48,1664]{3,2,1,0:T(8,128)(2,1)}, u32[]{:S(2)}, u32[]{:S(2)}) collective-permute-start(bf16[2,2,48,1664]{3,2,1,0:T(8,128)(2,1)} %collective-permute-done.6.l1), channel_id=1, source_target_pairs={{0,64},{1,65},{2,66},{3,67},{4,68},{5,69},{6,70},{7,71},{8,72},{9,... | collective-permute-start | bytes 1916936 | tf_op jit(solution)/shard_map/ppermute | solution.py:36
  75.3 14.8 %all-to-all-start.1 = ((bf16[32,4,896]{2,1,0:T(4,128)(2,1)}), bf16[32,4,896]{2,1,0:T(4,128)(2,1)S(1)}, u32[]{:S(2)}, u32[]{:S(2)}) async-start(bf16[32,4,896]{2,1,0:T(4,128)(2,1)} %get-tuple-element.24), calls=%async_computation.1 | async-start | bytes 458752 | tf_op jit(solution)/shard_map/all_to_all | solution.py:661
  89.6 1.6 %collective-permute-start.16 = (f32[4,768]{1,0:T(4,128)}, f32[4,768]{1,0:T(4,128)S(1)}, u32[]{:S(2)}, u32[]{:S(2)}) collective-permute-start(f32[4,768]{1,0:T(4,128)} %get-tuple-element.27.own_ref), channel_id=1, source_target_pairs={{0,64},{1,65},{2,66},{3,67},{4,68},{5,69},{6,70},{7,71},{8,72},{9,... | collective-permute-start | bytes 36872 | tf_op jit(solution)/shard_map/ppermute | solution.py:36
  91.2 0.6 copy-start.9
  91.8 13.1 %copy-start.5 = (f32[4,768]{1,0:T(4,128)S(1)}, f32[4,768]{1,0:T(4,128)}, u32[]{:S(2)}) copy-start(f32[4,768]{1,0:T(4,128)} %slice_divide_fusion.means_ref) | copy-start | bytes 36868
  101.5 3.3 %collective-permute-start.17 = (bf16[5,3072]{1,0:T(8,128)(2,1)}, bf16[5,3072]{1,0:T(8,128)(2,1)S(1)}, u32[]{:S(2)}, u32[]{:S(2)}) collective-permute-start(bf16[5,3072]{1,0:T(8,128)(2,1)} %get-tuple-element.34), channel_id=1, source_target_pairs={{0,1},{1,0},{2,3},{3,2},{4,5},{5,4},{6,7},{7,6},{8,9},{9,8},{10,11... | collective-permute-start | bytes 92168 | tf_op jit(solution)/shard_map/ppermute | solution.py:36
  101.9 7.9 %collective-permute-start.20 = (bf16[5,3072]{1,0:T(8,128)(2,1)}, bf16[5,3072]{1,0:T(8,128)(2,1)S(1)}, u32[]{:S(2)}, u32[]{:S(2)}) collective-permute-start(bf16[5,3072]{1,0:T(8,128)(2,1)} %get-tuple-element.38), channel_id=1, source_target_pairs={{0,3},{1,2},{2,1},{3,0},{4,7},{5,6},{6,5},{7,4},{8,11},{9,10},{10,... | collective-permute-start | bytes 92168 | tf_op jit(solution)/shard_map/ppermute | solution.py:36
  102.7 7.2 %collective-permute-start.21 = (bf16[5,3072]{1,0:T(8,128)(2,1)}, bf16[5,3072]{1,0:T(8,128)(2,1)S(1)}, u32[]{:S(2)}, u32[]{:S(2)}) collective-permute-start(bf16[5,3072]{1,0:T(8,128)(2,1)} %get-tuple-element.39), channel_id=1, source_target_pairs={{0,2},{1,3},{2,0},{3,1},{4,6},{5,7},{6,4},{7,5},{8,10},{9,11},{10,... | collective-permute-start | bytes 92168 | tf_op jit(solution)/shard_map/ppermute | solution.py:36
  104.9 6.4 %collective-permute-start.18 = (f32[1,768]{1,0:T(1,128)S(1)}, f32[1,768]{1,0:T(1,128)S(1)}, u32[]{:S(2)}, u32[]{:S(2)}) collective-permute-start(f32[1,768]{1,0:T(1,128)S(1)} %get-tuple-element.50), channel_id=1, source_target_pairs={{0,0},{1,1},{2,64},{3,65},{4,4},{5,5},{6,68},{7,69},{8,8},{9,9},{1... | collective-permute-start | bytes 9224 | tf_op jit(solution)/shard_map/ppermute | solution.py:36
  108.5 4.3 %collective-permute-start.19 = (f32[1,768]{1,0:T(1,128)S(1)}, f32[1,768]{1,0:T(1,128)S(1)}, u32[]{:S(2)}, u32[]{:S(2)}) collective-permute-start(f32[1,768]{1,0:T(1,128)S(1)} %get-tuple-element.51), channel_id=1, source_target_pairs={{0,1},{1,0},{2,65},{3,64},{4,5},{5,4},{6,69},{7,68},{8,9},{9,8},{1... | collective-permute-start | bytes 9224 | tf_op jit(solution)/shard_map/ppermute | solution.py:36
  110.7 2.8 %collective-permute-start.22 = (f32[5,3072]{1,0:T(8,128)S(1)}, f32[5,3072]{1,0:T(8,128)S(1)}, u32[]{:S(2)}, u32[]{:S(2)}) collective-permute-start(f32[5,3072]{1,0:T(8,128)S(1)} %convert_add_fusion), channel_id=1, source_target_pairs={{0,64},{1,65},{2,66},{3,67},{4,68},{5,69},{6,70},{7,71},{8,72},{9,... | collective-permute-start | bytes 184328 | tf_op jit(solution)/shard_map/ppermute | solution.py:36

commit v5 on v4

--- a/solution.py
+++ b/solution.py
@@ -11,7 +11,7 @@
 D = 768
 PIXELS = 3072
 IPC = 10
-SYN_AT = PIXELS + 128
+SYN_AT = PIXELS
 SLOT = 6
 SYN = 4 * SLOT
 BLOCK_ROWS = 48
@@ -188,7 +188,7 @@
 def real_kernel(
     where_ref, mine_ref, theirs_ref, images_ref, l0, l1, l2, l3, o0, o1, o2, o3,
     csum_ref, w_out, wp_out,
-    e_ref, n_ref, qkv_ref, att_ref, feat_ref, hot_ref, x_ref, posx_ref, w_ref, wp_ref, sems,
+    e_ref, n_ref, qkv_ref, att_ref, feat_ref, tag_ref, x_ref, posx_ref, w_ref, wp_ref, sems,
 ):
     tiles = STEP // 8
     groups = REAL // STEP
@@ -197,6 +197,11 @@
     for k in range(4):
         pltpu.make_async_copy(
             images_ref.at[k, :, :SYN_AT], x_ref.at[32 * k : 32 * k + 32], sems.at[1]
+        ).start()
+        pltpu.make_async_copy(
+            images_ref.at[k, 16:32, SYN_AT : SYN_AT + 128],
+            tag_ref.at[16 * k : 16 * k + 16],
+            sems.at[5],
         ).start()
     near_block = ((0, 0), (0, 1), (1, 0), (1, 1))
     far_block = ((2, 0), (3, 0), (2, 1), (3, 1))
@@ -218,9 +223,12 @@
                     ).start()
     wp_ref[...] = jnp.zeros_like(wp_ref)
     spread_position(where_ref, mine_ref, theirs_ref, posx_ref)
-    cls = lax.broadcasted_iota(jnp.int32, (REAL, 128), 1).astype(F32)
+    cls = lax.broadcasted_iota(jnp.int32, (128, REAL), 0).astype(F32)
     pltpu.make_async_copy(x_ref, x_ref, sems.at[1]).wait()
-    hot_ref[...] = jnp.where(x_ref[:, PIXELS:].astype(F32) == cls, 1.0, 0.0).astype(BF)
+    pltpu.make_async_copy(tag_ref, tag_ref, sems.at[5]).wait()
+    tags = tag_ref[...].astype(F32)
+    index = tags[14:15] + tags[30:31] + tags[46:47] + tags[62:63]
+    hot = jnp.where(cls == index, 1.0, 0.0).astype(BF)
     feat_ref[:, D:] = jnp.ones((REAL, 128), BF)
     patch_cols = w_ref.at[:, : 2 * 128]
     pltpu.make_async_copy(patch_cols, patch_cols, sems.at[0]).wait()
@@ -281,7 +289,7 @@
         feat_ref[pl.ds(at, STEP), :D] = jnp.concatenate(feats, axis=0).astype(BF)
 
     loop(groups, group)
-    sums = dot_tn(hot_ref[...], feat_ref[...])
+    sums = dot(hot, feat_ref[...])
     for b in range(16):
         block = sums[4 * b : 4 * b + 4].astype(csum_ref.dtype)
         csum_ref[b] = block
@@ -520,12 +528,12 @@
             buffer((rows, 3 * D), BF),
             buffer((rows, D), BF),
             buffer((REAL, D + 128), BF),
-            buffer((REAL, 128), BF),
-            buffer((REAL, PIXELS + 128), BF),
+            buffer((64, 128), BF),
+            buffer((REAL, PIXELS), BF),
             buffer((128, D), F32),
             buffer((D, 2 * COLS), BF),
             buffer((2, 256, D), BF),
-            pltpu.SemaphoreType.DMA((5,)),
+            pltpu.SemaphoreType.DMA((6,)),
         ],
         compiler_params=pltpu.CompilerParams(vmem_limit_bytes=VMEM_LIMIT),
         cost_estimate=pl.CostEstimate(
@@ -639,13 +647,12 @@
 
     hit = real_labels[:, None] == class_ids[None, :]
     index = jnp.sum(jnp.where(hit, jnp.arange(64, dtype=F32)[None, :], 0.0), axis=1)
-    tagged = jnp.concatenate(
-        [real_images, jnp.broadcast_to(index[:, None], (64, 128)).astype(BF)], axis=1
-    )
+    tag = jnp.tile(lax.dynamic_slice_in_dim(index, 32 * core, 32, 0), 4)
+    tag = jnp.pad(jnp.where(jnp.arange(128) // 32 == x, tag, 0.0).astype(BF), (0, 384))
     syn = lax.dynamic_slice_in_dim(synthetic, 5 * core, 5, 0).astype(BF).reshape(30, 512)
+    syn = jnp.concatenate([syn, tag[None], jnp.zeros((1, 512), BF)], axis=0)
     images = jnp.concatenate(
-        [lax.dynamic_slice_in_dim(tagged, 32 * core, 32, 0), jnp.pad(syn, ((0, 2), (0, 0)))],
-        axis=1,
+        [lax.dynamic_slice_in_dim(real_images, 32 * core, 32, 0), syn], axis=1
     )
     rings = [[flat(c, yz // 4, yz % 4, xx) for xx in range(4)] for c in range(2) for yz in range(16)]
     images = lax.all_to_all(

time: 115 us -> 115 us (level)
  transfers between devices with their start and end apart: 25 -> 25, of which waited for: 11 -> 11; matrix products, arithmetic and copies ran while one was open for 4% -> 5% of each run, Pallas kernels for 8% -> 8%
where the time goes in v5:
time: 115 us; the launch traced here: 114 us
  Pallas kernels  41.2 us (36%)
  starting transfers between devices  37.4 us (33%)
  waiting for transfers between devices  24.9 us (22%)
  other arithmetic  5.31 us (5%)
  local copies, waits for them, and re-layouts  3.96 us (3%)
  between operations  1.28 us (1%)
    ppermute x23, starting transfers between devices, permute(): lax.ppermute(a, AXES, [(flat(*p), flat(*target(*p))) for p in PLACES])  28.6 us
    pallas_call x1, Pallas kernels, run_real(): pl.pallas_call(real_kernel, in_specs=[SMEM_SPEC, VMEM_SPEC, VMEM_SPEC] +...  22.5 us
    ppermute x23, waiting for transfers between devices, permute(): lax.ppermute(a, AXES, [(flat(*p), flat(*target(*p))) for p in PLACES])  13.9 us
    all_to_all x1, waiting for transfers between devices, local(): lax.all_to_all(jnp.broadcast_to(images[None], (4, 32, SYN_AT + 512)), AXE...  11 us
    pallas_call x1, Pallas kernels, run_back(): pl.pallas_call(back_kernel, in_specs=[SMEM_SPEC] + [VMEM_SPEC] * 3 + [ANY...  9.78 us
    pallas_call x1, Pallas kernels, run_synth(): pl.pallas_call(synth_kernel, in_specs=[SMEM_SPEC, VMEM_SPEC, VMEM_SPEC] +...  8.93 us
    all_to_all x1, starting transfers between devices, local(): got = lax.all_to_all(csum, AXES, 0, 0, axis_index_groups=groups)  5.34 us
    all_to_all x1, starting transfers between devices, local(): lax.all_to_all(jnp.broadcast_to(images[None], (4, 32, SYN_AT + 512)), AXE...  3.5 us
  transfers between devices with their start and end apart: 25, of which 11 were waited for; matrix products, arithmetic and copies ran while one was open for 5% of the time, Pallas kernels for 8%

profile of v5, /device:TPU:1, one launch (start us, length us, event | category | flops | bytes accessed | tf_op | source)
XLA Modules:
  0.0 114.1 jit_solution(10551054399465010130)
XLA Ops:
  0.9 0.7 reshape.27
  1.6 1.1 pad_maximum_fusion.5
  2.8 0.1 maximum_bitcast_fusion
  3.1 3.4 %collective-permute-start.3 = (bf16[12,1664]{1,0:T(8,128)(2,1)S(1)}, bf16[12,1664]{1,0:T(8,128)(2,1)S(1)}, u32[]{:S(2)}, u32[]{:S(2)}) collective-permute-start(bf16[12,1664]{1,0:T(8,128)(2,1)S(1)} %get-tuple-element.44), channel_id=1, source_target_pairs={{0,1},{1,64},{2,65},{3,0},{4,5},{5,68},{6,69},{7,4},{8,9},{9,72},{... | collective-permute-start | bytes 119816 | tf_op jit(solution)/shard_map/ppermute | solution.py:36
  6.4 2.7 %collective-permute-start.2 = (bf16[12,1664]{1,0:T(8,128)(2,1)S(1)}, bf16[12,1664]{1,0:T(8,128)(2,1)S(1)}, u32[]{:S(2)}, u32[]{:S(2)}) collective-permute-start(bf16[12,1664]{1,0:T(8,128)(2,1)S(1)} %get-tuple-element.45), channel_id=1, source_target_pairs={{0,64},{1,65},{2,0},{3,1},{4,68},{5,69},{6,4},{7,5},{8,72},{9,73},... | collective-permute-start | bytes 119816 | tf_op jit(solution)/shard_map/ppermute | solution.py:36
  9.2 1.2 %collective-permute-start.1 = (bf16[12,1664]{1,0:T(8,128)(2,1)S(1)}, bf16[12,1664]{1,0:T(8,128)(2,1)S(1)}, u32[]{:S(2)}, u32[]{:S(2)}) collective-permute-start(bf16[12,1664]{1,0:T(8,128)(2,1)S(1)} %get-tuple-element.46), channel_id=1, source_target_pairs={{0,65},{1,0},{2,1},{3,64},{4,69},{5,4},{6,5},{7,68},{8,73},{9,8},{... | collective-permute-start | bytes 119816 | tf_op jit(solution)/shard_map/ppermute | solution.py:36
  10.4 1.9 %collective-permute-start = (bf16[12,1664]{1,0:T(8,128)(2,1)S(1)}, bf16[12,1664]{1,0:T(8,128)(2,1)S(1)}, u32[]{:S(2)}, u32[]{:S(2)}) collective-permute-start(bf16[12,1664]{1,0:T(8,128)(2,1)S(1)} %get-tuple-element.47), channel_id=1, source_target_pairs={{0,0},{1,1},{2,64},{3,65},{4,4},{5,5},{6,68},{7,69},{8,8},{9,9},{1... | collective-permute-start | bytes 119816 | tf_op jit(solution)/shard_map/ppermute | solution.py:36
  12.3 0.9 dynamic-slice_convert_fusion
  13.3 0.2 select_reduce_fusion
  13.7 3.6 %collective-permute-done = bf16[12,1664]{1,0:T(8,128)(2,1)S(1)} collective-permute-done((bf16[12,1664]{1,0:T(8,128)(2,1)S(1)}, bf16[12,1664]{1,0:T(8,128)(2,1)S(1)}, u32[]{:S(2)}, u32[]{:S(2)}) %collective-permute-start) | collective-permute-done | bytes 39968 | tf_op jit(solution)/shard_map/ppermute | solution.py:36
  17.6 1.7 %collective-permute-start.9 = (bf16[48,1664]{1,0:T(8,128)(2,1)S(1)}, bf16[48,1664]{1,0:T(8,128)(2,1)S(1)}, u32[]{:S(2)}, u32[]{:S(2)}) collective-permute-start(bf16[48,1664]{1,0:T(8,128)(2,1)S(1)} %reshape.30), channel_id=1, source_target_pairs={{0,16},{1,17},{2,18},{3,19},{4,20},{5,21},{6,22},{7,23},{8,24},{9,... | collective-permute-start | bytes 479240 | tf_op jit(solution)/shard_map/ppermute | solution.py:36
  19.3 3.3 %collective-permute-start.8 = (bf16[48,1664]{1,0:T(8,128)(2,1)S(1)}, bf16[48,1664]{1,0:T(8,128)(2,1)S(1)}, u32[]{:S(2)}, u32[]{:S(2)}) collective-permute-start(bf16[48,1664]{1,0:T(8,128)(2,1)S(1)} %reshape.30), channel_id=1, source_target_pairs={{0,32},{1,33},{2,34},{3,35},{4,36},{5,37},{6,38},{7,39},{8,40},{9,... | collective-permute-start | bytes 479240 | tf_op jit(solution)/shard_map/ppermute | solution.py:36
  22.7 0.8 collective-permute-start.4
  23.5 0.6 collective-permute-done.9
  24.1 2.9 %collective-permute-done.8 = bf16[48,1664]{1,0:T(8,128)(2,1)S(1)} collective-permute-done((bf16[48,1664]{1,0:T(8,128)(2,1)S(1)}, bf16[48,1664]{1,0:T(8,128)(2,1)S(1)}, u32[]{:S(2)}, u32[]{:S(2)}) %collective-permute-start.8) | collective-permute-done | bytes 159776 | tf_op jit(solution)/shard_map/ppermute | solution.py:36
  27.0 2.9 %collective-permute-start.10 = (bf16[2,48,1664]{2,1,0:T(8,128)(2,1)S(1)}, bf16[2,48,1664]{2,1,0:T(8,128)(2,1)S(1)}, u32[]{:S(2)}, u32[]{:S(2)}) collective-permute-start(bf16[2,48,1664]{2,1,0:T(8,128)(2,1)S(1)} %get-tuple-element.41), channel_id=1, source_target_pairs={{0,12},{1,13},{2,14},{3,15},{4,8},{5,9},{6,10},{7,11},{8,4},{9,5},... | collective-permute-start | bytes 958472 | tf_op jit(solution)/shard_map/ppermute | solution.py:36
  30.1 1.0 broadcast_in_dim.36
  31.1 3.5 %all-to-all-start = ((bf16[4,32,3584]{2,1,0:T(8,128)(2,1)}), bf16[4,32,3584]{2,1,0:T(8,128)(2,1)S(1)}, u32[]{:S(2)}, u32[]{:S(2)}) async-start(bf16[4,32,3584]{2,1,0:T(8,128)(2,1)} %broadcast_in_dim.36), calls=%async_computation | async-start | bytes 1835008 | tf_op jit(solution)/shard_map/all_to_all | solution.py:658
  34.6 1.2 %collective-permute-done.5 = bf16[2,48,1664]{2,1,0:T(8,128)(2,1)S(1)} collective-permute-done((bf16[2,48,1664]{2,1,0:T(8,128)(2,1)S(1)}, bf16[2,48,1664]{2,1,0:T(8,128)(2,1)S(1)}, u32[]{:S(2)}, u32[]{:S(2)}) %collective-permute-start.5) | collective-permute-done | bytes 319520 | tf_op jit(solution)/shard_map/ppermute | solution.py:36
  36.2 0.3 collective-permute-start.11
  36.5 0.5 collective-permute-start.12
  37.0 0.7 collective-permute-done.7.theirs_ref
  37.7 11.0 %all-to-all-done.images_ref = bf16[4,32,3584]{2,1,0:T(8,128)(2,1)S(1)} async-done(((bf16[4,32,3584]{2,1,0:T(8,128)(2,1)}), bf16[4,32,3584]{2,1,0:T(8,128)(2,1)S(1)}, u32[]{:S(2)}, u32[]{:S(2)}) %all-to-all-start) | async-done | bytes 917536 | tf_op jit(solution)/shard_map/all_to_all | solution.py:658
  48.8 0.5 collective-permute-start.15
  49.2 0.3 collective-permute-start.13
  49.5 0.6 pad_add_fusion.where_ref
  50.1 1.0 collective-permute-done.15.o3
  51.1 1.1 collective-permute-done.13.o1
  52.2 22.5 %real_forward.1 = (bf16[32,4,896]{2,1,0:T(4,128)(2,1)}, bf16[768,3328]{1,0:T(8,128)(2,1)}, bf16[2,256,768]{2,1,0:T(8,128)(2,1)}) custom-call(s32[4]{0:T(128)} %pad_add_fusion.where_ref, bf16[2,16,768]{2,1,0:T(8,128)(2,1)} %mine_ref.3, bf16[2,16,768]{2,1,0:T(8,128)(2,1)} %copy-done.7, bf16[4,32,3584]{2,1,0:T(8,128)(2,1)} %copy-done.1, ...), custom_call_target="tpu_custom_call" | custom-call | flops 14000000000 | bytes 12000000 | tf_op jit(solution)/shard_map/real_forward/pallas_call | solution.py:516
  74.7 5.3 %all-to-all-start.1 = ((bf16[32,4,896]{2,1,0:T(4,128)(2,1)}), bf16[32,4,896]{2,1,0:T(4,128)(2,1)S(1)}, u32[]{:S(2)}, u32[]{:S(2)}) async-start(bf16[32,4,896]{2,1,0:T(4,128)(2,1)} %get-tuple-element.24), calls=%async_computation.1 | async-start | bytes 458752 | tf_op jit(solution)/shard_map/all_to_all | solution.py:668
  80.1 8.9 %synth_forward.1 = (f32[4,768]{1,0:T(4,128)}, bf16[384,768]{1,0:T(8,128)(2,1)}, f32[384,128]{1,0:T(8,128)}, bf16[384,2304]{1,0:T(8,128)(2,1)}, bf16[384,1536]{1,...) custom-call(s32[4]{0:T(128)} %pad_add_fusion.where_ref, bf16[2,16,768]{2,1,0:T(8,128)(2,1)} %mine_ref.3, ...), custom_call_target="tpu_custom_call" | custom-call | flops 3000000000 | bytes 12000000 | tf_op jit(solution)/shard_map/synth_forward/pallas_call | solution.py:559
  89.0 0.5 collective-permute-start.16
  89.5 0.1 convert_reduce_fusion
  89.7 0.1 fusion.2
  89.8 0.7 slice_divide_fusion.means_ref
  90.5 0.1 collective-permute-done.16.their_ref
  90.6 0.6 copy-done.8
  91.2 9.8 %synth_backward.1 = (bf16[5,3072]{1,0:T(8,128)(2,1)}, bf16[5,3072]{1,0:T(8,128)(2,1)}, bf16[5,3072]{1,0:T(8,128)(2,1)}, bf16[5,3072]{1,0:T(8,128)(2,1)}) custom-call(s32[4]{0:T(128)} %pad_add_fusion.where_ref, f32[4,768]{1,0:T(4,128)} %slice_divide_fusion.means_ref, f32[4,768]{1,0:T(4,128)} %get-tuple-element.27.own_ref, f32[4,768]{1,0:T(4,128)} %copy-done.8, ...), custom_call_target="tpu_custom_call" | custom-call | flops 4000000000 | bytes 12000000 | tf_op jit(solution)/shard_map/synth_backward/pallas_call | solution.py:585
  101.0 0.4 collective-permute-start.17
  101.3 0.9 collective-permute-start.20
  102.3 2.0 %collective-permute-start.21 = (bf16[5,3072]{1,0:T(8,128)(2,1)}, bf16[5,3072]{1,0:T(8,128)(2,1)S(1)}, u32[]{:S(2)}, u32[]{:S(2)}) collective-permute-start(bf16[5,3072]{1,0:T(8,128)(2,1)} %get-tuple-element.39), channel_id=1, source_target_pairs={{0,2},{1,3},{2,0},{3,1},{4,6},{5,7},{6,4},{7,5},{8,10},{9,11},{10,... | collective-permute-start | bytes 92168 | tf_op jit(solution)/shard_map/ppermute | solution.py:36
  104.3 4.1 %collective-permute-start.18 = (f32[1,768]{1,0:T(1,128)S(1)}, f32[1,768]{1,0:T(1,128)S(1)}, u32[]{:S(2)}, u32[]{:S(2)}) collective-permute-start(f32[1,768]{1,0:T(1,128)S(1)} %get-tuple-element.50), channel_id=1, source_target_pairs={{0,0},{1,1},{2,64},{3,65},{4,4},{5,5},{6,68},{7,69},{8,8},{9,9},{1... | collective-permute-start | bytes 9224 | tf_op jit(solution)/shard_map/ppermute | solution.py:36
  108.5 0.8 collective-permute-start.19
  109.3 0.8 convert_add_fusion
  110.2 0.5 collective-permute-done.18
  110.8 2.0 %collective-permute-done.19 = f32[1,768]{1,0:T(1,128)S(1)} collective-permute-done((f32[1,768]{1,0:T(1,128)S(1)}, f32[1,768]{1,0:T(1,128)S(1)}, u32[]{:S(2)}, u32[]{:S(2)}) %collective-permute-start.19) | collective-permute-done | bytes 3104 | tf_op jit(solution)/shard_map/ppermute | solution.py:36
  112.8 0.6 pad_maximum_fusion.6
  113.4 0.7 pad_maximum_fusion.4
  (73 shorter events, 1.3 us)
Async XLA Ops:
  0.6 12.7 %copy-start = (bf16[64,3072]{1,0:T(8,128)(2,1)S(1)}, bf16[64,3072]{1,0:T(8,128)(2,1)}, u32[]{:S(2)}) copy-start(bf16[64,3072]{1,0:T(8,128)(2,1)} %param.8) | copy-start | bytes 1179652
  0.6 12.7 %copy-start.9 = (s32[64]{0:T(128)S(1)}, s32[64]{0:T(128)}, u32[]{:S(2)}) copy-start(s32[64]{0:T(128)} %param.10) | copy-start | bytes 772
  0.7 12.7 %copy-start.10 = (s32[64]{0:T(128)S(1)}, s32[64]{0:T(128)}, u32[]{:S(2)}) copy-start(s32[64]{0:T(128)} %param.9) | copy-start | bytes 772
  3.1 14.4 %collective-permute-start.3 = (bf16[12,1664]{1,0:T(8,128)(2,1)S(1)}, bf16[12,1664]{1,0:T(8,128)(2,1)S(1)}, u32[]{:S(2)}, u32[]{:S(2)}) collective-permute-start(bf16[12,1664]{1,0:T(8,128)(2,1)S(1)} %get-tuple-element.44), channel_id=1, source_target_pairs={{0,1},{1,64},{2,65},{3,0},{4,5},{5,68},{6,69},{7,4},{8,9},{9,72},{... | collective-permute-start | bytes 119816 | tf_op jit(solution)/shard_map/ppermute | solution.py:36
  6.4 10.9 %collective-permute-start.2 = (bf16[12,1664]{1,0:T(8,128)(2,1)S(1)}, bf16[12,1664]{1,0:T(8,128)(2,1)S(1)}, u32[]{:S(2)}, u32[]{:S(2)}) collective-permute-start(bf16[12,1664]{1,0:T(8,128)(2,1)S(1)} %get-tuple-element.45), channel_id=1, source_target_pairs={{0,64},{1,65},{2,0},{3,1},{4,68},{5,69},{6,4},{7,5},{8,72},{9,73},... | collective-permute-start | bytes 119816 | tf_op jit(solution)/shard_map/ppermute | solution.py:36
  9.2 8.2 %collective-permute-start.1 = (bf16[12,1664]{1,0:T(8,128)(2,1)S(1)}, bf16[12,1664]{1,0:T(8,128)(2,1)S(1)}, u32[]{:S(2)}, u32[]{:S(2)}) collective-permute-start(bf16[12,1664]{1,0:T(8,128)(2,1)S(1)} %get-tuple-element.46), channel_id=1, source_target_pairs={{0,65},{1,0},{2,1},{3,64},{4,69},{5,4},{6,5},{7,68},{8,73},{9,8},{... | collective-permute-start | bytes 119816 | tf_op jit(solution)/shard_map/ppermute | solution.py:36
  10.4 6.9 %collective-permute-start = (bf16[12,1664]{1,0:T(8,128)(2,1)S(1)}, bf16[12,1664]{1,0:T(8,128)(2,1)S(1)}, u32[]{:S(2)}, u32[]{:S(2)}) collective-permute-start(bf16[12,1664]{1,0:T(8,128)(2,1)S(1)} %get-tuple-element.47), channel_id=1, source_target_pairs={{0,0},{1,1},{2,64},{3,65},{4,4},{5,5},{6,68},{7,69},{8,8},{9,9},{1... | collective-permute-start | bytes 119816 | tf_op jit(solution)/shard_map/ppermute | solution.py:36
  17.6 6.5 %collective-permute-start.9 = (bf16[48,1664]{1,0:T(8,128)(2,1)S(1)}, bf16[48,1664]{1,0:T(8,128)(2,1)S(1)}, u32[]{:S(2)}, u32[]{:S(2)}) collective-permute-start(bf16[48,1664]{1,0:T(8,128)(2,1)S(1)} %reshape.30), channel_id=1, source_target_pairs={{0,16},{1,17},{2,18},{3,19},{4,20},{5,21},{6,22},{7,23},{8,24},{9,... | collective-permute-start | bytes 479240 | tf_op jit(solution)/shard_map/ppermute | solution.py:36
  19.3 7.7 %collective-permute-start.8 = (bf16[48,1664]{1,0:T(8,128)(2,1)S(1)}, bf16[48,1664]{1,0:T(8,128)(2,1)S(1)}, u32[]{:S(2)}, u32[]{:S(2)}) collective-permute-start(bf16[48,1664]{1,0:T(8,128)(2,1)S(1)} %reshape.30), channel_id=1, source_target_pairs={{0,32},{1,33},{2,34},{3,35},{4,36},{5,37},{6,38},{7,39},{8,40},{9,... | collective-permute-start | bytes 479240 | tf_op jit(solution)/shard_map/ppermute | solution.py:36
  22.7 7.2 %collective-permute-start.4 = (bf16[48,1664]{1,0:T(8,128)(2,1)S(1)}, bf16[48,1664]{1,0:T(8,128)(2,1)S(1)}, u32[]{:S(2)}, u32[]{:S(2)}) collective-permute-start(bf16[48,1664]{1,0:T(8,128)(2,1)S(1)} %reshape.30), channel_id=1, source_target_pairs={{0,48},{1,49},{2,50},{3,51},{4,52},{5,53},{6,54},{7,55},{8,56},{9,... | collective-permute-start | bytes 479240 | tf_op jit(solution)/shard_map/ppermute | solution.py:36
  27.0 9.1 %collective-permute-start.10 = (bf16[2,48,1664]{2,1,0:T(8,128)(2,1)S(1)}, bf16[2,48,1664]{2,1,0:T(8,128)(2,1)S(1)}, u32[]{:S(2)}, u32[]{:S(2)}) collective-permute-start(bf16[2,48,1664]{2,1,0:T(8,128)(2,1)S(1)} %get-tuple-element.41), channel_id=1, source_target_pairs={{0,12},{1,13},{2,14},{3,15},{4,8},{5,9},{6,10},{7,11},{8,4},{9,5},... | collective-permute-start | bytes 958472 | tf_op jit(solution)/shard_map/ppermute | solution.py:36
  30.0 5.9 %collective-permute-start.5 = (bf16[2,48,1664]{2,1,0:T(8,128)(2,1)S(1)}, bf16[2,48,1664]{2,1,0:T(8,128)(2,1)S(1)}, u32[]{:S(2)}, u32[]{:S(2)}) collective-permute-start(bf16[2,48,1664]{2,1,0:T(8,128)(2,1)S(1)} %get-tuple-element.43), channel_id=1, source_target_pairs={{0,4},{1,5},{2,6},{3,7},{4,0},{5,1},{6,2},{7,3},{8,12},{9,13},{10,... | collective-permute-start | bytes 958472 | tf_op jit(solution)/shard_map/ppermute | solution.py:36
  31.1 17.6 %all-to-all-start = ((bf16[4,32,3584]{2,1,0:T(8,128)(2,1)}), bf16[4,32,3584]{2,1,0:T(8,128)(2,1)S(1)}, u32[]{:S(2)}, u32[]{:S(2)}) async-start(bf16[4,32,3584]{2,1,0:T(8,128)(2,1)} %broadcast_in_dim.36), calls=%async_computation | async-start | bytes 1835008 | tf_op jit(solution)/shard_map/all_to_all | solution.py:658
  34.6 1.8 %copy-start.6 = (bf16[2,16,768]{2,1,0:T(8,128)(2,1)S(1)}, bf16[2,16,768]{2,1,0:T(8,128)(2,1)}, u32[]{:S(2)}) copy-start(bf16[2,16,768]{2,1,0:T(8,128)(2,1)} %mine_ref.3) | copy-start | bytes 147460
  36.0 16.2 %copy-start.2 = (bf16[2,2,48,1664]{3,2,1,0:T(8,128)(2,1)}, bf16[2,2,48,1664]{3,2,1,0:T(8,128)(2,1)S(1)}, u32[]{:S(2)}) copy-start(bf16[2,2,48,1664]{3,2,1,0:T(8,128)(2,1)S(1)} %pad_maximum_fusion.l0) | copy-start | bytes 1916932
  36.0 12.8 %collective-permute-start.6 = (bf16[2,2,48,1664]{3,2,1,0:T(8,128)(2,1)S(1)}, bf16[2,2,48,1664]{3,2,1,0:T(8,128)(2,1)}, u32[]{:S(2)}, u32[]{:S(2)}) collective-permute-start(bf16[2,2,48,1664]{3,2,1,0:T(8,128)(2,1)S(1)} %pad_maximum_fusion.l0), channel_id=1, source_target_pairs={{0,12},{1,13},{2,14},{3,15},{4,8},{5,9},{6,10},{7,11},{8,4},{9,5},... | collective-permute-start | bytes 1916936 | tf_op jit(solution)/shard_map/ppermute | solution.py:36
  36.2 16.0 %copy-start.3 = (bf16[2,2,48,1664]{3,2,1,0:T(8,128)(2,1)}, bf16[2,2,48,1664]{3,2,1,0:T(8,128)(2,1)S(1)}, u32[]{:S(2)}) copy-start(bf16[2,2,48,1664]{3,2,1,0:T(8,128)(2,1)S(1)} %pad_maximum_fusion.1.l2) | copy-start | bytes 1916932
  36.2 12.6 %collective-permute-start.11 = (bf16[2,2,48,1664]{3,2,1,0:T(8,128)(2,1)S(1)}, bf16[2,2,48,1664]{3,2,1,0:T(8,128)(2,1)S(1)}, u32[]{:S(2)}, u32[]{:S(2)}) collective-permute-start(bf16[2,2,48,1664]{3,2,1,0:T(8,128)(2,1)S(1)} %pad_maximum_fusion.1.l2), channel_id=1, source_target_pairs={{0,4},{1,5},{2,6},{3,7},{4,0},{5,1},{6,2},{7,3},{8,12},{9,13},{10,... | collective-permute-start | bytes 1916936 | tf_op jit(solution)/shard_map/ppermute | solution.py:36
  36.5 1.3 %collective-permute-start.7 = (bf16[2,16,768]{2,1,0:T(8,128)(2,1)S(1)}, bf16[2,16,768]{2,1,0:T(8,128)(2,1)S(1)}, u32[]{:S(2)}, u32[]{:S(2)}) collective-permute-start(bf16[2,16,768]{2,1,0:T(8,128)(2,1)S(1)} %copy-done.6), channel_id=1, source_target_pairs={{0,64},{1,65},{2,66},{3,67},{4,68},{5,69},{6,70},{7,71},{8,72},{9,... | collective-permute-start | bytes 147464 | tf_op jit(solution)/shard_map/ppermute | solution.py:36
  36.5 13.6 %collective-permute-start.12 = (bf16[2,2,48,1664]{3,2,1,0:T(8,128)(2,1)S(1)}, bf16[2,2,48,1664]{3,2,1,0:T(8,128)(2,1)}, u32[]{:S(2)}, u32[]{:S(2)}) collective-permute-start(bf16[2,2,48,1664]{3,2,1,0:T(8,128)(2,1)S(1)} %pad_maximum_fusion.l0), channel_id=1, source_target_pairs={{0,64},{1,65},{2,66},{3,67},{4,68},{5,69},{6,70},{7,71},{8,72},{9,... | collective-permute-start | bytes 1916936 | tf_op jit(solution)/shard_map/ppermute | solution.py:36
  37.0 13.1 %collective-permute-start.14 = (bf16[2,2,48,1664]{3,2,1,0:T(8,128)(2,1)S(1)}, bf16[2,2,48,1664]{3,2,1,0:T(8,128)(2,1)}, u32[]{:S(2)}, u32[]{:S(2)}) collective-permute-start(bf16[2,2,48,1664]{3,2,1,0:T(8,128)(2,1)S(1)} %pad_maximum_fusion.1.l2), channel_id=1, source_target_pairs={{0,64},{1,65},{2,66},{3,67},{4,68},{5,69},{6,70},{7,71},{8,72},{9,... | collective-permute-start | bytes 1916936 | tf_op jit(solution)/shard_map/ppermute | solution.py:36
  37.7 14.5 %copy-start.7 = (bf16[2,16,768]{2,1,0:T(8,128)(2,1)}, bf16[2,16,768]{2,1,0:T(8,128)(2,1)S(1)}, u32[]{:S(2)}) copy-start(bf16[2,16,768]{2,1,0:T(8,128)(2,1)S(1)} %collective-permute-done.7.theirs_ref) | copy-start | bytes 147460
  48.7 3.5 %copy-start.1 = (bf16[4,32,3584]{2,1,0:T(8,128)(2,1)}, bf16[4,32,3584]{2,1,0:T(8,128)(2,1)S(1)}, u32[]{:S(2)}) copy-start(bf16[4,32,3584]{2,1,0:T(8,128)(2,1)S(1)} %all-to-all-done.images_ref) | copy-start | bytes 2752516
  48.7 3.5 %copy-start.5 = (bf16[2,2,48,1664]{3,2,1,0:T(8,128)(2,1)}, bf16[2,2,48,1664]{3,2,1,0:T(8,128)(2,1)S(1)}, u32[]{:S(2)}) copy-start(bf16[2,2,48,1664]{3,2,1,0:T(8,128)(2,1)S(1)} %collective-permute-done.11.l3) | copy-start | bytes 1916932
  48.8 2.3 %collective-permute-start.15 = (bf16[2,2,48,1664]{3,2,1,0:T(8,128)(2,1)S(1)}, bf16[2,2,48,1664]{3,2,1,0:T(8,128)(2,1)}, u32[]{:S(2)}, u32[]{:S(2)}) collective-permute-start(bf16[2,2,48,1664]{3,2,1,0:T(8,128)(2,1)S(1)} %collective-permute-done.11.l3), channel_id=1, source_target_pairs={{0,64},{1,65},{2,66},{3,67},{4,68},{5,69},{6,70},{7,71},{8,72},{9,... | collective-permute-start | bytes 1916936 | tf_op jit(solution)/shard_map/ppermute | solution.py:36
  49.2 3.0 %collective-permute-start.13 = (bf16[2,2,48,1664]{3,2,1,0:T(8,128)(2,1)}, bf16[2,2,48,1664]{3,2,1,0:T(8,128)(2,1)}, u32[]{:S(2)}, u32[]{:S(2)}) collective-permute-start(bf16[2,2,48,1664]{3,2,1,0:T(8,128)(2,1)} %collective-permute-done.6.l1), channel_id=1, source_target_pairs={{0,64},{1,65},{2,66},{3,67},{4,68},{5,69},{6,70},{7,71},{8,72},{9,... | collective-permute-start | bytes 1916936 | tf_op jit(solution)/shard_map/ppermute | solution.py:36
  74.7 14.8 %all-to-all-start.1 = ((bf16[32,4,896]{2,1,0:T(4,128)(2,1)}), bf16[32,4,896]{2,1,0:T(4,128)(2,1)S(1)}, u32[]{:S(2)}, u32[]{:S(2)}) async-start(bf16[32,4,896]{2,1,0:T(4,128)(2,1)} %get-tuple-element.24), calls=%async_computation.1 | async-start | bytes 458752 | tf_op jit(solution)/shard_map/all_to_all | solution.py:668
  89.0 1.6 %collective-permute-start.16 = (f32[4,768]{1,0:T(4,128)}, f32[4,768]{1,0:T(4,128)S(1)}, u32[]{:S(2)}, u32[]{:S(2)}) collective-permute-start(f32[4,768]{1,0:T(4,128)} %get-tuple-element.27.own_ref), channel_id=1, source_target_pairs={{0,64},{1,65},{2,66},{3,67},{4,68},{5,69},{6,70},{7,71},{8,72},{9,... | collective-permute-start | bytes 36872 | tf_op jit(solution)/shard_map/ppermute | solution.py:36
  90.6 0.6 copy-start.8
  91.2 13.1 %copy-start.4 = (f32[4,768]{1,0:T(4,128)S(1)}, f32[4,768]{1,0:T(4,128)}, u32[]{:S(2)}) copy-start(f32[4,768]{1,0:T(4,128)} %slice_divide_fusion.means_ref) | copy-start | bytes 36868
  101.0 3.3 %collective-permute-start.17 = (bf16[5,3072]{1,0:T(8,128)(2,1)}, bf16[5,3072]{1,0:T(8,128)(2,1)S(1)}, u32[]{:S(2)}, u32[]{:S(2)}) collective-permute-start(bf16[5,3072]{1,0:T(8,128)(2,1)} %get-tuple-element.34), channel_id=1, source_target_pairs={{0,1},{1,0},{2,3},{3,2},{4,5},{5,4},{6,7},{7,6},{8,9},{9,8},{10,11... | collective-permute-start | bytes 92168 | tf_op jit(solution)/shard_map/ppermute | solution.py:36
  101.3 7.9 %collective-permute-start.20 = (bf16[5,3072]{1,0:T(8,128)(2,1)}, bf16[5,3072]{1,0:T(8,128)(2,1)S(1)}, u32[]{:S(2)}, u32[]{:S(2)}) collective-permute-start(bf16[5,3072]{1,0:T(8,128)(2,1)} %get-tuple-element.38), channel_id=1, source_target_pairs={{0,3},{1,2},{2,1},{3,0},{4,7},{5,6},{6,5},{7,4},{8,11},{9,10},{10,... | collective-permute-start | bytes 92168 | tf_op jit(solution)/shard_map/ppermute | solution.py:36
  102.3 7.0 %collective-permute-start.21 = (bf16[5,3072]{1,0:T(8,128)(2,1)}, bf16[5,3072]{1,0:T(8,128)(2,1)S(1)}, u32[]{:S(2)}, u32[]{:S(2)}) collective-permute-start(bf16[5,3072]{1,0:T(8,128)(2,1)} %get-tuple-element.39), channel_id=1, source_target_pairs={{0,2},{1,3},{2,0},{3,1},{4,6},{5,7},{6,4},{7,5},{8,10},{9,11},{10,... | collective-permute-start | bytes 92168 | tf_op jit(solution)/shard_map/ppermute | solution.py:36
  104.3 6.4 %collective-permute-start.18 = (f32[1,768]{1,0:T(1,128)S(1)}, f32[1,768]{1,0:T(1,128)S(1)}, u32[]{:S(2)}, u32[]{:S(2)}) collective-permute-start(f32[1,768]{1,0:T(1,128)S(1)} %get-tuple-element.50), channel_id=1, source_target_pairs={{0,0},{1,1},{2,64},{3,65},{4,4},{5,5},{6,68},{7,69},{8,8},{9,9},{1... | collective-permute-start | bytes 9224 | tf_op jit(solution)/shard_map/ppermute | solution.py:36
  108.5 4.3 %collective-permute-start.19 = (f32[1,768]{1,0:T(1,128)S(1)}, f32[1,768]{1,0:T(1,128)S(1)}, u32[]{:S(2)}, u32[]{:S(2)}) collective-permute-start(f32[1,768]{1,0:T(1,128)S(1)} %get-tuple-element.51), channel_id=1, source_target_pairs={{0,1},{1,0},{2,65},{3,64},{4,5},{5,4},{6,69},{7,68},{8,9},{9,8},{1... | collective-permute-start | bytes 9224 | tf_op jit(solution)/shard_map/ppermute | solution.py:36
  110.1 3.3 %collective-permute-start.22 = (f32[5,3072]{1,0:T(8,128)S(1)}, f32[5,3072]{1,0:T(8,128)S(1)}, u32[]{:S(2)}, u32[]{:S(2)}) collective-permute-start(f32[5,3072]{1,0:T(8,128)S(1)} %convert_add_fusion), channel_id=1, source_target_pairs={{0,64},{1,65},{2,66},{3,67},{4,68},{5,69},{6,70},{7,71},{8,72},{9,... | collective-permute-start | bytes 184328 | tf_op jit(solution)/shard_map/ppermute | solution.py:36

commit v6 on v5

--- a/solution.py
+++ b/solution.py
@@ -278,7 +278,7 @@
         at = (u % 6) * 128
         vbd = by_head(qkv_ref[rows, 2 * D + at : 2 * D + at + 128], low)
         o = dot(ex, jnp.concatenate([vbd, ones], axis=1))
-        att_ref[rows, at : at + 128] = (o[:, :128] / o[:, 128:]).astype(BF)
+        att_ref[rows, at : at + 128] = (o[:, :128] * pl.reciprocal(o[:, 128:])).astype(BF)
 
     def group(g):
         at = mult(g * STEP, STEP)
@@ -376,9 +376,9 @@
         xhat, rstd = normalise(e_ref[rows])
         xhat2_ref[rows] = xhat.astype(BF)
         r2_ref[rows] = jnp.broadcast_to(rstd, (128, 128))
+        pltpu.make_async_copy(xhat2_ref.at[rows], xhat2_out.at[rows], sems.at[4]).start()
+        pltpu.make_async_copy(r2_ref.at[rows], r2_out.at[rows], sems.at[5]).start()
         feats.append(patch_sum(xhat))
-    saves[4].start()
-    saves[5].start()
     feats = jnp.concatenate(feats, axis=0)
     for s in range(4):
         sum_ref[s : s + 1] = jnp.sum(feats[SLOT * s : SLOT * s + 5], axis=0, keepdims=True)

time: 115 us -> 115 us (level)
  no operation moved by 1% of the time
where the time goes in v6:
time: 115 us; the launch traced here: 114 us
  Pallas kernels  41.1 us (36%)
  starting transfers between devices  37.5 us (33%)
  waiting for transfers between devices  24.9 us (22%)
  other arithmetic  5.31 us (5%)
  local copies, waits for them, and re-layouts  3.96 us (3%)
  between operations  1.28 us (1%)
    ppermute x23, starting transfers between devices, permute(): lax.ppermute(a, AXES, [(flat(*p), flat(*target(*p))) for p in PLACES])  28.6 us
    pallas_call x1, Pallas kernels, run_real(): pl.pallas_call(real_kernel, in_specs=[SMEM_SPEC, VMEM_SPEC, VMEM_SPEC] +...  22.5 us
    ppermute x23, waiting for transfers between devices, permute(): lax.ppermute(a, AXES, [(flat(*p), flat(*target(*p))) for p in PLACES])  13.9 us
    all_to_all x1, waiting for transfers between devices, local(): lax.all_to_all(jnp.broadcast_to(images[None], (4, 32, SYN_AT + 512)), AXE...  11 us
    pallas_call x1, Pallas kernels, run_back(): pl.pallas_call(back_kernel, in_specs=[SMEM_SPEC] + [VMEM_SPEC] * 3 + [ANY...  9.76 us
    pallas_call x1, Pallas kernels, run_synth(): pl.pallas_call(synth_kernel, in_specs=[SMEM_SPEC, VMEM_SPEC, VMEM_SPEC] +...  8.84 us
    all_to_all x1, starting transfers between devices, local(): got = lax.all_to_all(csum, AXES, 0, 0, axis_index_groups=groups)  5.34 us
    all_to_all x1, starting transfers between devices, local(): lax.all_to_all(jnp.broadcast_to(images[None], (4, 32, SYN_AT + 512)), AXE...  3.5 us
  transfers between devices with their start and end apart: 25, of which 11 were waited for; matrix products, arithmetic and copies ran while one was open for 5% of the time, Pallas kernels for 8%

profile of v6, /device:TPU:1, one launch (start us, length us, event | category | flops | bytes accessed | tf_op | source)
XLA Modules:
  0.0 114.0 jit_solution(10444876417154297637)
XLA Ops:
  0.9 0.7 reshape.27
  1.6 1.1 pad_maximum_fusion.5
  2.8 0.1 maximum_bitcast_fusion
  3.1 3.4 %collective-permute-start.3 = (bf16[12,1664]{1,0:T(8,128)(2,1)S(1)}, bf16[12,1664]{1,0:T(8,128)(2,1)S(1)}, u32[]{:S(2)}, u32[]{:S(2)}) collective-permute-start(bf16[12,1664]{1,0:T(8,128)(2,1)S(1)} %get-tuple-element.44), channel_id=1, source_target_pairs={{0,1},{1,64},{2,65},{3,0},{4,5},{5,68},{6,69},{7,4},{8,9},{9,72},{... | collective-permute-start | bytes 119816 | tf_op jit(solution)/shard_map/ppermute | solution.py:36
  6.4 2.7 %collective-permute-start.2 = (bf16[12,1664]{1,0:T(8,128)(2,1)S(1)}, bf16[12,1664]{1,0:T(8,128)(2,1)S(1)}, u32[]{:S(2)}, u32[]{:S(2)}) collective-permute-start(bf16[12,1664]{1,0:T(8,128)(2,1)S(1)} %get-tuple-element.45), channel_id=1, source_target_pairs={{0,64},{1,65},{2,0},{3,1},{4,68},{5,69},{6,4},{7,5},{8,72},{9,73},... | collective-permute-start | bytes 119816 | tf_op jit(solution)/shard_map/ppermute | solution.py:36
  9.2 1.2 %collective-permute-start.1 = (bf16[12,1664]{1,0:T(8,128)(2,1)S(1)}, bf16[12,1664]{1,0:T(8,128)(2,1)S(1)}, u32[]{:S(2)}, u32[]{:S(2)}) collective-permute-start(bf16[12,1664]{1,0:T(8,128)(2,1)S(1)} %get-tuple-element.46), channel_id=1, source_target_pairs={{0,65},{1,0},{2,1},{3,64},{4,69},{5,4},{6,5},{7,68},{8,73},{9,8},{... | collective-permute-start | bytes 119816 | tf_op jit(solution)/shard_map/ppermute | solution.py:36
  10.4 1.9 %collective-permute-start = (bf16[12,1664]{1,0:T(8,128)(2,1)S(1)}, bf16[12,1664]{1,0:T(8,128)(2,1)S(1)}, u32[]{:S(2)}, u32[]{:S(2)}) collective-permute-start(bf16[12,1664]{1,0:T(8,128)(2,1)S(1)} %get-tuple-element.47), channel_id=1, source_target_pairs={{0,0},{1,1},{2,64},{3,65},{4,4},{5,5},{6,68},{7,69},{8,8},{9,9},{1... | collective-permute-start | bytes 119816 | tf_op jit(solution)/shard_map/ppermute | solution.py:36
  12.3 0.9 dynamic-slice_convert_fusion
  13.3 0.2 select_reduce_fusion
  13.7 3.6 %collective-permute-done = bf16[12,1664]{1,0:T(8,128)(2,1)S(1)} collective-permute-done((bf16[12,1664]{1,0:T(8,128)(2,1)S(1)}, bf16[12,1664]{1,0:T(8,128)(2,1)S(1)}, u32[]{:S(2)}, u32[]{:S(2)}) %collective-permute-start) | collective-permute-done | bytes 39968 | tf_op jit(solution)/shard_map/ppermute | solution.py:36
  17.6 1.7 %collective-permute-start.9 = (bf16[48,1664]{1,0:T(8,128)(2,1)S(1)}, bf16[48,1664]{1,0:T(8,128)(2,1)S(1)}, u32[]{:S(2)}, u32[]{:S(2)}) collective-permute-start(bf16[48,1664]{1,0:T(8,128)(2,1)S(1)} %reshape.30), channel_id=1, source_target_pairs={{0,16},{1,17},{2,18},{3,19},{4,20},{5,21},{6,22},{7,23},{8,24},{9,... | collective-permute-start | bytes 479240 | tf_op jit(solution)/shard_map/ppermute | solution.py:36
  19.3 3.3 %collective-permute-start.8 = (bf16[48,1664]{1,0:T(8,128)(2,1)S(1)}, bf16[48,1664]{1,0:T(8,128)(2,1)S(1)}, u32[]{:S(2)}, u32[]{:S(2)}) collective-permute-start(bf16[48,1664]{1,0:T(8,128)(2,1)S(1)} %reshape.30), channel_id=1, source_target_pairs={{0,32},{1,33},{2,34},{3,35},{4,36},{5,37},{6,38},{7,39},{8,40},{9,... | collective-permute-start | bytes 479240 | tf_op jit(solution)/shard_map/ppermute | solution.py:36
  22.7 0.8 collective-permute-start.4
  23.5 0.6 collective-permute-done.9
  24.1 2.9 %collective-permute-done.8 = bf16[48,1664]{1,0:T(8,128)(2,1)S(1)} collective-permute-done((bf16[48,1664]{1,0:T(8,128)(2,1)S(1)}, bf16[48,1664]{1,0:T(8,128)(2,1)S(1)}, u32[]{:S(2)}, u32[]{:S(2)}) %collective-permute-start.8) | collective-permute-done | bytes 159776 | tf_op jit(solution)/shard_map/ppermute | solution.py:36
  27.0 2.9 %collective-permute-start.10 = (bf16[2,48,1664]{2,1,0:T(8,128)(2,1)S(1)}, bf16[2,48,1664]{2,1,0:T(8,128)(2,1)S(1)}, u32[]{:S(2)}, u32[]{:S(2)}) collective-permute-start(bf16[2,48,1664]{2,1,0:T(8,128)(2,1)S(1)} %get-tuple-element.41), channel_id=1, source_target_pairs={{0,12},{1,13},{2,14},{3,15},{4,8},{5,9},{6,10},{7,11},{8,4},{9,5},... | collective-permute-start | bytes 958472 | tf_op jit(solution)/shard_map/ppermute | solution.py:36
  30.1 1.0 broadcast_in_dim.36
  31.1 3.5 %all-to-all-start = ((bf16[4,32,3584]{2,1,0:T(8,128)(2,1)}), bf16[4,32,3584]{2,1,0:T(8,128)(2,1)S(1)}, u32[]{:S(2)}, u32[]{:S(2)}) async-start(bf16[4,32,3584]{2,1,0:T(8,128)(2,1)} %broadcast_in_dim.36), calls=%async_computation | async-start | bytes 1835008 | tf_op jit(solution)/shard_map/all_to_all | solution.py:658
  34.6 1.2 %collective-permute-done.5 = bf16[2,48,1664]{2,1,0:T(8,128)(2,1)S(1)} collective-permute-done((bf16[2,48,1664]{2,1,0:T(8,128)(2,1)S(1)}, bf16[2,48,1664]{2,1,0:T(8,128)(2,1)S(1)}, u32[]{:S(2)}, u32[]{:S(2)}) %collective-permute-start.5) | collective-permute-done | bytes 319520 | tf_op jit(solution)/shard_map/ppermute | solution.py:36
  36.2 0.3 collective-permute-start.11
  36.5 0.5 collective-permute-start.12
  37.0 0.7 collective-permute-done.7.theirs_ref
  37.7 11.0 %all-to-all-done.images_ref = bf16[4,32,3584]{2,1,0:T(8,128)(2,1)S(1)} async-done(((bf16[4,32,3584]{2,1,0:T(8,128)(2,1)}), bf16[4,32,3584]{2,1,0:T(8,128)(2,1)S(1)}, u32[]{:S(2)}, u32[]{:S(2)}) %all-to-all-start) | async-done | bytes 917536 | tf_op jit(solution)/shard_map/all_to_all | solution.py:658
  48.8 0.5 collective-permute-start.15
  49.2 0.3 collective-permute-start.13
  49.5 0.6 pad_add_fusion.where_ref
  50.1 1.0 collective-permute-done.15.o3
  51.1 1.1 collective-permute-done.13.o1
  52.2 22.5 %real_forward.1 = (bf16[32,4,896]{2,1,0:T(4,128)(2,1)}, bf16[768,3328]{1,0:T(8,128)(2,1)}, bf16[2,256,768]{2,1,0:T(8,128)(2,1)}) custom-call(s32[4]{0:T(128)} %pad_add_fusion.where_ref, bf16[2,16,768]{2,1,0:T(8,128)(2,1)} %mine_ref.3, bf16[2,16,768]{2,1,0:T(8,128)(2,1)} %copy-done.7, bf16[4,32,3584]{2,1,0:T(8,128)(2,1)} %copy-done.1, ...), custom_call_target="tpu_custom_call" | custom-call | flops 14000000000 | bytes 12000000 | tf_op jit(solution)/shard_map/real_forward/pallas_call | solution.py:516
  74.7 5.3 %all-to-all-start.1 = ((bf16[32,4,896]{2,1,0:T(4,128)(2,1)}), bf16[32,4,896]{2,1,0:T(4,128)(2,1)S(1)}, u32[]{:S(2)}, u32[]{:S(2)}) async-start(bf16[32,4,896]{2,1,0:T(4,128)(2,1)} %get-tuple-element.24), calls=%async_computation.1 | async-start | bytes 458752 | tf_op jit(solution)/shard_map/all_to_all | solution.py:668
  80.1 8.8 %synth_forward.1 = (f32[4,768]{1,0:T(4,128)}, bf16[384,768]{1,0:T(8,128)(2,1)}, f32[384,128]{1,0:T(8,128)}, bf16[384,2304]{1,0:T(8,128)(2,1)}, bf16[384,1536]{1,...) custom-call(s32[4]{0:T(128)} %pad_add_fusion.where_ref, bf16[2,16,768]{2,1,0:T(8,128)(2,1)} %mine_ref.3, ...), custom_call_target="tpu_custom_call" | custom-call | flops 3000000000 | bytes 12000000 | tf_op jit(solution)/shard_map/synth_forward/pallas_call | solution.py:559
  88.9 0.5 collective-permute-start.16
  89.5 0.1 convert_reduce_fusion
  89.6 0.1 fusion.2
  89.7 0.7 slice_divide_fusion.means_ref
  90.4 0.1 collective-permute-done.16.their_ref
  90.5 0.6 copy-done.8
  91.1 9.8 %synth_backward.1 = (bf16[5,3072]{1,0:T(8,128)(2,1)}, bf16[5,3072]{1,0:T(8,128)(2,1)}, bf16[5,3072]{1,0:T(8,128)(2,1)}, bf16[5,3072]{1,0:T(8,128)(2,1)}) custom-call(s32[4]{0:T(128)} %pad_add_fusion.where_ref, f32[4,768]{1,0:T(4,128)} %slice_divide_fusion.means_ref, f32[4,768]{1,0:T(4,128)} %get-tuple-element.27.own_ref, f32[4,768]{1,0:T(4,128)} %copy-done.8, ...), custom_call_target="tpu_custom_call" | custom-call | flops 4000000000 | bytes 12000000 | tf_op jit(solution)/shard_map/synth_backward/pallas_call | solution.py:585
  100.9 0.4 collective-permute-start.17
  101.3 1.0 collective-permute-start.20
  102.2 2.0 %collective-permute-start.21 = (bf16[5,3072]{1,0:T(8,128)(2,1)}, bf16[5,3072]{1,0:T(8,128)(2,1)S(1)}, u32[]{:S(2)}, u32[]{:S(2)}) collective-permute-start(bf16[5,3072]{1,0:T(8,128)(2,1)} %get-tuple-element.39), channel_id=1, source_target_pairs={{0,2},{1,3},{2,0},{3,1},{4,6},{5,7},{6,4},{7,5},{8,10},{9,11},{10,... | collective-permute-start | bytes 92168 | tf_op jit(solution)/shard_map/ppermute | solution.py:36
  104.2 4.1 %collective-permute-start.18 = (f32[1,768]{1,0:T(1,128)S(1)}, f32[1,768]{1,0:T(1,128)S(1)}, u32[]{:S(2)}, u32[]{:S(2)}) collective-permute-start(f32[1,768]{1,0:T(1,128)S(1)} %get-tuple-element.50), channel_id=1, source_target_pairs={{0,0},{1,1},{2,64},{3,65},{4,4},{5,5},{6,68},{7,69},{8,8},{9,9},{1... | collective-permute-start | bytes 9224 | tf_op jit(solution)/shard_map/ppermute | solution.py:36
  108.4 0.8 collective-permute-start.19
  109.2 0.8 convert_add_fusion
  110.1 0.5 collective-permute-done.18
  110.6 2.0 %collective-permute-done.19 = f32[1,768]{1,0:T(1,128)S(1)} collective-permute-done((f32[1,768]{1,0:T(1,128)S(1)}, f32[1,768]{1,0:T(1,128)S(1)}, u32[]{:S(2)}, u32[]{:S(2)}) %collective-permute-start.19) | collective-permute-done | bytes 3104 | tf_op jit(solution)/shard_map/ppermute | solution.py:36
  112.7 0.6 pad_maximum_fusion.6
  113.3 0.7 pad_maximum_fusion.4
  (73 shorter events, 1.3 us)
Async XLA Ops:
  0.6 12.7 %copy-start = (bf16[64,3072]{1,0:T(8,128)(2,1)S(1)}, bf16[64,3072]{1,0:T(8,128)(2,1)}, u32[]{:S(2)}) copy-start(bf16[64,3072]{1,0:T(8,128)(2,1)} %param.8) | copy-start | bytes 1179652
  0.6 12.7 %copy-start.9 = (s32[64]{0:T(128)S(1)}, s32[64]{0:T(128)}, u32[]{:S(2)}) copy-start(s32[64]{0:T(128)} %param.10) | copy-start | bytes 772
  0.7 12.7 %copy-start.10 = (s32[64]{0:T(128)S(1)}, s32[64]{0:T(128)}, u32[]{:S(2)}) copy-start(s32[64]{0:T(128)} %param.9) | copy-start | bytes 772
  3.1 14.4 %collective-permute-start.3 = (bf16[12,1664]{1,0:T(8,128)(2,1)S(1)}, bf16[12,1664]{1,0:T(8,128)(2,1)S(1)}, u32[]{:S(2)}, u32[]{:S(2)}) collective-permute-start(bf16[12,1664]{1,0:T(8,128)(2,1)S(1)} %get-tuple-element.44), channel_id=1, source_target_pairs={{0,1},{1,64},{2,65},{3,0},{4,5},{5,68},{6,69},{7,4},{8,9},{9,72},{... | collective-permute-start | bytes 119816 | tf_op jit(solution)/shard_map/ppermute | solution.py:36
  6.4 10.9 %collective-permute-start.2 = (bf16[12,1664]{1,0:T(8,128)(2,1)S(1)}, bf16[12,1664]{1,0:T(8,128)(2,1)S(1)}, u32[]{:S(2)}, u32[]{:S(2)}) collective-permute-start(bf16[12,1664]{1,0:T(8,128)(2,1)S(1)} %get-tuple-element.45), channel_id=1, source_target_pairs={{0,64},{1,65},{2,0},{3,1},{4,68},{5,69},{6,4},{7,5},{8,72},{9,73},... | collective-permute-start | bytes 119816 | tf_op jit(solution)/shard_map/ppermute | solution.py:36
  9.2 8.2 %collective-permute-start.1 = (bf16[12,1664]{1,0:T(8,128)(2,1)S(1)}, bf16[12,1664]{1,0:T(8,128)(2,1)S(1)}, u32[]{:S(2)}, u32[]{:S(2)}) collective-permute-start(bf16[12,1664]{1,0:T(8,128)(2,1)S(1)} %get-tuple-element.46), channel_id=1, source_target_pairs={{0,65},{1,0},{2,1},{3,64},{4,69},{5,4},{6,5},{7,68},{8,73},{9,8},{... | collective-permute-start | bytes 119816 | tf_op jit(solution)/shard_map/ppermute | solution.py:36
  10.4 6.9 %collective-permute-start = (bf16[12,1664]{1,0:T(8,128)(2,1)S(1)}, bf16[12,1664]{1,0:T(8,128)(2,1)S(1)}, u32[]{:S(2)}, u32[]{:S(2)}) collective-permute-start(bf16[12,1664]{1,0:T(8,128)(2,1)S(1)} %get-tuple-element.47), channel_id=1, source_target_pairs={{0,0},{1,1},{2,64},{3,65},{4,4},{5,5},{6,68},{7,69},{8,8},{9,9},{1... | collective-permute-start | bytes 119816 | tf_op jit(solution)/shard_map/ppermute | solution.py:36
  17.6 6.5 %collective-permute-start.9 = (bf16[48,1664]{1,0:T(8,128)(2,1)S(1)}, bf16[48,1664]{1,0:T(8,128)(2,1)S(1)}, u32[]{:S(2)}, u32[]{:S(2)}) collective-permute-start(bf16[48,1664]{1,0:T(8,128)(2,1)S(1)} %reshape.30), channel_id=1, source_target_pairs={{0,16},{1,17},{2,18},{3,19},{4,20},{5,21},{6,22},{7,23},{8,24},{9,... | collective-permute-start | bytes 479240 | tf_op jit(solution)/shard_map/ppermute | solution.py:36
  19.3 7.7 %collective-permute-start.8 = (bf16[48,1664]{1,0:T(8,128)(2,1)S(1)}, bf16[48,1664]{1,0:T(8,128)(2,1)S(1)}, u32[]{:S(2)}, u32[]{:S(2)}) collective-permute-start(bf16[48,1664]{1,0:T(8,128)(2,1)S(1)} %reshape.30), channel_id=1, source_target_pairs={{0,32},{1,33},{2,34},{3,35},{4,36},{5,37},{6,38},{7,39},{8,40},{9,... | collective-permute-start | bytes 479240 | tf_op jit(solution)/shard_map/ppermute | solution.py:36
  22.7 7.2 %collective-permute-start.4 = (bf16[48,1664]{1,0:T(8,128)(2,1)S(1)}, bf16[48,1664]{1,0:T(8,128)(2,1)S(1)}, u32[]{:S(2)}, u32[]{:S(2)}) collective-permute-start(bf16[48,1664]{1,0:T(8,128)(2,1)S(1)} %reshape.30), channel_id=1, source_target_pairs={{0,48},{1,49},{2,50},{3,51},{4,52},{5,53},{6,54},{7,55},{8,56},{9,... | collective-permute-start | bytes 479240 | tf_op jit(solution)/shard_map/ppermute | solution.py:36
  27.0 9.1 %collective-permute-start.10 = (bf16[2,48,1664]{2,1,0:T(8,128)(2,1)S(1)}, bf16[2,48,1664]{2,1,0:T(8,128)(2,1)S(1)}, u32[]{:S(2)}, u32[]{:S(2)}) collective-permute-start(bf16[2,48,1664]{2,1,0:T(8,128)(2,1)S(1)} %get-tuple-element.41), channel_id=1, source_target_pairs={{0,12},{1,13},{2,14},{3,15},{4,8},{5,9},{6,10},{7,11},{8,4},{9,5},... | collective-permute-start | bytes 958472 | tf_op jit(solution)/shard_map/ppermute | solution.py:36
  30.0 5.9 %collective-permute-start.5 = (bf16[2,48,1664]{2,1,0:T(8,128)(2,1)S(1)}, bf16[2,48,1664]{2,1,0:T(8,128)(2,1)S(1)}, u32[]{:S(2)}, u32[]{:S(2)}) collective-permute-start(bf16[2,48,1664]{2,1,0:T(8,128)(2,1)S(1)} %get-tuple-element.43), channel_id=1, source_target_pairs={{0,4},{1,5},{2,6},{3,7},{4,0},{5,1},{6,2},{7,3},{8,12},{9,13},{10,... | collective-permute-start | bytes 958472 | tf_op jit(solution)/shard_map/ppermute | solution.py:36
  31.1 17.6 %all-to-all-start = ((bf16[4,32,3584]{2,1,0:T(8,128)(2,1)}), bf16[4,32,3584]{2,1,0:T(8,128)(2,1)S(1)}, u32[]{:S(2)}, u32[]{:S(2)}) async-start(bf16[4,32,3584]{2,1,0:T(8,128)(2,1)} %broadcast_in_dim.36), calls=%async_computation | async-start | bytes 1835008 | tf_op jit(solution)/shard_map/all_to_all | solution.py:658
  34.6 1.8 %copy-start.6 = (bf16[2,16,768]{2,1,0:T(8,128)(2,1)S(1)}, bf16[2,16,768]{2,1,0:T(8,128)(2,1)}, u32[]{:S(2)}) copy-start(bf16[2,16,768]{2,1,0:T(8,128)(2,1)} %mine_ref.3) | copy-start | bytes 147460
  36.0 16.2 %copy-start.2 = (bf16[2,2,48,1664]{3,2,1,0:T(8,128)(2,1)}, bf16[2,2,48,1664]{3,2,1,0:T(8,128)(2,1)S(1)}, u32[]{:S(2)}) copy-start(bf16[2,2,48,1664]{3,2,1,0:T(8,128)(2,1)S(1)} %pad_maximum_fusion.l0) | copy-start | bytes 1916932
  36.0 12.8 %collective-permute-start.6 = (bf16[2,2,48,1664]{3,2,1,0:T(8,128)(2,1)S(1)}, bf16[2,2,48,1664]{3,2,1,0:T(8,128)(2,1)}, u32[]{:S(2)}, u32[]{:S(2)}) collective-permute-start(bf16[2,2,48,1664]{3,2,1,0:T(8,128)(2,1)S(1)} %pad_maximum_fusion.l0), channel_id=1, source_target_pairs={{0,12},{1,13},{2,14},{3,15},{4,8},{5,9},{6,10},{7,11},{8,4},{9,5},... | collective-permute-start | bytes 1916936 | tf_op jit(solution)/shard_map/ppermute | solution.py:36
  36.2 16.0 %copy-start.3 = (bf16[2,2,48,1664]{3,2,1,0:T(8,128)(2,1)}, bf16[2,2,48,1664]{3,2,1,0:T(8,128)(2,1)S(1)}, u32[]{:S(2)}) copy-start(bf16[2,2,48,1664]{3,2,1,0:T(8,128)(2,1)S(1)} %pad_maximum_fusion.1.l2) | copy-start | bytes 1916932
  36.2 12.6 %collective-permute-start.11 = (bf16[2,2,48,1664]{3,2,1,0:T(8,128)(2,1)S(1)}, bf16[2,2,48,1664]{3,2,1,0:T(8,128)(2,1)S(1)}, u32[]{:S(2)}, u32[]{:S(2)}) collective-permute-start(bf16[2,2,48,1664]{3,2,1,0:T(8,128)(2,1)S(1)} %pad_maximum_fusion.1.l2), channel_id=1, source_target_pairs={{0,4},{1,5},{2,6},{3,7},{4,0},{5,1},{6,2},{7,3},{8,12},{9,13},{10,... | collective-permute-start | bytes 1916936 | tf_op jit(solution)/shard_map/ppermute | solution.py:36
  36.5 1.3 %collective-permute-start.7 = (bf16[2,16,768]{2,1,0:T(8,128)(2,1)S(1)}, bf16[2,16,768]{2,1,0:T(8,128)(2,1)S(1)}, u32[]{:S(2)}, u32[]{:S(2)}) collective-permute-start(bf16[2,16,768]{2,1,0:T(8,128)(2,1)S(1)} %copy-done.6), channel_id=1, source_target_pairs={{0,64},{1,65},{2,66},{3,67},{4,68},{5,69},{6,70},{7,71},{8,72},{9,... | collective-permute-start | bytes 147464 | tf_op jit(solution)/shard_map/ppermute | solution.py:36
  36.5 13.6 %collective-permute-start.12 = (bf16[2,2,48,1664]{3,2,1,0:T(8,128)(2,1)S(1)}, bf16[2,2,48,1664]{3,2,1,0:T(8,128)(2,1)}, u32[]{:S(2)}, u32[]{:S(2)}) collective-permute-start(bf16[2,2,48,1664]{3,2,1,0:T(8,128)(2,1)S(1)} %pad_maximum_fusion.l0), channel_id=1, source_target_pairs={{0,64},{1,65},{2,66},{3,67},{4,68},{5,69},{6,70},{7,71},{8,72},{9,... | collective-permute-start | bytes 1916936 | tf_op jit(solution)/shard_map/ppermute | solution.py:36
  37.0 13.1 %collective-permute-start.14 = (bf16[2,2,48,1664]{3,2,1,0:T(8,128)(2,1)S(1)}, bf16[2,2,48,1664]{3,2,1,0:T(8,128)(2,1)}, u32[]{:S(2)}, u32[]{:S(2)}) collective-permute-start(bf16[2,2,48,1664]{3,2,1,0:T(8,128)(2,1)S(1)} %pad_maximum_fusion.1.l2), channel_id=1, source_target_pairs={{0,64},{1,65},{2,66},{3,67},{4,68},{5,69},{6,70},{7,71},{8,72},{9,... | collective-permute-start | bytes 1916936 | tf_op jit(solution)/shard_map/ppermute | solution.py:36
  37.7 14.5 %copy-start.7 = (bf16[2,16,768]{2,1,0:T(8,128)(2,1)}, bf16[2,16,768]{2,1,0:T(8,128)(2,1)S(1)}, u32[]{:S(2)}) copy-start(bf16[2,16,768]{2,1,0:T(8,128)(2,1)S(1)} %collective-permute-done.7.theirs_ref) | copy-start | bytes 147460
  48.7 3.5 %copy-start.1 = (bf16[4,32,3584]{2,1,0:T(8,128)(2,1)}, bf16[4,32,3584]{2,1,0:T(8,128)(2,1)S(1)}, u32[]{:S(2)}) copy-start(bf16[4,32,3584]{2,1,0:T(8,128)(2,1)S(1)} %all-to-all-done.images_ref) | copy-start | bytes 2752516
  48.7 3.5 %copy-start.5 = (bf16[2,2,48,1664]{3,2,1,0:T(8,128)(2,1)}, bf16[2,2,48,1664]{3,2,1,0:T(8,128)(2,1)S(1)}, u32[]{:S(2)}) copy-start(bf16[2,2,48,1664]{3,2,1,0:T(8,128)(2,1)S(1)} %collective-permute-done.11.l3) | copy-start | bytes 1916932
  48.8 2.3 %collective-permute-start.15 = (bf16[2,2,48,1664]{3,2,1,0:T(8,128)(2,1)S(1)}, bf16[2,2,48,1664]{3,2,1,0:T(8,128)(2,1)}, u32[]{:S(2)}, u32[]{:S(2)}) collective-permute-start(bf16[2,2,48,1664]{3,2,1,0:T(8,128)(2,1)S(1)} %collective-permute-done.11.l3), channel_id=1, source_target_pairs={{0,64},{1,65},{2,66},{3,67},{4,68},{5,69},{6,70},{7,71},{8,72},{9,... | collective-permute-start | bytes 1916936 | tf_op jit(solution)/shard_map/ppermute | solution.py:36
  49.2 3.0 %collective-permute-start.13 = (bf16[2,2,48,1664]{3,2,1,0:T(8,128)(2,1)}, bf16[2,2,48,1664]{3,2,1,0:T(8,128)(2,1)}, u32[]{:S(2)}, u32[]{:S(2)}) collective-permute-start(bf16[2,2,48,1664]{3,2,1,0:T(8,128)(2,1)} %collective-permute-done.6.l1), channel_id=1, source_target_pairs={{0,64},{1,65},{2,66},{3,67},{4,68},{5,69},{6,70},{7,71},{8,72},{9,... | collective-permute-start | bytes 1916936 | tf_op jit(solution)/shard_map/ppermute | solution.py:36
  74.7 14.7 %all-to-all-start.1 = ((bf16[32,4,896]{2,1,0:T(4,128)(2,1)}), bf16[32,4,896]{2,1,0:T(4,128)(2,1)S(1)}, u32[]{:S(2)}, u32[]{:S(2)}) async-start(bf16[32,4,896]{2,1,0:T(4,128)(2,1)} %get-tuple-element.24), calls=%async_computation.1 | async-start | bytes 458752 | tf_op jit(solution)/shard_map/all_to_all | solution.py:668
  88.9 1.6 %collective-permute-start.16 = (f32[4,768]{1,0:T(4,128)}, f32[4,768]{1,0:T(4,128)S(1)}, u32[]{:S(2)}, u32[]{:S(2)}) collective-permute-start(f32[4,768]{1,0:T(4,128)} %get-tuple-element.27.own_ref), channel_id=1, source_target_pairs={{0,64},{1,65},{2,66},{3,67},{4,68},{5,69},{6,70},{7,71},{8,72},{9,... | collective-permute-start | bytes 36872 | tf_op jit(solution)/shard_map/ppermute | solution.py:36
  90.5 0.6 copy-start.8
  91.1 13.1 %copy-start.4 = (f32[4,768]{1,0:T(4,128)S(1)}, f32[4,768]{1,0:T(4,128)}, u32[]{:S(2)}) copy-start(f32[4,768]{1,0:T(4,128)} %slice_divide_fusion.means_ref) | copy-start | bytes 36868
  100.9 3.3 %collective-permute-start.17 = (bf16[5,3072]{1,0:T(8,128)(2,1)}, bf16[5,3072]{1,0:T(8,128)(2,1)S(1)}, u32[]{:S(2)}, u32[]{:S(2)}) collective-permute-start(bf16[5,3072]{1,0:T(8,128)(2,1)} %get-tuple-element.34), channel_id=1, source_target_pairs={{0,1},{1,0},{2,3},{3,2},{4,5},{5,4},{6,7},{7,6},{8,9},{9,8},{10,11... | collective-permute-start | bytes 92168 | tf_op jit(solution)/shard_map/ppermute | solution.py:36
  101.3 7.9 %collective-permute-start.20 = (bf16[5,3072]{1,0:T(8,128)(2,1)}, bf16[5,3072]{1,0:T(8,128)(2,1)S(1)}, u32[]{:S(2)}, u32[]{:S(2)}) collective-permute-start(bf16[5,3072]{1,0:T(8,128)(2,1)} %get-tuple-element.38), channel_id=1, source_target_pairs={{0,3},{1,2},{2,1},{3,0},{4,7},{5,6},{6,5},{7,4},{8,11},{9,10},{10,... | collective-permute-start | bytes 92168 | tf_op jit(solution)/shard_map/ppermute | solution.py:36
  102.2 7.0 %collective-permute-start.21 = (bf16[5,3072]{1,0:T(8,128)(2,1)}, bf16[5,3072]{1,0:T(8,128)(2,1)S(1)}, u32[]{:S(2)}, u32[]{:S(2)}) collective-permute-start(bf16[5,3072]{1,0:T(8,128)(2,1)} %get-tuple-element.39), channel_id=1, source_target_pairs={{0,2},{1,3},{2,0},{3,1},{4,6},{5,7},{6,4},{7,5},{8,10},{9,11},{10,... | collective-permute-start | bytes 92168 | tf_op jit(solution)/shard_map/ppermute | solution.py:36
  104.2 6.4 %collective-permute-start.18 = (f32[1,768]{1,0:T(1,128)S(1)}, f32[1,768]{1,0:T(1,128)S(1)}, u32[]{:S(2)}, u32[]{:S(2)}) collective-permute-start(f32[1,768]{1,0:T(1,128)S(1)} %get-tuple-element.50), channel_id=1, source_target_pairs={{0,0},{1,1},{2,64},{3,65},{4,4},{5,5},{6,68},{7,69},{8,8},{9,9},{1... | collective-permute-start | bytes 9224 | tf_op jit(solution)/shard_map/ppermute | solution.py:36
  108.4 4.3 %collective-permute-start.19 = (f32[1,768]{1,0:T(1,128)S(1)}, f32[1,768]{1,0:T(1,128)S(1)}, u32[]{:S(2)}, u32[]{:S(2)}) collective-permute-start(f32[1,768]{1,0:T(1,128)S(1)} %get-tuple-element.51), channel_id=1, source_target_pairs={{0,1},{1,0},{2,65},{3,64},{4,5},{5,4},{6,69},{7,68},{8,9},{9,8},{1... | collective-permute-start | bytes 9224 | tf_op jit(solution)/shard_map/ppermute | solution.py:36
  110.0 3.3 %collective-permute-start.22 = (f32[5,3072]{1,0:T(8,128)S(1)}, f32[5,3072]{1,0:T(8,128)S(1)}, u32[]{:S(2)}, u32[]{:S(2)}) collective-permute-start(f32[5,3072]{1,0:T(8,128)S(1)} %convert_add_fusion), channel_id=1, source_target_pairs={{0,64},{1,65},{2,66},{3,67},{4,68},{5,69},{6,70},{7,71},{8,72},{9,... | collective-permute-start | bytes 184328 | tf_op jit(solution)/shard_map/ppermute | solution.py:36
